TPU v7x, 32 devices: a whole 2x2x4 slice. The times are simulated.
32 devices in a mesh: dp: 16 (over z, x, core), mp: 2 (over y).
Axes of the slice: x: 2, y: 2, z: 4, core: 2. Of those that a mesh axis runs over, the one named last changes fastest.
Arguments:
- history: bfloat16 [9, 2048, 6144], P(None, 'dp'), may hold values from -6 to 6
- mix_in: float32 [6144, 36], P('dp'), may hold values from -3 to 3
- doc_ids: int32 [16, 384], P('dp'), may hold values from 0 to 3, never falling along the last dimension, each value on 1 to 192 neighbouring positions
- group_ids: int32 [16, 384], P('dp'), may hold values from 0 to 7
- group_scale: float32 [8], replicated, may hold values from 0.5 to 2
- w_qkv: bfloat16 [3, 2048, 2048], P(None, 'dp', 'mp'), may hold values from -0.125 to 0.125
- w_out: bfloat16 [2048, 2048], P('dp', 'mp'), may hold values from -0.375 to 0.375
- w_up: bfloat16 [2048, 8192], P('dp', 'mp'), may hold values from -0.125 to 0.125
- w_down: bfloat16 [2048, 8192], P('dp', 'mp'), may hold values from -0.0625 to 0.0625
- w_mix1: bfloat16 [2048, 40], P('dp'), may hold values from -0.125 to 0.125
- w_mix2: bfloat16 [40, 40], replicated, may hold values from -1 to 1
- gains: bfloat16 [5, 2048], P(None, 'dp'), may hold values from 0.25 to 1.75
- cot_out: bfloat16 [2048, 6144], P('dp'), may hold values from -6 to 6
- cot_mix: bfloat16 [6144, 40], P('dp'), may hold values from -15 to 15
Outputs:
- block_out: bfloat16 [2048, 6144], P('dp')
- mix_out: float32 [6144, 40], P('dp')
- grad_history: bfloat16 [9, 2048, 6144], P(None, 'dp')
- grad_mix_in: float32 [6144, 36], P('dp')
- grad_qkv: float32 [3, 2048, 2048], P(None, 'dp', 'mp')
- grad_w_out: float32 [2048, 2048], P('dp', 'mp')
- grad_w_up: float32 [2048, 8192], P('dp', 'mp')
- grad_w_down: float32 [2048, 8192], P('dp', 'mp')
- grad_w_mix1: float32 [2048, 40], P('dp')
- grad_w_mix2: float32 [40, 40], replicated
- grad_gains: float32 [5, 2048], P(None, 'dp')
Inputs may be any that keep to these rules, and one draw needn't show every extreme that they name: `doc_ids`: in each row the ids never fall; each document has 1 to 192 tokens, and one has exactly 192.
All inputs are finite; a program needn't handle non-finite values.
Results may differ from a plain program's by a relative error of at most 0.012.
Values may be sent and summed in bfloat16 or wider, within the bound.
A program may use at most 384 MiB of HBM per device.

v0:
```python
import math

import jax
import jax.numpy as jnp
from jax import lax
from jax.sharding import PartitionSpec as P

HEAD = 128
ROT = 32
HIST = 9
STREAMS = 4
GROUPS = 8
TOK_DEV = 384


def rms_norm(inputs, scales):
    return inputs * lax.rsqrt(jnp.mean(inputs * inputs, axis=-1, keepdims=True) + 1e-05) * scales


def rotary(heads_in, angles):
    halfway = ROT // 2
    cosine = jnp.cos(angles)[:, None, :]
    sine_part = jnp.sin(angles)[:, None, :]
    first_half = heads_in[..., :halfway]
    second_half = heads_in[..., halfway:ROT]
    return jnp.concatenate(
        [
            first_half * cosine - second_half * sine_part,
            second_half * cosine + first_half * sine_part,
            heads_in[..., ROT:],
        ],
        axis=-1,
    )


def angle_table(length):
    halfway = ROT // 2
    frequency = jnp.exp(jnp.arange(halfway, dtype=jnp.float32) * (-2.0 * math.log(10000.0) / ROT))
    places = (jnp.arange(length) % TOK_DEV).astype(jnp.float32)
    return places[:, None] * frequency[None, :]


def gelu_exact(inputs):
    return jax.nn.gelu(inputs, approximate=False)


def outer_sum(left, right):
    return jnp.einsum("td,te->de", left, right, preferred_element_type=jnp.float32)


def right_product(left, matrix):
    return jnp.einsum("ti,oi->to", left, matrix, preferred_element_type=jnp.float32)


def masked_scores(queries, key_heads, allowed, scale_qk):
    scores = (
        jnp.einsum("hqd,hkd->hqk", queries, key_heads, preferred_element_type=jnp.float32)
        * scale_qk
    )
    return jnp.where(allowed[None], scores, -1000000000.0)


def body(
    history,
    mix_in,
    doc_ids,
    group_ids,
    group_scale,
    w_qkv,
    w_out,
    w_up,
    w_down,
    w_mix1,
    w_mix2,
    gains,
    cot_out,
    cot_mix,
):
    f32 = jnp.float32
    bf16 = jnp.bfloat16
    hist_tok, cot_tok = (
        lax.all_to_all(history, "dp", split_axis=2, concat_axis=1, tiled=True),
        lax.all_to_all(cot_out[None], "dp", split_axis=2, concat_axis=1, tiled=True),
    )
    full_qkv, full_o, full_up, full_down, full_m1, full_gain = (
        lax.all_gather(w_qkv, "dp", axis=1, tiled=True),
        lax.all_gather(w_out, "dp", axis=0, tiled=True),
        lax.all_gather(w_up, "dp", axis=0, tiled=True),
        lax.all_gather(w_down, "dp", axis=0, tiled=True),
        lax.all_gather(w_mix1, "dp", axis=0, tiled=True),
        lax.all_gather(gains, "dp", axis=1, tiled=True),
    )
    gain_f = full_gain.astype(f32)
    tokens_here = hist_tok.shape[2]
    heads_here = full_qkv.shape[2] // HEAD
    width_here = heads_here * HEAD
    mixing = mix_in.reshape(tokens_here, STREAMS, HIST)
    streams = mixing[:, :, 0, None] * hist_tok[0].astype(f32).T[:, None, :]
    for entry_num in range(1, HIST):
        streams = (
            streams + mixing[:, :, entry_num, None] * hist_tok[entry_num].astype(f32).T[:, None, :]
        )
    normed = []
    norm_pulls = []
    for stream_num in range(STREAMS):
        normed_f, norm_pull = jax.vjp(rms_norm, streams[:, stream_num], gain_f[stream_num])
        normed.append(normed_f.astype(bf16))
        norm_pulls.append(norm_pull)
    angles = angle_table(tokens_here)

    def project(stream_num):
        return jnp.dot(
            normed[stream_num], full_qkv[stream_num], preferred_element_type=f32
        ).reshape(tokens_here, heads_here, HEAD)

    queries = rotary(project(0), angles).astype(bf16).transpose(1, 0, 2)
    key_heads = rotary(project(1), angles).astype(bf16).transpose(1, 0, 2)
    values = project(2).astype(bf16).transpose(1, 0, 2)
    scale_qk = HEAD ** (-0.5)
    positions = jnp.arange(tokens_here)
    doc_row = doc_ids[0]
    allowed = (positions[:, None] >= positions[None, :]) & (doc_row[:, None] == doc_row[None, :])
    scores = masked_scores(queries, key_heads, allowed, scale_qk)
    row_max = jnp.max(scores, axis=-1, keepdims=True)
    log_total = row_max + jnp.log(jnp.sum(jnp.exp(scores - row_max), axis=-1, keepdims=True))
    probs_low = jnp.exp(scores - log_total).astype(bf16)
    attended = jnp.einsum("hqk,hkd->hqd", probs_low, values, preferred_element_type=f32)
    attn_cat = attended.astype(bf16).transpose(1, 0, 2).reshape(tokens_here, width_here)
    up_pre = jnp.dot(normed[3], full_up, preferred_element_type=f32)
    hidden = gelu_exact(up_pre).astype(bf16)
    branch_part = right_product(attn_cat, full_o) + right_product(hidden, full_down)
    branch = lax.psum(branch_part, "mp")
    out_full = streams[:, 3] + branch
    out_low = out_full.astype(bf16)
    mix_norm_f, mix_pull = jax.vjp(rms_norm, out_full, gain_f[4])
    mix_normed = mix_norm_f.astype(bf16)
    mix_pre = jnp.dot(mix_normed, full_m1, preferred_element_type=f32)
    mix_hidden = gelu_exact(mix_pre).astype(bf16)
    mix_out = jnp.dot(mix_hidden, w_mix2, preferred_element_type=f32)
    out_hidden = lax.all_to_all(out_low.T[None], "dp", split_axis=1, concat_axis=2, tiled=True)[0]
    back_qkv, back_o, back_up, back_down, back_m1 = (
        lax.all_gather(w_qkv, "dp", axis=1, tiled=True),
        lax.all_gather(w_out, "dp", axis=0, tiled=True),
        lax.all_gather(w_up, "dp", axis=0, tiled=True),
        lax.all_gather(w_down, "dp", axis=0, tiled=True),
        lax.all_gather(w_mix1, "dp", axis=0, tiled=True),
    )
    row_scale = jnp.sum(
        jnp.where(group_ids[0][:, None] == jnp.arange(GROUPS)[None, :], group_scale[None, :], 0.0),
        axis=1,
    )
    seed = cot_tok[0].astype(f32).T * row_scale[:, None]
    grad_mix2_part = outer_sum(mix_hidden, cot_mix)
    grad_mix_hidden = jnp.dot(cot_mix, w_mix2.T, preferred_element_type=f32)
    grad_mix_pre = jax.vjp(gelu_exact, mix_pre)[1](grad_mix_hidden)[0].astype(bf16)
    grad_m1_part = outer_sum(mix_normed, grad_mix_pre)
    grad_mix_normed = jnp.dot(grad_mix_pre, back_m1.T, preferred_element_type=f32)
    grad_from_mix, grad_gain_mix = mix_pull(grad_mix_normed)
    grad_out_full = seed + grad_from_mix
    grad_branch = grad_out_full.astype(bf16)
    grad_o_part = outer_sum(grad_branch, attn_cat)
    grad_down_part = outer_sum(grad_branch, hidden)
    grad_attended = jnp.dot(grad_branch, back_o, preferred_element_type=f32).astype(bf16)
    grad_attended = grad_attended.reshape(tokens_here, heads_here, HEAD).transpose(1, 0, 2)
    grad_hidden = jnp.dot(grad_branch, back_down, preferred_element_type=f32)
    grad_up_pre = jax.vjp(gelu_exact, up_pre)[1](grad_hidden)[0].astype(bf16)
    grad_up_part = outer_sum(normed[3], grad_up_pre)
    grad_normed_ff = jnp.dot(grad_up_pre, back_up.T, preferred_element_type=f32)
    scores_again = masked_scores(queries, key_heads, allowed, scale_qk)
    attn_probs = jnp.exp(scores_again - log_total)
    grad_probs = jnp.einsum("hqd,hkd->hqk", grad_attended, values, preferred_element_type=f32)
    grad_values = jnp.einsum(
        "hqk,hqd->hkd", attn_probs.astype(bf16), grad_attended, preferred_element_type=f32
    )
    inner = jnp.sum(attn_probs * grad_probs, axis=-1, keepdims=True)
    grad_scores = (attn_probs * (grad_probs - inner)).astype(bf16)
    grad_q_rot = (
        jnp.einsum("hqk,hkd->hqd", grad_scores, key_heads, preferred_element_type=f32) * scale_qk
    )
    grad_k_rot = (
        jnp.einsum("hqk,hqd->hkd", grad_scores, queries, preferred_element_type=f32) * scale_qk
    )
    grad_proj_q = (
        rotary(grad_q_rot.transpose(1, 0, 2), -angles).reshape(tokens_here, width_here).astype(bf16)
    )
    grad_proj_k = (
        rotary(grad_k_rot.transpose(1, 0, 2), -angles).reshape(tokens_here, width_here).astype(bf16)
    )
    grad_proj_v = grad_values.transpose(1, 0, 2).reshape(tokens_here, width_here).astype(bf16)
    grad_projs = (grad_proj_q, grad_proj_k, grad_proj_v)
    grad_qkv_part = jnp.stack(
        [outer_sum(normed[stream_num], grad_projs[stream_num]) for stream_num in range(3)]
    )
    norm_terms = tuple(
        (
            jnp.dot(grad_projs[stream_num], back_qkv[stream_num].T, preferred_element_type=f32)
            for stream_num in range(3)
        )
    )
    grad_normed = (
        lax.psum(norm_terms[0].astype(jnp.bfloat16), "mp").astype(jnp.float32),
        lax.psum(norm_terms[1].astype(jnp.bfloat16), "mp").astype(jnp.float32),
        lax.psum(norm_terms[2].astype(jnp.bfloat16), "mp").astype(jnp.float32),
        lax.psum(grad_normed_ff.astype(jnp.bfloat16), "mp").astype(jnp.float32),
    )
    stream_grads = []
    gain_grads = []
    for stream_num in range(STREAMS):
        grad_stream, grad_gain = norm_pulls[stream_num](grad_normed[stream_num])
        stream_grads.append(grad_stream)
        gain_grads.append(grad_gain)
    stream_grads[3] = stream_grads[3] + grad_out_full
    gain_grads.append(grad_gain_mix)
    grad_streams = jnp.stack(stream_grads, axis=1)
    grad_gain_part = jnp.stack(gain_grads)
    grad_mix_in = jnp.stack(
        [
            jnp.sum(grad_streams * hist_tok[entry_num].astype(f32).T[:, None, :], axis=-1)
            for entry_num in range(HIST)
        ],
        axis=-1,
    ).reshape(tokens_here, STREAMS * HIST)
    grad_hist_low = jnp.einsum(
        "tsj,tsd->jdt", mixing, grad_streams, precision=lax.Precision.HIGHEST
    ).astype(bf16)
    grad_history = lax.all_to_all(grad_hist_low, "dp", split_axis=1, concat_axis=2, tiled=True)
    grad_qkv, grad_w_out, grad_w_up, grad_w_down, grad_w_mix1, grad_gains = (
        lax.psum_scatter(grad_qkv_part, "dp", scatter_dimension=1, tiled=True),
        lax.psum_scatter(grad_o_part, "dp", scatter_dimension=0, tiled=True),
        lax.psum_scatter(grad_up_part, "dp", scatter_dimension=0, tiled=True),
        lax.psum_scatter(grad_down_part, "dp", scatter_dimension=0, tiled=True),
        lax.psum_scatter(grad_m1_part, "dp", scatter_dimension=0, tiled=True),
        lax.psum_scatter(grad_gain_part, "dp", scatter_dimension=1, tiled=True),
    )
    grad_w_mix2 = lax.psum(grad_mix2_part, "dp")
    return (
        out_hidden,
        mix_out,
        grad_history,
        grad_mix_in,
        grad_qkv,
        grad_w_out,
        grad_w_up,
        grad_w_down,
        grad_w_mix1,
        grad_w_mix2,
        grad_gains,
    )


def solution(mesh):
    return jax.shard_map(
        body,
        mesh=mesh,
        in_specs=(
            P(None, "dp", None),
            P("dp", None),
            P("dp", None),
            P("dp", None),
            P(),
            P(None, "dp", "mp"),
            P("dp", "mp"),
            P("dp", "mp"),
            P("dp", "mp"),
            P("dp", None),
            P(),
            P(None, "dp"),
            P("dp", None),
            P("dp", None),
        ),
        out_specs=(
            P("dp", None),
            P("dp", None),
            P(None, "dp", None),
            P("dp", None),
            P(None, "dp", "mp"),
            P("dp", "mp"),
            P("dp", "mp"),
            P("dp", "mp"),
            P("dp", None),
            P(),
            P(None, "dp"),
        ),
        check_vma=False,
    )
```

profile of v0, /device:TPU:21, one launch (start us, length us, event | category | flops | bytes accessed | tf_op | source)
XLA Modules:
  0.0 2980.9 jit_solution(18199732354178298046)
XLA Ops:
  9.4 33.9 %copy.309 = bf16[9,128,6144]{1,0,2:T(8,128)(2,1)} copy(bf16[9,128,6144]{2,1,0:T(8,128)(2,1)} %param.14) | data formatting | bytes 28311552 | tf_op args[0]
  43.3 6.4 all-to-all-start
  50.9 6.9 copy.330
  58.5 34.5 %reduce.2 = bf16[6144,128]{1,0:T(8,128)(2,1)} reduce(bf16[6144,1,128]{2,1,0:T(2,128)(2,1)S(1)} %bitcast.330, bf16[]{:T(256)} %broadcast.713), dimensions={1}, to_apply=%bitcast.267.reduce_sub_computation | reduce | bytes 3145730
  97.4 752.0 %all_gather.23 = bf16[5,2048]{1,0:T(8,128)(2,1)S(1)} all-gather(bf16[5,128]{1,0:T(8,128)(2,1)S(1)} %copy-done.77), channel_id=1, replica_groups=mesh['dp'=16,'mp'=2] {'dp'}, dimensions={1}, use_global_device_ids=true | all-gather | bytes 21760 | tf_op jit(solution)/shard_map/all_gather | solution.py:91
  851.1 9.3 slice_bitcast_fusion.2
  860.4 6.5 copy.321
  866.9 6.5 copy.322
  873.4 6.5 copy.325
  879.9 4.6 all-to-all-start.2
  885.1 30.7 %copy.311 = bf16[9,128,16,384]{3,1,2,0:T(8,128)(2,1)} copy(bf16[9,128,16,384]{1,0,3,2:T(8,128)(2,1)} %bitcast) | data formatting | bytes 28311552 | tf_op jit(solution)/shard_map/all_to_all | solution.py:82
  915.7 10.3 fusion.96
  930.4 6.1 convert_bitcast_fusion.1
  943.6 5.0 convert_bitcast_fusion.3
  955.6 5.0 convert_bitcast_fusion.5
  967.7 5.0 convert_bitcast_fusion.7
  979.8 12.6 multiply_add_fusion
  1011.6 5.9 fusion.99
  1017.6 24.9 multiply_convert_fusion
  1042.4 14.5 convolution_add_fusion
  1057.7 16.5 all_gather.28
  1074.8 8.1 reshape.488
  1089.7 52.8 %all-reduce.4.cloned.1.call-done = f32[384,2048]{1,0:T(8,128)} async-done(((f32[384,2048]{1,0:T(8,128)}), f32[384,2048]{1,0:T(8,128)}) %all-reduce.4.cloned.1.call-update) | async-done | bytes 3145744 | tf_op jit(solution)/shard_map/psum | solution.py:132
  1158.6 5.0 convolution_convert_fusion.2
  1172.8 17.7 add_convert_fusion
  1190.5 12.4 convolution_convert_fusion
  1214.6 153.2 %all-reduce.6.cloned.1.call-done = (bf16[384,2048]{1,0:T(8,128)(2,1)}, bf16[384,2048]{1,0:T(8,128)(2,1)}, bf16[384,2048]{1,0:T(8,128)(2,1)}, bf16[384,2048]{1,0:T(8,128)(2,1)}) async-done(((bf16[384,2048]{1,0:T(8,128)(2,1)}, bf16[384,2048]{1,0:T(8,128)(2,1)}, bf16[384,2048]{1,0:T(8,128)(2,1)}, bf16[384,2048]{1,0:T(8,128)(2,1)}), (bf16[384,2048]{1,0:T(8,128)(2,1)}, bf16[384,2048]{1,0:T(8,128)(2,1)}, ...) | async-done | bytes 6291472 | tf_op jit(solution)/shard_map/psum | solution.py:204
  1367.9 6.6 fusion.32
  1374.6 6.6 fusion.34
  1382.4 5.7 fusion.102
  1402.6 8.7 pad_maximum_fusion
  1411.4 17.8 fusion.89
  1429.4 17.3 fusion.103
  1448.8 7.9 copy.328
  1456.8 34.5 %reduce.3 = bf16[2048,384]{1,0:T(8,128)(2,1)} reduce(bf16[2048,1,384]{2,1,0:T(2,128)(2,1)S(1)} %bitcast.331, bf16[]{:T(256)} %broadcast.713), dimensions={1}, to_apply=%bitcast.265.reduce_sub_computation | reduce | bytes 3145730
  1495.7 6.7 all-to-all-start.1
  1502.5 8.3 fusion.36
  1516.0 12.6 multiply_reduce_fusion.2
  1528.7 46.0 %convert_bitcast_fusion = bf16[9,2048,384]{1,0,2:T(8,128)(2,1)} fusion(f32[384,4,9]{2,1,0:T(4,128)} %copy.338, f32[384,4,2048]{2,0,1:T(8,128)S(1)} %get-tuple-element.150), kind=kOutput, calls=%fused_computation.1 | convolution fusion | flops 346816512 | bytes 26793984 | tf_op jit(solution)/shard_map/tsj,tsd->jdt/dot_general | solution.py:223
  1574.7 35.4 %copy.339 = bf16[9,2048,384]{2,0,1:T(8,128)(2,1)} copy(bf16[9,2048,384]{1,0,2:T(8,128)(2,1)} %convert_bitcast_fusion) | data formatting | bytes 28311552 | tf_op jit(solution)/shard_map/convert_element_type | solution.py:225
  1611.3 6.0 all-to-all-start.3
  1617.5 730.3 %psum.47 = f32[40,40]{1,0:T(8,128)} all-reduce(f32[40,40]{1,0:T(8,128)S(1)} %fusion.105), channel_id=1, replica_groups=mesh['dp'=16,'mp'=2] {'dp'}, use_global_device_ids=true, to_apply=%region_33.34 | all-reduce | flops 1600 | bytes 12800 | tf_op jit(solution)/shard_map/psum | solution.py:235
  2348.6 8.3 reshape.486
  2363.6 8.3 multiply_reduce_fusion
  2372.9 31.1 %copy.341 = bf16[9,128,16,384]{1,3,2,0:T(8,128)(2,1)} copy(bf16[9,128,16,384]{3,0,1,2:T(8,128)(2,1)} %bitcast.73) | data formatting | bytes 28311552 | tf_op jit(solution)/shard_map/all_to_all | solution.py:226
  2403.9 18.6 copy.343
  2422.6 214.2 %reduce-scatter.11.cloned.1.call-done = f32[128,4096]{1,0:T(8,128)} async-done(((f32[2048,4096]{1,0:T(8,128)}), f32[128,4096]{1,0:T(8,128)}) %reduce-scatter.11.cloned.1.call-update) | async-done | bytes 2097168 | tf_op jit(solution)/shard_map/reduce_scatter | solution.py:230
  2636.8 337.0 %reduce-scatter.13.cloned.1.call-done = f32[128,4096]{1,0:T(8,128)} async-done(((f32[2048,4096]{1,0:T(8,128)}), f32[128,4096]{1,0:T(8,128)}) %reduce-scatter.13.cloned.1.call-update) | async-done | bytes 2097168 | tf_op jit(solution)/shard_map/reduce_scatter | solution.py:231
  (306 shorter events, 144.5 us)
Async XLA Ops:
  7.2 1139.6 %copy-start = (bf16[384,40]{0,1:T(8,128)(2,1)S(1)}, bf16[384,40]{0,1:T(8,128)(2,1)}, u32[]{:S(2)}) copy-start(bf16[384,40]{0,1:T(8,128)(2,1)} %param.27) | copy-start | bytes 92164
  7.2 843.9 %all-gather.5.cloned.1.call-start = ((), (), s32[]{:S(2)}) async-start(), calls=%async_computation.10 | async-start | bytes 13369344 | tf_op jit(solution)/shard_map/all_gather | solution.py:86
  7.9 1003.7 %all-gather.7.cloned.1.call-start = ((), (), s32[]{:S(2)}) async-start(), calls=%async_computation.11 | async-start | bytes 4456448 | tf_op jit(solution)/shard_map/all_gather | solution.py:87
  8.7 1008.9 %all-gather.9.cloned.1.call-start = ((), (), s32[]{:S(2)}) async-start(), calls=%async_computation.12 | async-start | bytes 17825792 | tf_op jit(solution)/shard_map/all_gather | solution.py:88
  43.3 836.6 %all-to-all-start = ((bf16[9,128,6144]{1,0,2:T(8,128)(2,1)}), bf16[9,128,6144]{1,0,2:T(8,128)(2,1)}, u32[]{:S(2)}, u32[]{:S(2)}) async-start(bf16[9,128,6144]{1,0,2:T(8,128)(2,1)} %copy.309), calls=%async_computation | async-start | bytes 50331648 | tf_op jit(solution)/shard_map/all_to_all | solution.py:82
  49.7 992.7 %all-gather.11.cloned.1.call-start = ((), (), s32[]{:S(2)}) async-start(), calls=%async_computation.13 | async-start | bytes 17825792 | tf_op jit(solution)/shard_map/all_gather | solution.py:89
  58.5 38.9 %copy-start.78 = (s32[1,384]{1,0:T(1,128)S(1)}, s32[1,384]{1,0:T(1,128)}, u32[]{:S(2)}) copy-start(s32[1,384]{1,0:T(1,128)} %param.16) | copy-start | bytes 4612
  58.5 38.9 %copy-start.77 = (bf16[5,128]{1,0:T(8,128)(2,1)S(1)}, bf16[5,128]{1,0:T(8,128)(2,1)}, u32[]{:S(2)}) copy-start(bf16[5,128]{1,0:T(8,128)(2,1)} %param.25) | copy-start | bytes 3844
  851.1 142.7 %copy-start.45 = (f32[1,2048]{1,0:T(1,128)}, f32[1,2048]{1,0:T(1,128)S(1)}, u32[]{:S(2)}) copy-start(f32[1,2048]{1,0:T(1,128)S(1)} %get-tuple-element.185) | copy-start | bytes 24580
  851.1 149.3 %copy-start.43 = (f32[1,2048]{1,0:T(1,128)}, f32[1,2048]{1,0:T(1,128)S(1)}, u32[]{:S(2)}) copy-start(f32[1,2048]{1,0:T(1,128)S(1)} %get-tuple-element.184) | copy-start | bytes 24580
  851.1 154.2 %copy-start.41 = (f32[1,2048]{1,0:T(1,128)}, f32[1,2048]{1,0:T(1,128)S(1)}, u32[]{:S(2)}) copy-start(f32[1,2048]{1,0:T(1,128)S(1)} %get-tuple-element.186) | copy-start | bytes 24580
  879.9 194.9 %all-to-all-start.2 = ((bf16[16,2,24576]{2,1,0:T(2,128)(2,1)}), bf16[16,2,24576]{2,1,0:T(2,128)(2,1)}, u32[]{:S(2)}, u32[]{:S(2)}) async-start(bf16[16,2,24576]{2,1,0:T(2,128)(2,1)} %reshape.487), calls=%async_computation.2 | async-start | bytes 3145728 | tf_op jit(solution)/shard_map/all_to_all | solution.py:83
  884.5 258.1 %all-reduce.4.cloned.1.call-start = ((), (), s32[]{:S(2)}) async-start(), calls=%async_computation.14 | async-start | bytes 6291456 | tf_op jit(solution)/shard_map/psum | solution.py:132
  930.4 49.4 %copy-start.3 = (f32[384,2048]{1,0:T(8,128)}, f32[384,2048]{1,0:T(8,128)S(1)}, u32[]{:S(2)}) copy-start(f32[384,2048]{1,0:T(8,128)S(1)} %copy.312) | copy-start | bytes 9437188
  992.5 12.8 copy-start.1
  993.7 9.3 copy-start.67
  993.7 9.3 copy-start.65
  1042.4 14.5 copy-start.20
  1056.9 17.2 copy-start.80
  1057.0 310.8 %all-reduce.6.cloned.1.call-start = ((), (), s32[]{:S(2)}) async-start(), calls=%async_computation.21 | async-start | bytes 12582912 | tf_op jit(solution)/shard_map/psum | solution.py:204
  1089.7 56.1 %copy-start.49 = (f32[1,2048]{1,0:T(1,128)S(1)}, f32[1,2048]{1,0:T(1,128)}, u32[]{:S(2)}) copy-start(f32[1,2048]{1,0:T(1,128)} %get-tuple-element.182) | copy-start | bytes 24580
  1158.6 8.8 slice-start
  1172.8 30.1 %slice-start.2 = ((s8[12582912]{0:T(1024)(128)(4,1)}), s8[4194304]{0:T(1024)(128)(4,1)S(1)}, s32[]{:S(2)}) async-start(s8[12582912]{0:T(1024)(128)(4,1)} %bitcast.328), calls=%async_computation.24 | async-start | bytes 8388608
  1172.8 30.1 %slice-start.3 = ((s8[12582912]{0:T(1024)(128)(4,1)}), s8[4194304]{0:T(1024)(128)(4,1)S(1)}, s32[]{:S(2)}) async-start(s8[12582912]{0:T(1024)(128)(4,1)} %bitcast.328), calls=%async_computation.25 | async-start | bytes 8388608
  1190.5 12.4 slice-start.4
  1213.3 154.5 %copy-start.44 = (f32[1,2048]{1,0:T(1,128)S(1)}, f32[1,2048]{1,0:T(1,128)}, u32[]{:S(2)}) copy-start(f32[1,2048]{1,0:T(1,128)} %copy-done.43) | copy-start | bytes 24580
  1213.3 154.5 %copy-start.46 = (f32[1,2048]{1,0:T(1,128)S(1)}, f32[1,2048]{1,0:T(1,128)}, u32[]{:S(2)}) copy-start(f32[1,2048]{1,0:T(1,128)} %copy-done.45) | copy-start | bytes 24580
  1213.3 154.5 %copy-start.61 = (f32[384]{0:T(512)S(1)}, f32[384]{0:T(512)}, u32[]{:S(2)}) copy-start(f32[384]{0:T(512)} %copy-done.60) | copy-start | bytes 4612
  1213.3 154.5 %copy-start.63 = (f32[384]{0:T(512)S(1)}, f32[384]{0:T(512)}, u32[]{:S(2)}) copy-start(f32[384]{0:T(512)} %copy-done.62) | copy-start | bytes 4612
  1213.4 1209.2 %reduce-scatter.15.cloned.1.call-start = ((), (), s32[]{:S(2)}) async-start(), calls=%async_computation.19 | async-start | bytes 348160 | tf_op jit(solution)/shard_map/reduce_scatter | solution.py:232
  1214.5 1208.0 %reduce-scatter.17.cloned.1.call-start = ((), (), s32[]{:S(2)}) async-start(), calls=%async_computation.20 | async-start | bytes 69632 | tf_op jit(solution)/shard_map/reduce_scatter | solution.py:233
  1374.6 7.8 copy-start.29
  1381.9 1040.7 %reduce-scatter.9.cloned.1.call-start = ((), (), s32[]{:S(2)}) async-start(), calls=%async_computation.16 | async-start | bytes 8912896 | tf_op jit(solution)/shard_map/reduce_scatter | solution.py:229
  1388.1 1034.5 %reduce-scatter.7.cloned.1.call-start = ((), (), s32[]{:S(2)}) async-start(), calls=%async_computation.15 | async-start | bytes 26738688 | tf_op jit(solution)/shard_map/reduce_scatter | solution.py:228
  1411.3 1225.4 %reduce-scatter.11.cloned.1.call-start = ((), (), s32[]{:S(2)}) async-start(), calls=%async_computation.17 | async-start | bytes 35651584 | tf_op jit(solution)/shard_map/reduce_scatter | solution.py:230
  1429.2 1544.6 %reduce-scatter.13.cloned.1.call-start = ((), (), s32[]{:S(2)}) async-start(), calls=%async_computation.18 | async-start | bytes 35651584 | tf_op jit(solution)/shard_map/reduce_scatter | solution.py:231
  1491.2 11.2 copy-start.68
  1491.2 11.2 copy-start.66
  1495.7 114.4 %all-to-all-start.1 = ((bf16[16,2,24576]{2,1,0:T(2,128)(2,1)}), bf16[16,2,24576]{2,1,0:T(2,128)(2,1)S(1)}, u32[]{:S(2)}, u32[]{:S(2)}) async-start(bf16[16,2,24576]{2,1,0:T(2,128)(2,1)} %reshape.485), calls=%async_computation.1 | async-start | bytes 3145728 | tf_op jit(solution)/shard_map/all_to_all | solution.py:140
  1502.4 8.3 copy-start.5
  1502.4 8.7 copy-start.6
  1502.5 10.9 copy-start.7
  1502.5 11.8 copy-start.8
  1502.5 12.7 copy-start.9
  1502.5 13.5 copy-start.10
  1510.7 17.9 copy-start.11
  1610.1 737.7 %copy-start.74 = (bf16[40,40]{1,0:T(8,128)(2,1)S(1)}, bf16[40,40]{1,0:T(8,128)(2,1)}, u32[]{:S(2)}) copy-start(bf16[40,40]{1,0:T(8,128)(2,1)} %param.24) | copy-start | bytes 9604
  1611.3 761.6 %all-to-all-start.3 = ((bf16[9,2048,384]{2,0,1:T(8,128)(2,1)}), bf16[9,2048,384]{2,0,1:T(8,128)(2,1)}, u32[]{:S(2)}, u32[]{:S(2)}) async-start(bf16[9,2048,384]{2,0,1:T(8,128)(2,1)} %copy.339), calls=%async_computation.3 | async-start | bytes 50331648 | tf_op jit(solution)/shard_map/all_to_all | solution.py:226
  (55 other events, 193.3 us)
Sparse Core Ops, SparseCore 0:
  10.2 252.0 all-gather.4
  264.4 275.7 all-gather.6
  542.4 171.7 all-gather.8
  716.2 157.6 all-gather.10
  1057.1 85.3 all-reduce.3
  1213.5 154.2 all-reduce.5
  1371.8 50.8 reduce-scatter.14
  1426.6 50.8 reduce-scatter.16
  1482.7 128.1 reduce-scatter.8
  1616.0 682.3 reduce-scatter.6
  2303.8 332.8 reduce-scatter.10
  2642.0 331.7 reduce-scatter.12
where the time goes:
time: 3000 us; the launch traced here: 2980 us
  blocking collectives  1500 us (50%)
  waiting for transfers between devices  760 us (25%)
  local copies, waits for them, and re-layouts  294 us (10%)
  matrix products  213 us (7%)
  other arithmetic  174 us (6%)
    all_gather x1, blocking collectives, body(): lax.all_gather(gains, 'dp', axis=1, tiled=True)  752 us
    psum x1, blocking collectives, body(): grad_w_mix2 = lax.psum(grad_mix2_part, 'dp')  730 us
    reduce_scatter x1, waiting for transfers between devices, body(): lax.psum_scatter(grad_down_part, 'dp', scatter_dimension=0, tiled=True)  337 us
    reduce_scatter x1, waiting for transfers between devices, body(): lax.psum_scatter(grad_up_part, 'dp', scatter_dimension=0, tiled=True)  214 us
    psum x1, waiting for transfers between devices, body(): lax.psum(grad_normed_ff.astype(jnp.bfloat16), 'mp').astype(jnp.float32)  153 us
    unnamed x188, local copies, waits for them, and re-layouts  99.6 us
    unnamed x6, other arithmetic  69 us
  transfers between devices with their start and end apart: 16, of which 4 were waited for; matrix products, arithmetic and copies ran while one was open for 20% of the time, Pallas kernels for 0%

commit v1 on v0

--- a/solution.py
+++ b/solution.py
@@ -1,8 +1,11 @@
+import functools
 import math
 
 import jax
 import jax.numpy as jnp
 from jax import lax
+from jax.experimental import pallas as pl
+from jax.experimental.pallas import tpu as pltpu
 from jax.sharding import PartitionSpec as P
 
 HEAD = 128
@@ -11,6 +14,325 @@
 STREAMS = 4
 GROUPS = 8
 TOK_DEV = 384
+
+
+MESH = pl.DeviceIdType.MESH
+
+
+def chip_at(pos, ring):
+    far = pos // (ring // 2)
+    return (1 - far) * 2 * pos + far * (2 * (ring - 1 - pos) + 1)
+
+
+def place_of(chip, ring):
+    odd = chip % 2
+    return (1 - odd) * (chip // 2) + odd * (ring - 1 - chip // 2)
+
+
+def ring_places(n):
+    ring = n // 2
+    me = lax.axis_index("dp")
+    core = me % 2
+    place = place_of(me // 2, ring)
+
+    def owner(offset):
+        return chip_at((place + offset + 2 * ring) % ring, ring) * 2 + core
+
+    mate = me + 1 - 2 * core
+    return me, mate, owner, ring
+
+
+def greet(devices):
+    barrier = pltpu.get_barrier_semaphore()
+    for device in devices:
+        pl.semaphore_signal(barrier, inc=1, device_id=device, device_id_type=MESH)
+    pl.semaphore_wait(barrier, len(devices))
+
+
+def rows_of(ref, start, count):
+    if len(ref.shape) == 3:
+        return ref.at[:, pl.ds(start, count), :]
+    return ref.at[pl.ds(start, count), :]
+
+
+def gather_kernel(n, count, *refs):
+    shards, fulls = refs[:count], refs[count : 2 * count]
+    local_sem, ring_send, ring_recv, core_send, core_recv = refs[2 * count :]
+    me, mate, owner, ring = ring_places(n)
+    ahead, behind = owner(1), owner(-1)
+    size = shards[0].shape[-2]
+    half = size // 2
+    greet([{"dp": ahead}, {"dp": behind}, {"dp": mate}])
+    local = []
+    for i in range(count):
+        local.append(
+            pltpu.make_async_copy(shards[i], rows_of(fulls[i], me * size, size), local_sem.at[i])
+        )
+
+    def ring_copy(way, step, i, first=False):
+        origin = owner(-step if way == 0 else step)
+        start = pl.multiple_of(origin * size + way * half, half)
+        there = rows_of(fulls[i], start, half)
+        here = rows_of(shards[i], way * half, half) if first else there
+        return pltpu.make_async_remote_copy(
+            src_ref=here,
+            dst_ref=there,
+            send_sem=ring_send.at[way, step, i],
+            recv_sem=ring_recv.at[way, step, i],
+            device_id={"dp": ahead if way == 0 else behind},
+            device_id_type=MESH,
+        )
+
+    def ring_arrival(way, step, i):
+        origin = owner(-step - 1 if way == 0 else step + 1)
+        start = pl.multiple_of(origin * size + way * half, half)
+        there = rows_of(fulls[i], start, half)
+        return pltpu.make_async_remote_copy(
+            src_ref=there,
+            dst_ref=there,
+            send_sem=ring_send.at[way, step, i],
+            recv_sem=ring_recv.at[way, step, i],
+            device_id={"dp": ahead if way == 0 else behind},
+            device_id_type=MESH,
+        )
+
+    def core_copy(way, step, i, first=False):
+        origin = owner(-step if way == 0 else step)
+        start = pl.multiple_of(origin * size + way * half, half)
+        there = rows_of(fulls[i], start, half)
+        here = rows_of(shards[i], way * half, half) if first else there
+        return pltpu.make_async_remote_copy(
+            src_ref=here,
+            dst_ref=there,
+            send_sem=core_send.at[way, step, i],
+            recv_sem=core_recv.at[way, step, i],
+            device_id={"dp": mate},
+            device_id_type=MESH,
+        )
+
+    for i in range(count):
+        for way in range(2):
+            ring_copy(way, 0, i, True).start()
+    for i in range(count):
+        for way in range(2):
+            core_copy(way, 0, i, True).start()
+        local[i].start()
+
+    @pl.loop(1, ring - 1)
+    def _(step):
+        for i in range(count):
+            for way in range(2):
+                ring_arrival(way, step - 1, i).wait_recv()
+                ring_copy(way, step, i).start()
+                core_copy(way, step, i).start()
+
+    for i in range(count):
+        for way in range(2):
+            ring_arrival(way, ring - 2, i).wait_recv()
+            core_copy(way, ring - 1, i).start()
+
+    for i in range(count):
+        local[i].wait()
+
+    @pl.loop(0, ring)
+    def _(step):
+        for i in range(count):
+            for way in range(2):
+                core_copy(way, step, i).wait()
+
+    @pl.loop(0, ring - 1)
+    def _(step):
+        for i in range(count):
+            for way in range(2):
+                ring_copy(way, step, i).wait_send()
+
+
+def gather_rows(n, *shards):
+    count, ring = len(shards), n // 2
+    hbm = pl.BlockSpec(memory_space=pl.ANY)
+    return pl.pallas_call(
+        functools.partial(gather_kernel, n, count),
+        out_shape=[
+            jax.ShapeDtypeStruct(s.shape[:-2] + (s.shape[-2] * n, s.shape[-1]), s.dtype)
+            for s in shards
+        ],
+        in_specs=[hbm] * count,
+        out_specs=[hbm] * count,
+        scratch_shapes=[
+            pltpu.SemaphoreType.DMA((count,)),
+            pltpu.SemaphoreType.DMA((2, ring - 1, count)),
+            pltpu.SemaphoreType.DMA((2, ring - 1, count)),
+            pltpu.SemaphoreType.DMA((2, ring, count)),
+            pltpu.SemaphoreType.DMA((2, ring, count)),
+        ],
+        compiler_params=pltpu.CompilerParams(collective_id=0, has_side_effects=True),
+    )(*shards)
+
+
+def scatter_kernel(n, count, *refs):
+    parts, sums, mates = refs[:count], refs[count : 2 * count], refs[2 * count : 3 * count]
+    slots, own, other = (refs[(3 + k) * count : (4 + k) * count] for k in range(3))
+    own_sem, other_sem, ring_send, ring_recv, core_send, core_recv = refs[6 * count :]
+    me, mate, owner, ring = ring_places(n)
+    ahead, behind = owner(1), owner(-1)
+    size = sums[0].shape[-2]
+    half = size // 2
+    greet([{"dp": ahead}, {"dp": behind}, {"dp": mate}])
+
+    def target(way, step):
+        return -1 - step if way == 0 else 1 + step
+
+    def core_copy(way, step, i):
+        theirs = owner(target(way, step)) + (mate - me)
+        start = pl.multiple_of(theirs * size + way * half, half)
+        return pltpu.make_async_remote_copy(
+            src_ref=rows_of(parts[i], start, half),
+            dst_ref=mates[i].at[way, step],
+            send_sem=core_send.at[way, step, i],
+            recv_sem=core_recv.at[way, step, i],
+            device_id={"dp": mate},
+            device_id_type=MESH,
+        )
+
+    def own_copy(way, step, i):
+        start = pl.multiple_of(owner(target(way, step)) * size + way * half, half)
+        spot = step % 2
+        return pltpu.make_async_copy(
+            rows_of(parts[i], start, half), own[i].at[way, spot], own_sem.at[way, spot, i]
+        )
+
+    def other_copy(way, step, i):
+        spot = step % 2
+        return pltpu.make_async_copy(
+            mates[i].at[way, step], other[i].at[way, spot], other_sem.at[way, spot, i]
+        )
+
+    def ring_copy(way, step, i):
+        return pltpu.make_async_remote_copy(
+            src_ref=slots[i].at[way, step],
+            dst_ref=slots[i].at[way, step + 1],
+            send_sem=ring_send.at[way, step, i],
+            recv_sem=ring_recv.at[way, step, i],
+            device_id={"dp": ahead if way == 0 else behind},
+            device_id_type=MESH,
+        )
+
+    def stage(way, step, i):
+        own_copy(way, step, i).start()
+        core_copy(way, step, i).wait_recv()
+        other_copy(way, step, i).start()
+
+    def staged(way, step, i):
+        own_copy(way, step, i).wait()
+        other_copy(way, step, i).wait()
+
+    def chunks(i):
+        lead = parts[i].shape[0] if len(parts[i].shape) == 3 else 1
+        return lead, half // 16
+
+    def add(way, step, i, first):
+        spot = step % 2
+        lead, tall = chunks(i)
+        deep = len(parts[i].shape) == 3
+        slot, mine, theirs = slots[i].at[way, step], own[i].at[way, spot], other[i].at[way, spot]
+
+        for k in range(lead):
+            @pl.loop(0, tall)
+            def _(r):
+                rows = pl.ds(pl.multiple_of(r * 16, 16), 16)
+                at = (k, rows) if deep else (rows,)
+                total = mine[at].astype(jnp.float32) + theirs[at].astype(jnp.float32)
+                if not first:
+                    total = total + slot[at].astype(jnp.float32)
+                slot[at] = total.astype(slot.dtype)
+
+    def finish(way, step, i):
+        spot = step % 2
+        lead, tall = chunks(i)
+        deep = len(parts[i].shape) == 3
+        slot, mine, theirs = slots[i].at[way, step], own[i].at[way, spot], other[i].at[way, spot]
+
+        for k in range(lead):
+            @pl.loop(0, tall)
+            def _(r):
+                rows = pl.ds(pl.multiple_of(r * 16, 16), 16)
+                into = pl.ds(pl.multiple_of(way * half + r * 16, 16), 16)
+                at = (k, rows) if deep else (rows,)
+                total = mine[at].astype(jnp.float32) + theirs[at].astype(jnp.float32)
+                total = total + slot[at].astype(jnp.float32)
+                sums[i][(k, into) if deep else (into,)] = total
+
+    each = [(i, way) for i in range(count) for way in range(2)]
+    for step in range(2):
+        for i, way in each:
+            core_copy(way, step, i).start()
+    for i, way in each:
+        stage(way, 0, i)
+    for i, way in each:
+        staged(way, 0, i)
+        add(way, 0, i, True)
+        ring_copy(way, 0, i).start()
+        stage(way, 1, i)
+
+    @pl.loop(1, ring - 1)
+    def _(step):
+        for i, way in each:
+            core_copy(way, step + 1, i).start()
+        for i, way in each:
+            staged(way, step, i)
+            ring_copy(way, step - 1, i).wait_recv()
+            add(way, step, i, False)
+            ring_copy(way, step, i).start()
+            stage(way, step + 1, i)
+
+    for i, way in each:
+        staged(way, ring - 1, i)
+        ring_copy(way, ring - 2, i).wait_recv()
+        finish(way, ring - 1, i)
+
+    @pl.loop(0, ring - 1)
+    def _(step):
+        for i, way in each:
+            ring_copy(way, step, i).wait_send()
+
+    @pl.loop(0, ring)
+    def _(step):
+        for i, way in each:
+            core_copy(way, step, i).wait_send()
+
+
+def scatter_rows(n, *parts):
+    count, ring = len(parts), n // 2
+    hbm = pl.BlockSpec(memory_space=pl.ANY)
+    vmem = pl.BlockSpec(memory_space=pltpu.VMEM)
+    bf16 = jnp.bfloat16
+
+    def cut(s, rows):
+        return s.shape[:-2] + (rows, s.shape[-1])
+
+    half = parts[0].shape[-2] // n // 2
+    found = pl.pallas_call(
+        functools.partial(scatter_kernel, n, count),
+        out_shape=[jax.ShapeDtypeStruct(cut(s, 2 * half), jnp.float32) for s in parts]
+        + [jax.ShapeDtypeStruct((2, ring) + cut(s, half), bf16) for s in parts],
+        in_specs=[hbm] * count,
+        out_specs=[vmem] * count + [hbm] * count,
+        scratch_shapes=[pltpu.VMEM((2, ring) + cut(s, half), bf16) for s in parts]
+        + [pltpu.VMEM((2, 2) + cut(s, half), bf16) for s in parts]
+        + [pltpu.VMEM((2, 2) + cut(s, half), bf16) for s in parts]
+        + [
+            pltpu.SemaphoreType.DMA((2, 2, count)),
+            pltpu.SemaphoreType.DMA((2, 2, count)),
+            pltpu.SemaphoreType.DMA((2, ring - 1, count)),
+            pltpu.SemaphoreType.DMA((2, ring - 1, count)),
+            pltpu.SemaphoreType.DMA((2, ring, count)),
+            pltpu.SemaphoreType.DMA((2, ring, count)),
+        ],
+        compiler_params=pltpu.CompilerParams(
+            collective_id=1, has_side_effects=True, vmem_limit_bytes=56 * 1024 * 1024
+        ),
+    )(*parts)
+    return found[:count]
 
 
 def rms_norm(inputs, scales):
@@ -82,11 +404,9 @@
         lax.all_to_all(history, "dp", split_axis=2, concat_axis=1, tiled=True),
         lax.all_to_all(cot_out[None], "dp", split_axis=2, concat_axis=1, tiled=True),
     )
-    full_qkv, full_o, full_up, full_down, full_m1, full_gain = (
-        lax.all_gather(w_qkv, "dp", axis=1, tiled=True),
-        lax.all_gather(w_out, "dp", axis=0, tiled=True),
-        lax.all_gather(w_up, "dp", axis=0, tiled=True),
-        lax.all_gather(w_down, "dp", axis=0, tiled=True),
+    n = lax.axis_size("dp")
+    full_qkv, full_o, full_up, full_down = gather_rows(n, w_qkv, w_out, w_up, w_down)
+    full_m1, full_gain = (
         lax.all_gather(w_mix1, "dp", axis=0, tiled=True),
         lax.all_gather(gains, "dp", axis=1, tiled=True),
     )
@@ -138,13 +458,7 @@
     mix_hidden = gelu_exact(mix_pre).astype(bf16)
     mix_out = jnp.dot(mix_hidden, w_mix2, preferred_element_type=f32)
     out_hidden = lax.all_to_all(out_low.T[None], "dp", split_axis=1, concat_axis=2, tiled=True)[0]
-    back_qkv, back_o, back_up, back_down, back_m1 = (
-        lax.all_gather(w_qkv, "dp", axis=1, tiled=True),
-        lax.all_gather(w_out, "dp", axis=0, tiled=True),
-        lax.all_gather(w_up, "dp", axis=0, tiled=True),
-        lax.all_gather(w_down, "dp", axis=0, tiled=True),
-        lax.all_gather(w_mix1, "dp", axis=0, tiled=True),
-    )
+    back_qkv, back_o, back_up, back_down, back_m1 = full_qkv, full_o, full_up, full_down, full_m1
     row_scale = jnp.sum(
         jnp.where(group_ids[0][:, None] == jnp.arange(GROUPS)[None, :], group_scale[None, :], 0.0),
         axis=1,
@@ -224,11 +538,14 @@
         "tsj,tsd->jdt", mixing, grad_streams, precision=lax.Precision.HIGHEST
     ).astype(bf16)
     grad_history = lax.all_to_all(grad_hist_low, "dp", split_axis=1, concat_axis=2, tiled=True)
-    grad_qkv, grad_w_out, grad_w_up, grad_w_down, grad_w_mix1, grad_gains = (
-        lax.psum_scatter(grad_qkv_part, "dp", scatter_dimension=1, tiled=True),
-        lax.psum_scatter(grad_o_part, "dp", scatter_dimension=0, tiled=True),
-        lax.psum_scatter(grad_up_part, "dp", scatter_dimension=0, tiled=True),
-        lax.psum_scatter(grad_down_part, "dp", scatter_dimension=0, tiled=True),
+    grad_qkv, grad_w_out, grad_w_up, grad_w_down = scatter_rows(
+        n,
+        grad_qkv_part.astype(bf16),
+        grad_o_part.astype(bf16),
+        grad_up_part.astype(bf16),
+        grad_down_part.astype(bf16),
+    )
+    grad_w_mix1, grad_gains = (
         lax.psum_scatter(grad_m1_part, "dp", scatter_dimension=0, tiled=True),
         lax.psum_scatter(grad_gain_part, "dp", scatter_dimension=1, tiled=True),
     )

time: 3000 us -> 2420 us (0.81)
  Pallas kernels: 0 us -> 1470 us
  blocking collectives: 1500 us -> 76.1 us
  waiting for transfers between devices: 760 us -> 151 us
    pallas_call x0 -> x2, Pallas kernels: none -> 1470 us  [the longest x1 735 us: gather_rows(): pl.pallas_call(functools.partial(gather_kernel, n, count), out_shape=[jax...]
    all_gather x1, blocking collectives: 752 us -> 16 us  [body(): lax.all_gather(gains, 'dp', axis=1, tiled=True)]
    psum x1, blocking collectives: 730 us -> 43.5 us  [body(): grad_w_mix2 = lax.psum(grad_mix2_part, 'dp')]
    reduce_scatter x4 -> x0, waiting for transfers between devices: 551 us -> none  [the longest x1 337 us: body(): lax.psum_scatter(grad_down_part, 'dp', scatter_dimension=0, tiled=True)]
    psum x1, waiting for transfers between devices: 153 us -> 97.2 us  [body(): lax.psum(grad_normed_ff.astype(jnp.bfloat16), 'mp').astype(jnp.float32)]
    unnamed x188 -> x216, local copies, waits for them, and re-layouts: 99.6 us -> 102 us
    unnamed x6 -> x9, other arithmetic: 69 us -> 70.3 us
  transfers between devices with their start and end apart: 16 -> 8, of which waited for: 4 -> 2; matrix products, arithmetic and copies ran while one was open for 20% -> 23% of each run, Pallas kernels for 0% -> 61%
where the time goes in v1:
time: 2420 us; the launch traced here: 2400 us
  Pallas kernels  1470 us (61%)
  local copies, waits for them, and re-layouts  295 us (12%)
  matrix products  200 us (8%)
  other arithmetic  168 us (7%)
  waiting for transfers between devices  151 us (6%)
  blocking collectives  76.1 us (3%)
  starting transfers between devices  26.4 us (1%)
    pallas_call x1, Pallas kernels, gather_rows(): pl.pallas_call(functools.partial(gather_kernel, n, count), out_shape=[jax...  735 us
    pallas_call x1, Pallas kernels, scatter_rows(): pl.pallas_call(functools.partial(scatter_kernel, n, count), out_shape=[ja...  733 us
    unnamed x216, local copies, waits for them, and re-layouts  102 us
    psum x1, waiting for transfers between devices, body(): lax.psum(grad_normed_ff.astype(jnp.bfloat16), 'mp').astype(jnp.float32)  97.2 us
    unnamed x9, other arithmetic  70.3 us
    psum x1, waiting for transfers between devices, body(): branch = lax.psum(branch_part, 'mp')  53.4 us
  transfers between devices with their start and end apart: 8, of which 2 were waited for; matrix products, arithmetic and copies ran while one was open for 23% of the time, Pallas kernels for 61%

profile of v1, /device:TPU:21, one launch (start us, length us, event | category | flops | bytes accessed | tf_op | source)
XLA Modules:
  0.0 2399.2 jit_solution(3472924893833895010)
XLA Ops:
  7.2 33.5 %copy.309 = bf16[9,128,6144]{1,0,2:T(8,128)(2,1)} copy(bf16[9,128,6144]{2,1,0:T(8,128)(2,1)} %param.14) | data formatting | bytes 28311552 | tf_op args[0]
  40.7 6.6 all-to-all-start
  48.0 6.8 copy.330
  55.4 34.4 %reduce.2 = bf16[6144,128]{1,0:T(8,128)(2,1)} reduce(bf16[6144,1,128]{2,1,0:T(2,128)(2,1)S(1)} %bitcast.334, bf16[]{:T(256)} %broadcast.713), dimensions={1}, to_apply=%bitcast.267.reduce_sub_computation | reduce | bytes 3145730
  94.2 735.4 %shard_map.221 = (bf16[3,2048,1024]{2,1,0:T(8,128)(2,1)}, bf16[2048,1024]{1,0:T(8,128)(2,1)}, bf16[2048,4096]{1,0:T(8,128)(2,1)}, bf16[2048,4096]{1,0:T(8,128)(2,1)}) custom-call(bf16[3,128,1024]{2,1,0:T(8,128)(2,1)} %refs_0_.1, bf16[128,1024]{1,0:T(8,128)(2,1)} %refs_1_.1, bf16[128,4096]{1,0:T(8,128)(2,1)} %refs_2_.1, bf16[128,4096]{1,0:T(8,128)(2,1)} %refs_3_.1), custom_call_target="tpu_custom_call" | custom-call | tf_op jit(solution)/shard_map/pallas_call | solution.py:153
  829.6 9.1 slice_bitcast_fusion.2
  838.7 6.5 copy.354
  845.2 6.5 copy.355
  851.7 6.5 copy.356
  858.3 16.0 all_gather.6
  876.0 6.4 all-to-all-start.2
  882.6 30.7 %copy.311 = bf16[9,128,16,384]{3,1,2,0:T(8,128)(2,1)} copy(bf16[9,128,16,384]{1,0,3,2:T(8,128)(2,1)} %bitcast) | data formatting | bytes 28311552 | tf_op jit(solution)/shard_map/all_to_all | solution.py:404
  913.3 10.3 fusion.95
  928.0 6.1 convert_bitcast_fusion.4
  941.1 5.0 convert_bitcast_fusion.6
  953.2 5.0 convert_bitcast_fusion.8
  965.4 5.0 convert_bitcast_fusion.10
  977.4 12.7 multiply_add_fusion
  1009.2 4.9 fusion.98
  1014.1 23.1 multiply_convert_fusion
  1037.2 12.4 convolution_add_fusion
  1050.3 16.5 all_gather.7
  1066.9 8.1 reshape.488
  1081.8 53.4 %all-reduce.4.cloned.1.call-done = f32[384,2048]{1,0:T(8,128)} async-done(((f32[384,2048]{1,0:T(8,128)}), f32[384,2048]{1,0:T(8,128)}) %all-reduce.4.cloned.1.call-update) | async-done | bytes 3145744 | tf_op jit(solution)/shard_map/psum | solution.py:452
  1151.3 4.8 convolution_convert_fusion.5
  1165.1 17.8 add_convert_fusion
  1182.9 12.4 convolution_convert_fusion.3
  1207.0 8.6 copy.328
  1215.6 35.8 %reduce.3 = bf16[2048,384]{1,0:T(8,128)(2,1)} reduce(bf16[2048,1,384]{2,1,0:T(2,128)(2,1)} %bitcast.335, bf16[]{:T(256)} %broadcast.713), dimensions={1}, to_apply=%bitcast.265.reduce_sub_computation | reduce | bytes 3145730
  1255.9 6.3 all-to-all-start.1
  1262.2 97.2 %all-reduce.6.cloned.1.call-done = (bf16[384,2048]{1,0:T(8,128)(2,1)}, bf16[384,2048]{1,0:T(8,128)(2,1)}, bf16[384,2048]{1,0:T(8,128)(2,1)}, bf16[384,2048]{1,0:T(8,128)(2,1)}) async-done(((bf16[384,2048]{1,0:T(8,128)(2,1)}, bf16[384,2048]{1,0:T(8,128)(2,1)}, bf16[384,2048]{1,0:T(8,128)(2,1)}, bf16[384,2048]{1,0:T(8,128)(2,1)}), (bf16[384,2048]{1,0:T(8,128)(2,1)}, bf16[384,2048]{1,0:T(8,128)(2,1)}, ...) | async-done | bytes 6291472 | tf_op jit(solution)/shard_map/psum | solution.py:518
  1359.5 6.6 fusion.32
  1366.3 7.5 fusion.34
  1381.2 15.1 multiply_reduce_fusion.2
  1396.2 46.2 %convert_bitcast_fusion = bf16[9,2048,384]{1,0,2:T(8,128)(2,1)} fusion(f32[384,4,9]{2,1,0:T(4,128)} %copy.338, f32[384,4,2048]{2,0,1:T(8,128)S(1)} %get-tuple-element.166), kind=kOutput, calls=%fused_computation | convolution fusion | flops 346816512 | bytes 26793984 | tf_op jit(solution)/shard_map/tsj,tsd->jdt/dot_general | solution.py:537
  1442.4 35.3 %copy.339 = bf16[9,2048,384]{2,0,1:T(8,128)(2,1)} copy(bf16[9,2048,384]{1,0,2:T(8,128)(2,1)} %convert_bitcast_fusion) | data formatting | bytes 28311552 | tf_op jit(solution)/shard_map/convert_element_type | solution.py:539
  1477.7 6.5 all-to-all-start.3
  1485.7 5.9 convolution_convert_fusion.2.refs_1_
  1491.7 4.6 convert_bitcast_fusion.1
  1501.4 5.6 pad_maximum_fusion.1.refs_0_
  1507.0 14.3 convolution_convert_fusion.refs_3_
  1521.4 14.6 convolution_convert_fusion.1.refs_2_
  1536.0 732.7 %shard_map.222 = (f32[3,128,1024]{2,1,0:T(8,128)}, f32[128,1024]{1,0:T(8,128)}, f32[128,4096]{1,0:T(8,128)}, f32[128,4096]{1,0:T(8,128)}, bf16[2,8,3,64,1024]{4,...) custom-call(bf16[3,2048,1024]{2,1,0:T(8,128)(2,1)} %pad_maximum_fusi, ...), custom_call_target="tpu_custom_call" | custom-call | tf_op jit(solution)/shard_map/pallas_call | solution.py:314
  2268.8 43.5 %psum.47 = f32[40,40]{1,0:T(8,128)} all-reduce(f32[40,40]{1,0:T(8,128)S(1)} %fusion.102), channel_id=1, replica_groups=mesh['dp'=16,'mp'=2] {'dp'}, use_global_device_ids=true, to_apply=%region_29.30 | all-reduce | flops 1600 | bytes 12800 | tf_op jit(solution)/shard_map/psum | solution.py:552
  2313.1 8.1 reshape.486
  2328.7 7.6 multiply_reduce_fusion
  2337.1 30.0 %copy.341 = bf16[9,128,16,384]{1,3,2,0:T(8,128)(2,1)} copy(bf16[9,128,16,384]{3,0,1,2:T(8,128)(2,1)} %bitcast.73) | data formatting | bytes 28311552 | tf_op jit(solution)/shard_map/all_to_all | solution.py:540
  2367.2 18.6 copy.343
  (315 shorter events, 137.1 us)
Async XLA Ops:
  7.2 1132.3 %copy-start = (bf16[384,40]{0,1:T(8,128)(2,1)S(1)}, bf16[384,40]{0,1:T(8,128)(2,1)}, u32[]{:S(2)}) copy-start(bf16[384,40]{0,1:T(8,128)(2,1)} %param.27) | copy-start | bytes 92164
  40.7 835.3 %all-to-all-start = ((bf16[9,128,6144]{1,0,2:T(8,128)(2,1)}), bf16[9,128,6144]{1,0,2:T(8,128)(2,1)}, u32[]{:S(2)}, u32[]{:S(2)}) async-start(bf16[9,128,6144]{1,0,2:T(8,128)(2,1)} %copy.309), calls=%async_computation | async-start | bytes 50331648 | tf_op jit(solution)/shard_map/all_to_all | solution.py:404
  876.0 115.5 %copy-start.51 = (f32[1,2048]{1,0:T(1,128)}, f32[1,2048]{1,0:T(1,128)S(1)}, u32[]{:S(2)}) copy-start(f32[1,2048]{1,0:T(1,128)S(1)} %get-tuple-element.200) | copy-start | bytes 24580
  876.0 122.0 %copy-start.53 = (f32[1,2048]{1,0:T(1,128)}, f32[1,2048]{1,0:T(1,128)S(1)}, u32[]{:S(2)}) copy-start(f32[1,2048]{1,0:T(1,128)S(1)} %get-tuple-element.201) | copy-start | bytes 24580
  876.0 126.9 %copy-start.49 = (f32[1,2048]{1,0:T(1,128)}, f32[1,2048]{1,0:T(1,128)S(1)}, u32[]{:S(2)}) copy-start(f32[1,2048]{1,0:T(1,128)S(1)} %get-tuple-element.202) | copy-start | bytes 24580
  876.0 190.9 %all-to-all-start.2 = ((bf16[16,2,24576]{2,1,0:T(2,128)(2,1)}), bf16[16,2,24576]{2,1,0:T(2,128)(2,1)}, u32[]{:S(2)}, u32[]{:S(2)}) async-start(bf16[16,2,24576]{2,1,0:T(2,128)(2,1)} %reshape.487), calls=%async_computation.2 | async-start | bytes 3145728 | tf_op jit(solution)/shard_map/all_to_all | solution.py:405
  882.4 252.8 %all-reduce.4.cloned.1.call-start = ((), (), s32[]{:S(2)}) async-start(), calls=%async_computation.6 | async-start | bytes 6291456 | tf_op jit(solution)/shard_map/psum | solution.py:452
  928.0 49.4 %copy-start.3 = (f32[384,2048]{1,0:T(8,128)}, f32[384,2048]{1,0:T(8,128)S(1)}, u32[]{:S(2)}) copy-start(f32[384,2048]{1,0:T(8,128)S(1)} %copy.312) | copy-start | bytes 9437188
  990.1 24.0 copy-start.1
  991.4 11.5 copy-start.70
  1005.8 8.3 slice-start.11
  1005.8 8.4 slice-start.12
  1049.6 17.2 copy-start.78
  1049.6 309.8 %all-reduce.6.cloned.1.call-start = ((), (), s32[]{:S(2)}) async-start(), calls=%async_computation.9 | async-start | bytes 12582912 | tf_op jit(solution)/shard_map/psum | solution.py:518
  1081.8 56.7 %copy-start.42 = (f32[1,2048]{1,0:T(1,128)S(1)}, f32[1,2048]{1,0:T(1,128)}, u32[]{:S(2)}) copy-start(f32[1,2048]{1,0:T(1,128)} %get-tuple-element.198) | copy-start | bytes 24580
  1151.3 8.6 slice-start.6
  1165.1 30.2 %slice-start.8 = ((s8[12582912]{0:T(1024)(128)(4,1)}), s8[4194304]{0:T(1024)(128)(4,1)S(1)}, s32[]{:S(2)}) async-start(s8[12582912]{0:T(1024)(128)(4,1)} %bitcast.332), calls=%async_computation.18 | async-start | bytes 8388608
  1165.1 30.2 %slice-start.9 = ((s8[12582912]{0:T(1024)(128)(4,1)}), s8[4194304]{0:T(1024)(128)(4,1)S(1)}, s32[]{:S(2)}) async-start(s8[12582912]{0:T(1024)(128)(4,1)} %bitcast.332), calls=%async_computation.19 | async-start | bytes 8388608
  1182.9 12.4 slice-start.10
  1182.9 12.4 copy-start.82
  1251.4 107.9 %copy-start.52 = (f32[1,2048]{1,0:T(1,128)S(1)}, f32[1,2048]{1,0:T(1,128)}, u32[]{:S(2)}) copy-start(f32[1,2048]{1,0:T(1,128)} %copy-done.51) | copy-start | bytes 24580
  1251.4 107.9 %copy-start.54 = (f32[1,2048]{1,0:T(1,128)S(1)}, f32[1,2048]{1,0:T(1,128)}, u32[]{:S(2)}) copy-start(f32[1,2048]{1,0:T(1,128)} %copy-done.53) | copy-start | bytes 24580
  1251.4 107.9 %copy-start.67 = (f32[384]{0:T(512)S(1)}, f32[384]{0:T(512)}, u32[]{:S(2)}) copy-start(f32[384]{0:T(512)} %copy-done.66) | copy-start | bytes 4612
  1251.4 107.9 %copy-start.69 = (f32[384]{0:T(512)S(1)}, f32[384]{0:T(512)}, u32[]{:S(2)}) copy-start(f32[384]{0:T(512)} %copy-done.68) | copy-start | bytes 4612
  1255.9 221.9 %all-to-all-start.1 = ((bf16[16,2,24576]{2,1,0:T(2,128)(2,1)}), bf16[16,2,24576]{2,1,0:T(2,128)(2,1)}, u32[]{:S(2)}, u32[]{:S(2)}) async-start(bf16[16,2,24576]{2,1,0:T(2,128)(2,1)} %reshape.485), calls=%async_computation.1 | async-start | bytes 3145728 | tf_op jit(solution)/shard_map/all_to_all | solution.py:460
  1359.4 6.7 copy-start.65
  1359.4 6.7 copy-start.63
  1359.4 6.7 copy-start.61
  1359.4 6.7 copy-start.10
  1359.4 6.7 copy-start.11
  1359.4 6.7 copy-start.12
  1359.5 6.7 copy-start.50
  1359.5 6.7 copy-start.71
  1359.5 14.3 slice-start
  1359.5 14.3 slice-start.1
  1366.2 7.5 copy-start.59
  1366.2 8.1 slice-start.2
  1366.2 9.4 copy-start.7
  1366.2 9.8 copy-start.9
  1477.7 7.9 copy-start.81
  1477.7 859.4 %all-to-all-start.3 = ((bf16[9,2048,384]{2,0,1:T(8,128)(2,1)}), bf16[9,2048,384]{2,0,1:T(8,128)(2,1)}, u32[]{:S(2)}, u32[]{:S(2)}) async-start(bf16[9,2048,384]{2,0,1:T(8,128)(2,1)} %copy.339), calls=%async_computation.3 | async-start | bytes 50331648 | tf_op jit(solution)/shard_map/all_to_all | solution.py:540
  1484.2 901.6 %reduce-scatter.3.cloned.1.call-start = ((), (), s32[]{:S(2)}) async-start(), calls=%async_computation.7 | async-start | bytes 348160 | tf_op jit(solution)/shard_map/reduce_scatter | solution.py:549
  1485.4 900.4 %reduce-scatter.5.cloned.1.call-start = ((), (), s32[]{:S(2)}) async-start(), calls=%async_computation.8 | async-start | bytes 69632 | tf_op jit(solution)/shard_map/reduce_scatter | solution.py:550
  1485.7 10.5 slice-start.3
  1485.7 10.5 slice-start.4
  1521.4 14.6 copy-start.41
  1521.4 14.6 copy-start.56
  1536.0 776.4 %copy-start.73 = (bf16[40,40]{1,0:T(8,128)(2,1)S(1)}, bf16[40,40]{1,0:T(8,128)(2,1)}, u32[]{:S(2)}) copy-start(bf16[40,40]{1,0:T(8,128)(2,1)} %param.24) | copy-start | bytes 9604
  (59 other events, 208.8 us)
Sparse Core Ops, SparseCore 0:
  1049.7 85.4 all-reduce.3
  1205.1 154.2 all-reduce.5
  1489.7 406.3 reduce-scatter.2
  2328.8 55.7 reduce-scatter.4

commit v2 on v0

v2 whole, which is shorter than its diff:
```python
import functools
import math

import jax
import jax.numpy as jnp
from jax import lax
from jax.experimental import pallas as pl
from jax.experimental.pallas import tpu as pltpu
from jax.sharding import PartitionSpec as P

HEAD = 128
ROT = 32
HIST = 9
STREAMS = 4
GROUPS = 8
TOK_DEV = 384
MIXH = 40
WIDE = 128
EPS = 1e-05
MESH = pl.DeviceIdType.MESH
DMA = pltpu.SemaphoreType.DMA
f32 = jnp.float32
bf16 = jnp.bfloat16


def chip_at(pos, ring):
    far = pos // (ring // 2)
    return (1 - far) * 2 * pos + far * (2 * (ring - 1 - pos) + 1)


def place_of(chip, ring):
    odd = chip % 2
    return (1 - odd) * (chip // 2) + odd * (ring - 1 - chip // 2)


def remote(src, dst, send, recv, device):
    return pltpu.make_async_remote_copy(
        src_ref=src,
        dst_ref=dst,
        send_sem=send,
        recv_sem=recv,
        device_id=device,
        device_id_type=MESH,
    )


def greet_plane(n, me, mp):
    barrier = pltpu.get_barrier_semaphore()

    @pl.loop(1, n)
    def _(k):
        pl.semaphore_signal(barrier, inc=1, device_id={"dp": (me + k) % n}, device_id_type=MESH)

    pl.semaphore_signal(barrier, inc=1, device_id={"mp": 1 - mp}, device_id_type=MESH)
    pl.semaphore_wait(barrier, n)


def rows_of(ref, start, count):
    if len(ref.shape) == 3:
        return ref.at[:, pl.ds(start, count), :]
    return ref.at[pl.ds(start, count), :]


class Ring:
    def __init__(self, n):
        self.n, self.ring = n, n // 2
        self.me = lax.axis_index("dp")
        self.core = self.me % 2
        self.place = place_of(self.me // 2, self.ring)
        self.mate = self.me + 1 - 2 * self.core
        self.next_of = ({"dp": self.owner(1)}, {"dp": self.owner(-1)})

    def owner(self, offset):
        return chip_at((self.place + offset + 2 * self.ring) % self.ring, self.ring) * 2 + self.core


def forward_kernel(n, count, *refs):
    hist, cot, mix, small = refs[:4]
    shards = refs[4 : 4 + count]
    inputs, mixes, smalls = refs[4 + count : 7 + count]
    fulls = refs[7 + count : 7 + 2 * count]
    (
        hist_buf,
        slots,
        hist_sem,
        cot_sem,
        own_sem,
        local_sem,
        mix_send,
        mix_recv,
        small_send,
        small_recv,
        a_send,
        a_recv,
        y_send,
        y_recv,
        ring_send,
        ring_recv,
        core_send,
        core_recv,
    ) = refs[7 + 2 * count :]
    where = Ring(n)
    me, ring, owner = where.me, where.ring, where.owner
    mp = lax.axis_index("mp")
    across = {"mp": 1 - mp}
    feat, tokens = hist.shape[1], mix.shape[1]
    h = feat // 2
    size = shards[0].shape[-2]
    half = size // 2
    greet_plane(n, me, mp)

    def origin_rows(offset, way):
        return pl.multiple_of(owner(offset) * size + way * half, half)

    def ring_copy(way, step, i, first=False):
        there = rows_of(fulls[i], origin_rows(-step if way == 0 else step, way), half)
        here = rows_of(shards[i], way * half, half) if first else there
        return remote(
            here, there, ring_send.at[way, step, i], ring_recv.at[way, step, i], where.next_of[way]
        )

    def ring_arrival(way, step, i):
        there = rows_of(fulls[i], origin_rows(-step - 1 if way == 0 else step + 1, way), half)
        return remote(
            there, there, ring_send.at[way, step, i], ring_recv.at[way, step, i], where.next_of[way]
        )

    def core_copy(way, step, i, first=False):
        there = rows_of(fulls[i], origin_rows(-step if way == 0 else step, way), half)
        here = rows_of(shards[i], way * half, half) if first else there
        return remote(
            here, there, core_send.at[way, step, i], core_recv.at[way, step, i], {"dp": where.mate}
        )

    def shard_copy(i):
        return pltpu.make_async_copy(shards[i], rows_of(fulls[i], me * size, size), local_sem.at[i])

    def turn(q):
        return (q + 1) % n

    def mix_copy(q):
        return remote(
            mix, mixes.at[me], mix_send.at[q], mix_recv.at[q], {"dp": (me + turn(q)) % n}
        )

    def small_copy(q):
        return remote(
            small,
            smalls.at[pl.ds(pl.multiple_of(me * feat, feat), feat)],
            small_send.at[q],
            small_recv.at[q],
            {"dp": (me + turn(q)) % n},
        )

    def lanes(peer):
        return pl.ds(pl.multiple_of(peer * tokens, 128), tokens)

    def hist_copy(q):
        peer = (me + turn(q)) % n
        return pltpu.make_async_copy(
            hist.at[:, pl.ds(pl.multiple_of(mp * h, h), h), lanes(peer)],
            hist_buf.at[q % 2],
            hist_sem.at[q % 2],
        )

    def cot_copy(q):
        peer = (me + turn(q)) % n
        return pltpu.make_async_copy(
            cot.at[pl.ds(pl.multiple_of(mp * h, h), h), lanes(peer)],
            slots.at[q, STREAMS],
            cot_sem.at[q],
        )

    def features(source, plane):
        return inputs.at[:, pl.ds(pl.multiple_of(source * feat + plane * h, h), h), :]

    def stream_copy(q):
        return remote(
            slots.at[q], features(me, mp), a_send.at[q], a_recv.at[q], {"dp": (me + turn(q)) % n}
        )

    def own_copy():
        return pltpu.make_async_copy(slots.at[n - 1], features(me, mp), own_sem)

    def across_copy(q, own=False):
        there = features((me - turn(q) + n) % n, mp)
        return remote(
            slots.at[n - 1] if own else there, there, y_send.at[q], y_recv.at[q], across
        )

    def mix_streams(q):
        peer = (me + turn(q)) % n

        @pl.loop(0, h // 16)
        def _(r):
            rows = pl.ds(pl.multiple_of(r * 16, 16), 16)
            sums = [None] * STREAMS
            for j in range(HIST):
                entry = hist_buf[q % 2, j, rows, :].astype(f32)
                for s in range(STREAMS):
                    term = mixes[peer, pl.ds(s * HIST + j, 1), :] * entry
                    sums[s] = term if j == 0 else sums[s] + term
            for s in range(STREAMS):
                slots[q, s, rows, :] = sums[s].astype(bf16)

    pieces = [(i, way) for i in range(count) for way in range(2)]

    @pl.loop(0, n - 1)
    def _(q):
        mix_copy(q).start()
        small_copy(q).start()
        cot_copy(q).start()

    cot_copy(n - 1).start()
    hist_copy(0).start()
    for i, way in pieces:
        ring_copy(way, 0, i, True).start()
    own_small = pltpu.make_async_copy(
        small, smalls.at[pl.ds(pl.multiple_of(me * feat, feat), feat)], local_sem.at[count]
    )
    own_small.start()
    mixes[me] = mix[...]

    @pl.loop(0, n - 1)
    def _(q):
        hist_copy(q).wait()
        hist_copy(q + 1).start()
        mix_copy(n - 2 - q).wait_recv()
        mix_streams(q)
        cot_copy(q).wait()
        stream_copy(q).start()

    hist_copy(n - 1).wait()
    mix_streams(n - 1)
    cot_copy(n - 1).wait()
    own_copy().start()
    across_copy(n - 1, True).start()
    for i, way in pieces:
        core_copy(way, 0, i, True).start()
    for i in range(count):
        shard_copy(i).start()

    @pl.loop(1, ring - 1)
    def _(step):
        for i, way in pieces:
            ring_arrival(way, step - 1, i).wait_recv()
            ring_copy(way, step, i).start()
            core_copy(way, step, i).start()
        for k in range(2):
            q = (step - 1) * 2 + k
            stream_copy(q).wait_recv()
            across_copy(q).start()

    @pl.loop((ring - 2) * 2, n - 1)
    def _(q):
        stream_copy(q).wait_recv()
        across_copy(q).start()

    for i, way in pieces:
        ring_arrival(way, ring - 2, i).wait_recv()
        core_copy(way, ring - 1, i).start()

    own_copy().wait()
    own_small.wait()
    for i in range(count):
        shard_copy(i).wait()

    @pl.loop(0, n - 1)
    def _(q):
        mix_copy(q).wait_send()
        small_copy(q).wait()
        stream_copy(q).wait_send()

    @pl.loop(0, n)
    def _(q):
        across_copy(q).wait()

    @pl.loop(0, ring)
    def _(step):
        for i, way in pieces:
            core_copy(way, step, i).wait()

    @pl.loop(0, ring - 1)
    def _(step):
        for i, way in pieces:
            ring_copy(way, step, i).wait_send()


def forward_exchange(n, history, cot_out, mix, small, shards):
    count, ring = len(shards), n // 2
    feat, tokens = history.shape[1], mix.shape[1]
    h = feat // 2
    hbm = pl.BlockSpec(memory_space=pl.ANY)
    vmem = pl.BlockSpec(memory_space=pltpu.VMEM)
    found = pl.pallas_call(
        functools.partial(forward_kernel, n, count),
        out_shape=[
            jax.ShapeDtypeStruct((STREAMS + 1, n * feat, tokens), bf16),
            jax.ShapeDtypeStruct((n,) + mix.shape, f32),
            jax.ShapeDtypeStruct((n * feat, WIDE), bf16),
        ]
        + [
            jax.ShapeDtypeStruct(s.shape[:-2] + (s.shape[-2] * n, s.shape[-1]), s.dtype)
            for s in shards
        ],
        in_specs=[hbm, hbm, vmem, hbm] + [hbm] * count,
        out_specs=[hbm, vmem, hbm] + [hbm] * count,
        scratch_shapes=[
            pltpu.VMEM((2, HIST, h, tokens), bf16),
            pltpu.VMEM((n, STREAMS + 1, h, tokens), bf16),
            DMA((2,)),
            DMA((n,)),
            DMA,
            DMA((count + 1,)),
        ]
        + [DMA((n,)) for _ in range(8)]
        + [DMA((2, ring - 1, count)) for _ in range(2)]
        + [DMA((2, ring, count)) for _ in range(2)],
        compiler_params=pltpu.CompilerParams(
            collective_id=0, has_side_effects=True, vmem_limit_bytes=32 * 1024 * 1024
        ),
    )(history, cot_out, mix, small, *shards)
    return found[0], found[1], found[2], found[3:]


def backward_kernel(n, count, *refs):
    grads, inner, scale, inputs, direct, output, smalls, little, second, hist, mixes = refs[:11]
    parts = refs[11 : 11 + count]
    refs = refs[11 + count :]
    across_land, feature_side, mix_sum, little_sum, second_sum = refs[:5]
    sums, mates = refs[5 : 5 + count], refs[5 + count : 5 + 2 * count]
    refs = refs[5 + 2 * count :]
    slots, own, other, final = (refs[k * count : (k + 1) * count] for k in range(4))
    (
        inner_land,
        d_buf,
        e_buf,
        x_buf,
        go_buf,
        g_buf,
        l_buf,
        g_slots,
        l_slots,
        l_land,
        second_land,
        f_buf,
        h_buf,
        m_slots,
        m_land,
        m_mine,
        m_other,
        l_sum,
        load_sem,
        out_sem,
        back_sem,
        own_sem,
        other_sem,
        final_sem,
        y_send,
        y_recv,
        p_sem,
        a_send,
        a_recv,
        l_send,
        l_recv,
        w_send,
        w_recv,
        fy_send,
        fy_recv,
        m_send,
        m_recv,
        end_sem,
        ring_send,
        ring_recv,
        core_send,
        core_recv,
    ) = refs[4 * count :]
    where = Ring(n)
    me, ring, owner = where.me, where.ring, where.owner
    mp = lax.axis_index("mp")
    across = {"mp": 1 - mp}
    feat, tokens = hist.shape[1], inner.shape[1]
    h = feat // 2
    size = sums[0].shape[-2]
    half = size // 2
    greet_plane(n, me, mp)

    def target(way, step):
        return -1 - step if way == 0 else 1 + step

    def core_copy(way, step, i):
        theirs = owner(target(way, step)) + (where.mate - me)
        start = pl.multiple_of(theirs * size + way * half, half)
        return remote(
            rows_of(parts[i], start, half),
            mates[i].at[way, step],
            core_send.at[way, step, i],
            core_recv.at[way, step, i],
            {"dp": where.mate},
        )

    def own_copy(way, step, i):
        start = pl.multiple_of(owner(target(way, step)) * size + way * half, half)
        spot = step % 2
        return pltpu.make_async_copy(
            rows_of(parts[i], start, half), own[i].at[way, spot], own_sem.at[way, spot, i]
        )

    def other_copy(way, step, i):
        spot = step % 2
        return pltpu.make_async_copy(
            mates[i].at[way, step], other[i].at[way, spot], other_sem.at[way, spot, i]
        )

    def ring_copy(way, step, i):
        return remote(
            slots[i].at[way, step],
            slots[i].at[way, step + 1],
            ring_send.at[way, step, i],
            ring_recv.at[way, step, i],
            where.next_of[way],
        )

    def final_copy(way, i):
        return pltpu.make_async_copy(
            final[i], rows_of(sums[i], way * half, half), final_sem.at[i]
        )

    def stage(way, step, i):
        own_copy(way, step, i).start()
        core_copy(way, step, i).wait_recv()
        other_copy(way, step, i).start()

    def staged(way, step, i):
        own_copy(way, step, i).wait()
        other_copy(way, step, i).wait()

    def add(way, step, i, first=False, last=False):
        spot = step % 2
        deep = len(parts[i].shape) == 3
        slot, mine, theirs = slots[i].at[way, step], own[i].at[way, spot], other[i].at[way, spot]
        for k in range(parts[i].shape[0] if deep else 1):

            @pl.loop(0, half // 16)
            def _(r):
                rows = pl.ds(pl.multiple_of(r * 16, 16), 16)
                at = (k, rows) if deep else (rows,)
                total = mine[at].astype(f32) + theirs[at].astype(f32)
                if not first:
                    total = total + slot[at].astype(f32)
                if last:
                    final[i][at] = total
                else:
                    slot[at] = total.astype(bf16)

    def turn(q):
        return (q + 1) % n

    def span(peer, plane):
        return pl.ds(pl.multiple_of(peer * feat + plane * h, h), h)

    def sum_copy(q):
        peer = (me + turn(q)) % n
        return remote(
            grads.at[:, span(peer, 1 - mp), :],
            across_land.at[q],
            y_send.at[q],
            y_recv.at[q],
            across,
        )

    def inner_copy():
        return remote(inner, inner_land, p_sem.at[0], p_sem.at[1], across)

    def loads(q):
        rows = span((me + turn(q)) % n, mp)
        spot = q % 2
        return [
            pltpu.make_async_copy(grads.at[:, rows, :], d_buf.at[spot], load_sem.at[spot, 0]),
            pltpu.make_async_copy(across_land.at[q], e_buf.at[spot], load_sem.at[spot, 1]),
            pltpu.make_async_copy(
                inputs.at[pl.ds(0, STREAMS), rows, :], x_buf.at[spot], load_sem.at[spot, 2]
            ),
            pltpu.make_async_copy(direct.at[rows, :], go_buf.at[spot], load_sem.at[spot, 3]),
            pltpu.make_async_copy(smalls.at[rows, :], g_buf.at[spot], load_sem.at[spot, 4]),
            pltpu.make_async_copy(little.at[rows, :], l_buf.at[spot], load_sem.at[spot, 5]),
        ]

    def out_copy(q):
        rows = span((me + turn(q)) % n, mp)
        return pltpu.make_async_copy(output.at[rows, :], g_slots.at[q, STREAMS], out_sem.at[q])

    def place(source, plane):
        return feature_side.at[source, :, pl.ds(pl.multiple_of(plane * h, h), h), :]

    def stream_copy(q):
        return remote(
            g_slots.at[q], place(me, mp), a_send.at[q], a_recv.at[q], {"dp": (me + turn(q)) % n}
        )

    def little_copy(q):
        return remote(
            l_slots.at[q], l_land.at[q], l_send.at[q], l_recv.at[q], {"dp": (me + turn(q)) % n}
        )

    def second_copy(q):
        return remote(
            second, second_land.at[me], w_send.at[q], w_recv.at[q], {"dp": (me + turn(q)) % n}
        )

    def home_copy():
        return pltpu.make_async_copy(g_slots.at[n - 1], place(me, mp), end_sem.at[0])

    def across_copy(q, own=False):
        there = place((me - turn(q) + n) % n, mp)
        return remote(
            g_slots.at[n - 1] if own else there, there, fy_send.at[q], fy_recv.at[q], across
        )

    def start_loads(q):
        sum_copy(q).wait_recv()
        for copy in loads(q):
            copy.start()

    def norm_backward(q):
        spot = q % 2
        for copy in loads(q):
            copy.wait()

        @pl.loop(0, h // 16)
        def _(r):
            rows = pl.ds(pl.multiple_of(r * 16, 16), 16)
            tail = l_buf[spot, rows, :]
            lane = lax.broadcasted_iota(jnp.int32, tail.shape, 1)
            for s in range(STREAMS):
                dy = d_buf[spot, s, rows, :].astype(f32) + e_buf[spot, s, rows, :].astype(f32)
                level = scale[pl.ds(s, 1), :]
                common = (inner[pl.ds(s, 1), :] + inner_land[pl.ds(s, 1), :]) * level
                common = common * (1.0 / (n * feat))
                unit = x_buf[spot, s, rows, :].astype(f32) * level
                gain = g_buf[spot, rows, :].astype(f32)[:, MIXH + s : MIXH + s + 1]
                grad = level * (gain * dy) - unit * common
                if s == STREAMS - 1:
                    grad = grad + go_buf[spot, rows, :]
                g_slots[q, s, rows, :] = grad.astype(bf16)
                gain_grad = jnp.sum(unit * dy, axis=1, keepdims=True)
                tail = jnp.where(lane == MIXH + s, gain_grad, tail)
            l_slots[q, rows, :] = tail

    def norm_turn(q, last=False):
        if not last:
            start_loads(q + 1)
        norm_backward(q)
        out_copy(q).wait()
        if last:
            home_copy().start()
            across_copy(q, True).start()
        else:
            stream_copy(q).start()
            little_copy(q).start()

    def hist_load(q):
        source = (me - turn(q) + n) % n
        return pltpu.make_async_copy(
            hist.at[
                :,
                pl.ds(pl.multiple_of(mp * h, h), h),
                pl.ds(pl.multiple_of(source * tokens, 128), tokens),
            ],
            h_buf.at[q % 2],
            back_sem.at[q % 2, 0],
        )

    def grad_load(q):
        source = (me - turn(q) + n) % n
        return pltpu.make_async_copy(
            feature_side.at[source, pl.ds(0, STREAMS), pl.ds(pl.multiple_of(mp * h, h), h), :],
            f_buf,
            back_sem.at[0, 1],
        )

    def mix_copy(q):
        return remote(
            m_slots.at[q],
            m_land.at[q],
            m_send.at[q],
            m_recv.at[q],
            {"dp": (me - turn(q) + n) % n},
        )

    def mix_backward(q):
        for s in range(STREAMS):
            totals = [None] * HIST
            for r in range(h // 16):
                grad = f_buf[s, r * 16 : r * 16 + 16, :].astype(f32)
                for j in range(HIST):
                    both = h_buf[q % 2, j, r * 16 : r * 16 + 16, :].astype(f32) * grad
                    both = both[0:8] + both[8:16]
                    totals[j] = both if r == 0 else totals[j] + both
            for j in range(HIST):
                m_slots[q, pl.ds(s * HIST + j, 1), :] = jnp.sum(totals[j], axis=0, keepdims=True)

    def mix_turn(q, last=False):
        if last:
            home_copy().wait()
        else:
            hist_load(q + 1).start()
            stream_copy(q).wait_recv()
            across_copy(q).start()
        grad_load(q).start()
        grad_load(q).wait()
        hist_load(q).wait()
        mix_backward(q)
        if not last:
            mix_copy(q).start()

    pieces = [(i, way) for i in range(count) for way in range(2)]
    units = len(pieces)

    inner_copy().start()
    for step in range(2):
        for i, way in pieces:
            core_copy(way, step, i).start()

    @pl.loop(0, n)
    def _(q):
        sum_copy(q).start()
        out_copy(q).start()

    second_land[me] = second[...]

    @pl.loop(0, n - 1)
    def _(q):
        second_copy(q).start()

    for i, way in pieces:
        stage(way, 0, i)
    for i, way in pieces:
        staged(way, 0, i)
        add(way, 0, i, first=True)
        ring_copy(way, 0, i).start()
        stage(way, 1, i)
    inner_copy().wait()
    start_loads(0)

    def ring_unit(step, i, way):
        staged(way, step, i)
        ring_copy(way, step - 1, i).wait_recv()
        add(way, step, i)
        ring_copy(way, step, i).start()
        stage(way, step + 1, i)

    def mates_ahead(step):
        for i, way in pieces:
            core_copy(way, step + 1, i).start()

    turns = n // units

    @pl.loop(1, 1 + turns)
    def _(step):
        mates_ahead(step)
        for u, (i, way) in enumerate(pieces):
            ring_unit(step, i, way)
            q = (step - 1) * units + u
            if u < units - 1:
                norm_turn(q)
            else:

                @pl.when(step < turns)
                def _():
                    norm_turn(q)

    norm_turn(n - 1, True)
    hist_load(0).start()

    @pl.loop(1 + turns, 1 + 2 * turns)
    def _(step):
        mates_ahead(step)
        for u, (i, way) in enumerate(pieces):
            ring_unit(step, i, way)
            q = (step - 1 - turns) * units + u
            if u < units - 1:
                mix_turn(q)
            else:

                @pl.when(step < 2 * turns)
                def _():
                    mix_turn(q)

    mix_turn(n - 1, True)

    @pl.loop(1 + 2 * turns, ring - 1)
    def _(step):
        mates_ahead(step)
        for i, way in pieces:
            ring_unit(step, i, way)

    @pl.loop(0, n - 1)
    def _(q):
        little_copy(q).wait_recv()
        second_copy(q).wait_recv()
        mix_copy(q).wait_recv()

    def sum_over(land, mine):
        return lax.fori_loop(0, n - 1, lambda q, total: total + land[q], mine)

    l_sum[...] = sum_over(l_land, l_slots[n - 1])
    m_mine[...] = sum_over(m_land, m_slots[n - 1])
    second_sum[...] = lax.fori_loop(
        1, n, lambda q, total: total + second_land[q], second_land[0]
    )
    here = pl.ds(pl.multiple_of(mp * h, h), h)
    little_home = pltpu.make_async_copy(l_sum, little_sum.at[here], end_sem.at[1])
    little_across = remote(l_sum, little_sum.at[here], end_sem.at[2], end_sem.at[3], across)
    mix_across = remote(m_mine, m_other, end_sem.at[4], end_sem.at[5], across)
    little_home.start()
    little_across.start()
    mix_across.start()

    for way in range(2):
        for i in range(count):
            staged(way, ring - 1, i)
            ring_copy(way, ring - 2, i).wait_recv()
            if way == 1:
                final_copy(0, i).wait()
            add(way, ring - 1, i, last=True)
            final_copy(way, i).start()

    mix_across.wait()
    mix_sum[...] = m_mine[...] + m_other[...]
    little_home.wait()
    little_across.wait()
    for i in range(count):
        final_copy(1, i).wait()

    @pl.loop(0, n - 1)
    def _(q):
        stream_copy(q).wait_send()
        little_copy(q).wait_send()
        second_copy(q).wait_send()
        mix_copy(q).wait_send()

    @pl.loop(0, n)
    def _(q):
        sum_copy(q).wait_send()
        across_copy(q).wait()

    @pl.loop(0, ring - 1)
    def _(step):
        for i, way in pieces:
            ring_copy(way, step, i).wait_send()

    @pl.loop(0, ring)
    def _(step):
        for i, way in pieces:
            core_copy(way, step, i).wait_send()


def backward_exchange(
    n, grads, inner, scale, inputs, direct, output, smalls, little, second, history, mixes, parts
):
    count, ring = len(parts), n // 2
    feat, tokens = history.shape[1], grads.shape[2]
    h = feat // 2
    hbm = pl.BlockSpec(memory_space=pl.ANY)
    vmem = pl.BlockSpec(memory_space=pltpu.VMEM)

    def cut(s, rows):
        return s.shape[:-2] + (rows, s.shape[-1])

    half = parts[0].shape[-2] // n // 2
    found = pl.pallas_call(
        functools.partial(backward_kernel, n, count),
        out_shape=[
            jax.ShapeDtypeStruct((n, STREAMS, h, tokens), bf16),
            jax.ShapeDtypeStruct((n, STREAMS + 1, feat, tokens), bf16),
            jax.ShapeDtypeStruct((STREAMS * HIST, tokens), f32),
            jax.ShapeDtypeStruct((feat, WIDE), f32),
            jax.ShapeDtypeStruct(second.shape, f32),
        ]
        + [jax.ShapeDtypeStruct(cut(s, 2 * half), f32) for s in parts]
        + [jax.ShapeDtypeStruct((2, ring) + cut(s, half), bf16) for s in parts],
        in_specs=[hbm, vmem, vmem, hbm, hbm, hbm, hbm, hbm, vmem, hbm, hbm] + [hbm] * count,
        out_specs=[hbm, hbm, vmem, hbm, vmem] + [hbm] * (2 * count),
        scratch_shapes=[pltpu.VMEM((2, ring) + cut(s, half), bf16) for s in parts]
        + [pltpu.VMEM((2, 2) + cut(s, half), bf16) for s in parts]
        + [pltpu.VMEM((2, 2) + cut(s, half), bf16) for s in parts]
        + [pltpu.VMEM(cut(s, half), f32) for s in parts]
        + [
            pltpu.VMEM(inner.shape, f32),
            pltpu.VMEM((2, STREAMS, h, tokens), bf16),
            pltpu.VMEM((2, STREAMS, h, tokens), bf16),
            pltpu.VMEM((2, STREAMS, h, tokens), bf16),
            pltpu.VMEM((2, h, tokens), f32),
            pltpu.VMEM((2, h, WIDE), bf16),
            pltpu.VMEM((2, h, WIDE), f32),
            pltpu.VMEM((n, STREAMS + 1, h, tokens), bf16),
            pltpu.VMEM((n, h, WIDE), f32),
            pltpu.VMEM((n, h, WIDE), f32),
            pltpu.VMEM((n,) + second.shape, f32),
            pltpu.VMEM((STREAMS, h, tokens), bf16),
            pltpu.VMEM((2, HIST, h, tokens), bf16),
            pltpu.VMEM((n, STREAMS * HIST, tokens), f32),
            pltpu.VMEM((n, STREAMS * HIST, tokens), f32),
            pltpu.VMEM((STREAMS * HIST, tokens), f32),
            pltpu.VMEM((STREAMS * HIST, tokens), f32),
            pltpu.VMEM((h, WIDE), f32),
            DMA((2, 6)),
            DMA((n,)),
            DMA((2, 2)),
            DMA((2, 2, count)),
            DMA((2, 2, count)),
            DMA((count,)),
            DMA((n,)),
            DMA((n,)),
            DMA((2,)),
        ]
        + [DMA((n,)) for _ in range(10)]
        + [DMA((6,))]
        + [DMA((2, ring - 1, count)) for _ in range(2)]
        + [DMA((2, ring, count)) for _ in range(2)],
        compiler_params=pltpu.CompilerParams(
            collective_id=1, has_side_effects=True, vmem_limit_bytes=60 * 1024 * 1024
        ),
    )(grads, inner, scale, inputs, direct, output, smalls, little, second, history, mixes, *parts)
    return found[1], found[2], found[3], found[4], found[5 : 5 + count]


def history_kernel(grads, mixes, grad_history, block_out):
    feat = grads.shape[2]

    @pl.loop(0, feat // 16)
    def _(r):
        rows = pl.ds(pl.multiple_of(r * 16, 16), 16)
        each = [grads[0, s, rows, :].astype(f32) for s in range(STREAMS)]
        for j in range(HIST):
            total = mixes[0, pl.ds(j, 1), :] * each[0]
            for s in range(1, STREAMS):
                total = total + mixes[0, pl.ds(s * HIST + j, 1), :] * each[s]
            grad_history[j, rows, :] = total.astype(bf16)

    block_out[...] = grads[0, STREAMS]


def history_gradient(feature_side, mixes):
    n, streams, feat, tokens = feature_side.shape
    return pl.pallas_call(
        history_kernel,
        grid=(n,),
        out_shape=[
            jax.ShapeDtypeStruct((HIST, feat, n * tokens), bf16),
            jax.ShapeDtypeStruct((feat, n * tokens), bf16),
        ],
        in_specs=[
            pl.BlockSpec((1, streams, feat, tokens), lambda i: (i, 0, 0, 0)),
            pl.BlockSpec((1,) + mixes.shape[1:], lambda i: (i, 0, 0)),
        ],
        out_specs=[
            pl.BlockSpec((HIST, feat, tokens), lambda i: (0, 0, i)),
            pl.BlockSpec((feat, tokens), lambda i: (0, i)),
        ],
        compiler_params=pltpu.CompilerParams(vmem_limit_bytes=32 * 1024 * 1024),
    )(feature_side, mixes)


def rotary(heads_in, angles):
    halfway = ROT // 2
    cosine = jnp.cos(angles)[:, None, :]
    sine_part = jnp.sin(angles)[:, None, :]
    first_half = heads_in[..., :halfway]
    second_half = heads_in[..., halfway:ROT]
    return jnp.concatenate(
        [
            first_half * cosine - second_half * sine_part,
            second_half * cosine + first_half * sine_part,
            heads_in[..., ROT:],
        ],
        axis=-1,
    )


def angle_table(length):
    halfway = ROT // 2
    frequency = jnp.exp(jnp.arange(halfway, dtype=f32) * (-2.0 * math.log(10000.0) / ROT))
    places = (jnp.arange(length) % TOK_DEV).astype(f32)
    return places[:, None] * frequency[None, :]


def gelu_exact(inputs):
    return jax.nn.gelu(inputs, approximate=False)


def product(spec, left, right):
    return jnp.einsum(spec, left, right, preferred_element_type=f32)


def body(
    history,
    mix_in,
    doc_ids,
    group_ids,
    group_scale,
    w_qkv,
    w_out,
    w_up,
    w_down,
    w_mix1,
    w_mix2,
    gains,
    cot_out,
    cot_mix,
):
    n = lax.axis_size("dp")
    tokens_here = mix_in.shape[0]
    width = n * history.shape[1]
    small = jnp.pad(
        jnp.concatenate([w_mix1, gains.T], axis=1), ((0, 0), (0, WIDE - MIXH - gains.shape[0]))
    )
    inputs, mixes, smalls, (full_qkv, full_o, full_up, full_down) = forward_exchange(
        n, history, cot_out, mix_in.T, small, (w_qkv, w_out, w_up, w_down)
    )
    full_m1 = smalls[:, :MIXH]
    gain_f = smalls[:, MIXH : MIXH + STREAMS + 1].astype(f32)
    heads_here = full_qkv.shape[2] // HEAD
    width_here = heads_here * HEAD
    streams = inputs[:STREAMS].astype(f32)
    level = lax.rsqrt(jnp.mean(streams * streams, axis=1) + EPS)
    normed = [
        (streams[s] * level[s][None, :] * gain_f[:, s : s + 1]).astype(bf16) for s in range(STREAMS)
    ]
    angles = angle_table(tokens_here)

    def project(s):
        return product("dt,dn->tn", normed[s], full_qkv[s]).reshape(tokens_here, heads_here, HEAD)

    queries = rotary(project(0), angles).astype(bf16).transpose(1, 0, 2)
    key_heads = rotary(project(1), angles).astype(bf16).transpose(1, 0, 2)
    values = project(2).astype(bf16).transpose(1, 0, 2)
    scale_qk = HEAD ** (-0.5)
    positions = jnp.arange(tokens_here)
    doc_row = doc_ids[0]
    allowed = (positions[:, None] >= positions[None, :]) & (doc_row[:, None] == doc_row[None, :])
    scores = product("hqd,hkd->hqk", queries, key_heads) * scale_qk
    scores = jnp.where(allowed[None], scores, -1000000000.0)
    row_max = jnp.max(scores, axis=-1, keepdims=True)
    log_total = row_max + jnp.log(jnp.sum(jnp.exp(scores - row_max), axis=-1, keepdims=True))
    attn_probs = jnp.exp(scores - log_total)
    probs_low = attn_probs.astype(bf16)
    attended = product("hqk,hkd->hqd", probs_low, values)
    attn_cat = attended.astype(bf16).transpose(1, 0, 2).reshape(tokens_here, width_here)
    up_pre = product("dt,dn->tn", normed[3], full_up)
    hidden = gelu_exact(up_pre).astype(bf16)
    branch_part = product("oi,ti->ot", full_o, attn_cat) + product("oi,ti->ot", full_down, hidden)
    branch_low = branch_part.astype(bf16)
    swap = [(0, 1), (1, 0)]
    branch = branch_low.astype(f32) + lax.ppermute(branch_low, "mp", swap).astype(f32)
    out_full = streams[3] + branch
    out_low = out_full.astype(bf16)
    mix_level = lax.rsqrt(jnp.mean(out_full * out_full, axis=0) + EPS)
    mix_unit = out_full * mix_level[None, :]
    mix_gain = gain_f[:, STREAMS : STREAMS + 1]
    mix_normed = (mix_unit * mix_gain).astype(bf16)
    mix_pre = product("dt,dm->tm", mix_normed, full_m1)
    mix_hidden = gelu_exact(mix_pre).astype(bf16)
    mix_out = product("tm,mo->to", mix_hidden, w_mix2)

    row_scale = jnp.sum(
        jnp.where(group_ids[0][:, None] == jnp.arange(GROUPS)[None, :], group_scale[None, :], 0.0),
        axis=1,
    )
    seed = inputs[STREAMS].astype(f32) * row_scale[None, :]
    grad_mix2_part = product("tm,to->mo", mix_hidden, cot_mix)
    grad_mix_hidden = product("to,mo->tm", cot_mix, w_mix2)
    grad_mix_pre = jax.vjp(gelu_exact, mix_pre)[1](grad_mix_hidden)[0].astype(bf16)
    grad_m1_part = product("dt,tm->dm", mix_normed, grad_mix_pre)
    grad_mix_normed = product("dm,tm->dt", full_m1, grad_mix_pre)
    grad_gain_mix = jnp.sum(mix_unit * grad_mix_normed, axis=1)
    mix_inner = jnp.mean(mix_unit * mix_gain * grad_mix_normed, axis=0)
    grad_out_full = seed + mix_level[None, :] * (
        mix_gain * grad_mix_normed - mix_unit * mix_inner[None, :]
    )
    grad_branch = grad_out_full.astype(bf16)
    grad_o_part = product("ot,ti->oi", grad_branch, attn_cat).astype(bf16)
    grad_down_part = product("ot,ti->oi", grad_branch, hidden).astype(bf16)
    grad_attended = product("ot,oi->ti", grad_branch, full_o).astype(bf16)
    grad_attended = grad_attended.reshape(tokens_here, heads_here, HEAD).transpose(1, 0, 2)
    grad_hidden = product("ot,oi->ti", grad_branch, full_down)
    grad_up_pre = jax.vjp(gelu_exact, up_pre)[1](grad_hidden)[0].astype(bf16)
    grad_up_part = product("dt,tn->dn", normed[3], grad_up_pre).astype(bf16)
    grad_normed_ff = product("dn,tn->dt", full_up, grad_up_pre)
    grad_probs = product("hqd,hkd->hqk", grad_attended, values)
    grad_values = product("hqk,hqd->hkd", probs_low, grad_attended)
    inner = jnp.sum(attn_probs * grad_probs, axis=-1, keepdims=True)
    grad_scores = (attn_probs * (grad_probs - inner)).astype(bf16)
    grad_q_rot = product("hqk,hkd->hqd", grad_scores, key_heads) * scale_qk
    grad_k_rot = product("hqk,hqd->hkd", grad_scores, queries) * scale_qk

    def flat(heads):
        return heads.reshape(tokens_here, width_here).astype(bf16)

    grad_projs = (
        flat(rotary(grad_q_rot.transpose(1, 0, 2), -angles)),
        flat(rotary(grad_k_rot.transpose(1, 0, 2), -angles)),
        flat(grad_values.transpose(1, 0, 2)),
    )
    grad_qkv_part = jnp.stack(
        [product("dt,tn->dn", normed[s], grad_projs[s]).astype(bf16) for s in range(3)]
    )
    grad_normed = jnp.stack(
        [product("dn,tn->dt", full_qkv[s], grad_projs[s]).astype(bf16) for s in range(3)]
        + [grad_normed_ff.astype(bf16)]
    )
    norm_inner = jnp.sum(jnp.stack(normed).astype(f32) * grad_normed.astype(f32), axis=1)

    def eight(rows):
        return jnp.pad(rows, ((0, 8 - rows.shape[0]), (0, 0)))

    little = jnp.concatenate(
        [
            grad_m1_part,
            jnp.zeros((width, STREAMS), f32),
            grad_gain_mix[:, None],
            jnp.zeros((width, WIDE - MIXH - STREAMS - 1), f32),
        ],
        axis=1,
    )
    second = jnp.pad(grad_mix2_part, ((0, 0), (0, WIDE - MIXH)))
    feature_side, mix_sum, little_sum, second_sum, sums = backward_exchange(
        n,
        grad_normed,
        eight(norm_inner),
        eight(level),
        inputs,
        grad_out_full,
        out_low,
        smalls,
        little,
        second,
        history,
        mixes,
        (grad_qkv_part, grad_o_part, grad_up_part, grad_down_part),
    )
    grad_history, block_out = history_gradient(feature_side, mixes)
    grad_qkv, grad_w_out, grad_w_up, grad_w_down = sums
    return (
        block_out,
        mix_out,
        grad_history,
        mix_sum.T,
        grad_qkv,
        grad_w_out,
        grad_w_up,
        grad_w_down,
        little_sum[:, :MIXH],
        second_sum[:, :MIXH],
        little_sum[:, MIXH : MIXH + STREAMS + 1].T,
    )


def solution(mesh):
    return jax.shard_map(
        body,
        mesh=mesh,
        in_specs=(
            P(None, "dp", None),
            P("dp", None),
            P("dp", None),
            P("dp", None),
            P(),
            P(None, "dp", "mp"),
            P("dp", "mp"),
            P("dp", "mp"),
            P("dp", "mp"),
            P("dp", None),
            P(),
            P(None, "dp"),
            P("dp", None),
            P("dp", None),
        ),
        out_specs=(
            P("dp", None),
            P("dp", None),
            P(None, "dp", None),
            P("dp", None),
            P(None, "dp", "mp"),
            P("dp", "mp"),
            P("dp", "mp"),
            P("dp", "mp"),
            P("dp", None),
            P(),
            P(None, "dp"),
        ),
        check_vma=False,
    )
```

time: 3000 us -> 1070 us (0.36)
  blocking collectives: 1500 us -> 0 us
  Pallas kernels: 0 us -> 749 us
  waiting for transfers between devices: 760 us -> 34 us
  local copies, waits for them, and re-layouts: 294 us -> 71.4 us
  other arithmetic: 174 us -> 44.8 us
  matrix products: 213 us -> 157 us
    all_gather x2 -> x0, blocking collectives: 768 us -> none  [the longest x1 752 us: body(): lax.all_gather(gains, 'dp', axis=1, tiled=True)]
    pallas_call x0 -> x3, Pallas kernels: none -> 749 us  [the longest x1 372 us: backward_exchange(): pl.pallas_call(functools.partial(backward_kernel, n, count), out_shape=[j...]
    psum x1 -> x0, blocking collectives: 730 us -> none  [body(): grad_w_mix2 = lax.psum(grad_mix2_part, 'dp')]
    reduce_scatter x6 -> x0, waiting for transfers between devices: 551 us -> none  [the longest x1 337 us: body(): lax.psum_scatter(grad_down_part, 'dp', scatter_dimension=0, tiled=True)]
    psum x2 -> x0, waiting for transfers between devices: 206 us -> none  [the longest x1 153 us: body(): lax.psum(grad_normed_ff.astype(jnp.bfloat16), 'mp').astype(jnp.float32)]
    unnamed x6 -> x5, other arithmetic: 69 us -> 0.04 us
    unnamed x188 -> x156, local copies, waits for them, and re-layouts: 99.6 us -> 31.1 us
    all_to_all x3 -> x0, local copies, waits for them, and re-layouts: 64.5 us -> none  [the longest x1 31.1 us: body(): lax.all_to_all(grad_hist_low, 'dp', split_axis=1, concat_axis=2, tiled=True)]
  transfers between devices with their start and end apart: 16 -> 1, of which waited for: 4 -> 1; matrix products, arithmetic and copies ran while one was open for 20% -> 0% of each run, Pallas kernels for 0% -> 0%
where the time goes in v2:
time: 1070 us; the launch traced here: 1060 us
  Pallas kernels  749 us (70%)
  matrix products  157 us (15%)
  local copies, waits for them, and re-layouts  71.4 us (7%)
  other arithmetic  44.8 us (4%)
  waiting for transfers between devices  34 us (3%)
    pallas_call x1, Pallas kernels, backward_exchange(): pl.pallas_call(functools.partial(backward_kernel, n, count), out_shape=[j...  372 us
    pallas_call x1, Pallas kernels, forward_exchange(): pl.pallas_call(functools.partial(forward_kernel, n, count), out_shape=[ja...  365 us
    dot_general x30, matrix products, product(): return jnp.einsum(spec, left, right, preferred_element_type=f32)  157 us
    ppermute x1, waiting for transfers between devices, body(): lax.ppermute(branch_low, 'mp', swap).astype(f32)  34 us
    unnamed x156, local copies, waits for them, and re-layouts  31.1 us
    dot_general x4, local copies, waits for them, and re-layouts, product(): return jnp.einsum(spec, left, right, preferred_element_type=f32)  28.8 us
  transfers between devices with their start and end apart: 1, of which 1 were waited for; matrix products, arithmetic and copies ran while one was open for 0% of the time, Pallas kernels for 0%

profile of v2, /device:TPU:21, one launch (start us, length us, event | category | flops | bytes accessed | tf_op | source)
XLA Modules:
  0.0 1057.3 jit_solution(17256529295062867235)
XLA Ops:
  1.6 1.4 copy-done.7
  8.3 364.6 %shard_map.221 = (bf16[5,2048,384]{2,1,0:T(8,128)(2,1)S(1)}, f32[16,36,384]{2,1,0:T(8,128)S(1)}, bf16[2048,128]{1,0:T(8,128)(2,1)S(1)}, bf16[3,2048,1024]{2,1,0:...) custom-call(bf16[9,128,6144]{2,1,0:T(8,128)(2,1)} %refs_9_.1, ...), custom_call_target="tpu_custom_call" | custom-call | tf_op jit(solution)/shard_map/pallas_call | solution.py:295
  373.8 2.0 copy-done.13
  377.0 1.8 copy-done.2
  378.9 5.6 slice_convert_fusion
  384.9 2.5 slice_reduce_fusion
  387.4 8.9 slice_bitcast_fusion.1
  396.3 6.5 copy.109
  402.9 7.0 multiply_convert_fusion.2
  409.9 2.3 fusion.48
  413.4 6.9 copy.108
  420.2 5.0 fusion.51
  427.3 6.5 copy.111
  434.6 1.3 subtract_convert_fusion.2
  436.0 2.1 fusion.15
  439.2 28.7 %multiply_convert_fusion = (bf16[384,4096]{1,0:T(8,128)(2,1)}, f32[384,4096]{1,0:T(8,128)}, f32[384,4096]{1,0:T(8,128)}) fusion(bf16[2048,4096]{1,0:T(8,128)(2,1)} %get-tuple-element.33, f32[4,2048,384]{2,1,0:T(8,128)} %slice_convert_fusion, f32[2048]{0:T(1024)S(1)} %get-tuple-element.92, f32[384]{0:T(512)S(1)} %get-tuple-element.96), kind=kOutput, calls=%fused_computation.9 | convolution fusion | flops 6547046400 | bytes 35661312 | tf_op jit(solution)/shard_map/dt,dn->tn/dot_general | solution.py:894
  467.9 1.9 fusion.57
  469.8 1.5 convolution_convert_fusion.6
  472.3 2.4 fusion.87
  474.7 13.8 %add_convert_fusion.1 = bf16[2048,384]{1,0:T(8,128)(2,1)} fusion(f32[2048,384]{1,0:T(8,128)S(1)} %fusion.87, bf16[2048,4096]{1,0:T(8,128)(2,1)} %get-tuple-element.32, bf16[384,4096]{1,0:T(8,128)(2,1)S(1)} %copy-done.65), kind=kOutput, calls=%fused_computation.65 | convolution fusion | flops 6444023808 | bytes 24641536 | tf_op jit(solution)/shard_map/oi,ti->ot/dot_general | solution.py:894
  490.7 34.0 %collective-permute-done = bf16[2048,384]{1,0:T(8,128)(2,1)} collective-permute-done((bf16[2048,384]{1,0:T(8,128)(2,1)}, bf16[2048,384]{1,0:T(8,128)(2,1)}, u32[]{:S(2)}, u32[]{:S(2)}) %collective-permute-start) | collective-permute-done | bytes 1572896 | tf_op jit(solution)/shard_map/ppermute | solution.py:956
  524.8 4.5 fusion.83
  534.2 3.5 fusion.84
  537.7 2.7 convolution_convert_fusion.4
  540.5 16.0 %add_convert_fusion = bf16[384,4096]{1,0:T(8,128)(2,1)S(1)} fusion(f32[384,4096]{1,0:T(8,128)S(1)} %bitcast.188, f32[384,4096]{1,0:T(8,128)} %get-tuple-element.133, bf16[2048,384]{1,0:T(8,128)(2,1)S(1)} %get-tuple-element.104, bf16[2048,4096]{1,0:T(8,128)(2,1)} %get-tuple-element.32), kind=kOutput, calls=%fused_computation.8 | convolution fusion | flops 6464471040 | bytes 34078720 | tf_op jit(solution)/shard_map/ot,oi->ti/dot_general | solution.py:894
  556.4 13.3 %fusion.34 = bf16[1,2048,384]{2,1,0:T(8,128)(2,1)} fusion(bf16[2048,4096]{1,0:T(8,128)(2,1)} %get-tuple-element.33, bf16[384,4096]{1,0:T(8,128)(2,1)S(1)} %add_convert_fusion), kind=kOutput, calls=%fused_computation.71 | convolution fusion | flops 6443237376 | bytes 21495808 | tf_op jit(solution)/shard_map/dn,tn->dt/dot_general | solution.py:894
  569.8 14.8 %convolution_convert_fusion.1.refs_13_ = bf16[2048,4096]{1,0:T(8,128)(2,1)} fusion(bf16[384,4096]{1,0:T(8,128)(2,1)S(1)} %add_convert_fusion, f32[4,2048,384]{2,1,0:T(8,128)} %slice_convert_fusion, f32[2048]{0:T(1024)S(1)} %get-tuple-element.92, f32[384]{0:T(512)S(1)} %get-tuple-element.96), kind=kOutput, calls=%fused_computation.1 | convolution fusion | flops 6453198848 | bytes 23078400 | tf_op jit(solution)/shard_map/dt,tn->dn/dot_general | solution.py:894
  584.6 2.3 copy.112
  587.0 5.0 convolution_convert_fusion.5
  592.0 1.4 multiply_reduce_fusion.2
  598.9 3.5 fusion.41
  602.4 4.4 convert_bitcast_fusion.2
  606.8 3.7 fusion.38
  610.5 4.3 convert_bitcast_fusion.1
  614.8 3.5 fusion.35
  618.4 4.4 convert_bitcast_fusion
  622.8 4.4 convolution_convert_fusion.2.refs_12_
  627.2 11.7 %convolution_convert_fusion.refs_14_ = bf16[2048,4096]{1,0:T(8,128)(2,1)} fusion(bf16[2048,384]{1,0:T(8,128)(2,1)S(1)} %copy-done.40, bf16[384,4096]{1,0:T(8,128)(2,1)S(1)} %copy-done.66), kind=kOutput, calls=%fused_computation | convolution fusion | flops 6450839552 | bytes 21495808 | tf_op jit(solution)/shard_map/ot,ti->oi/dot_general | solution.py:894
  639.5 1.4 copy.95
  640.9 7.6 pad_maximum_fusion.1.refs_0_
  649.2 1.7 multiply_reduce_fusion
  653.9 5.6 pad_maximum_fusion.refs_11_
  660.8 372.1 %shard_map.222 = (bf16[16,4,64,384]{3,2,1,0:T(8,128)(2,1)}, bf16[16,5,128,384]{3,2,1,0:T(8,128)(2,1)}, f32[36,384]{1,0:T(8,128)}, f32[128,128]{1,0:T(8,128)}, f3...) custom-call(bf16[4,2048,384]{2,1,0:T(8,128)(2,1)} %pad_maximum_fusio, ...), custom_call_target="tpu_custom_call" | custom-call | tf_op jit(solution)/shard_map/pallas_call | solution.py:772
  1033.8 1.5 copy.96
  1036.0 3.2 copy-done.3
  1039.2 12.1 %shard_map.223 = (bf16[9,128,6144]{2,1,0:T(8,128)(2,1)}, bf16[128,6144]{1,0:T(8,128)(2,1)}) custom-call(bf16[16,5,128,384]{3,2,1,0:T(8,128)(2,1)S(1)} %copy-done.3, f32[16,36,384]{2,1,0:T(8,128)S(1)} %copy-done.6), custom_call_target="tpu_custom_call" | custom-call | tf_op jit(solution)/shard_map/pallas_call | solution.py:847
  1053.9 1.3 copy.122
  1055.2 1.3 copy.123
  (197 shorter events, 37.6 us)
Async XLA Ops:
  0.6 529.9 %copy-start = (bf16[384,40]{0,1:T(8,128)(2,1)S(1)}, bf16[384,40]{0,1:T(8,128)(2,1)}, u32[]{:S(2)}) copy-start(bf16[384,40]{0,1:T(8,128)(2,1)} %param.27) | copy-start | bytes 92164
  375.8 3.1 copy-start.2
  375.8 157.0 %copy-start.4 = (bf16[2048,128]{1,0:T(8,128)(2,1)}, bf16[2048,128]{1,0:T(8,128)(2,1)S(1)}, u32[]{:S(2)}) copy-start(bf16[2048,128]{1,0:T(8,128)(2,1)S(1)} %get-tuple-element.30.refs_6_) | copy-start | bytes 1572868
  378.9 5.6 copy-start.57
  402.9 7.0 copy-start.28
  413.4 22.6 %copy-start.34 = (bf16[384,8,96]{0,2,1:T(8,128)(2,1)}, bf16[384,8,96]{0,2,1:T(8,128)(2,1)S(1)}, u32[]{:S(2)}) copy-start(bf16[384,8,96]{0,2,1:T(8,128)(2,1)S(1)} %slice.262) | copy-start | bytes 1769476
  438.2 31.6 %copy-start.16 = (f32[8,384,384]{1,2,0:T(8,128)}, f32[8,384,384]{1,2,0:T(8,128)S(1)}, u32[]{:S(2)}) copy-start(f32[8,384,384]{1,2,0:T(8,128)S(1)} %get-tuple-element.132) | copy-start | bytes 14155780
  439.2 28.7 %copy-start.27 = (bf16[1024,2048]{1,0:T(8,128)(2,1)S(1)}, bf16[1024,2048]{1,0:T(8,128)(2,1)}, u32[]{:S(2)}) copy-start(bf16[1024,2048]{1,0:T(8,128)(2,1)} %copy.111) | copy-start | bytes 12582916
  469.8 4.9 copy-start.41
  471.3 3.4 copy-start.62
  474.7 15.9 %copy-start.58 = (s32[1,384]{1,0:T(1,128)S(1)}, s32[1,384]{1,0:T(1,128)}, u32[]{:S(2)}) copy-start(s32[1,384]{1,0:T(1,128)} %param.17) | copy-start | bytes 4612
  474.7 15.9 %copy-start.61 = (f32[8]{0:T(128)S(1)}, f32[8]{0:T(128)}, u32[]{:S(2)}) copy-start(f32[8]{0:T(128)} %param.18) | copy-start | bytes 100
  488.5 36.2 %collective-permute-start = (bf16[2048,384]{1,0:T(8,128)(2,1)}, bf16[2048,384]{1,0:T(8,128)(2,1)}, u32[]{:S(2)}, u32[]{:S(2)}) collective-permute-start(bf16[2048,384]{1,0:T(8,128)(2,1)} %add_convert_fusion.1), channel_id=1, source_target_pairs={{0,1},{1,0},{2,3},{3,2},{4,5},{5,4},{6,7},{7,6},{8,9},{9,8},{10,11... | collective-permute-start | bytes 4718600 | tf_op jit(solution)/shard_map/ppermute | solution.py:956
  532.8 7.6 slice-start.5
  534.2 3.6 copy-start.15
  534.2 6.3 slice-start.6
  584.6 7.4 slice-start
  587.0 5.0 copy-start.33
  587.0 5.0 copy-start.42
  587.0 5.0 slice-start.1
  593.5 4.2 slice-start.2
  593.5 4.2 slice-start.3
  598.9 3.5 copy-start.21
  606.8 3.7 copy-start.19
  610.5 4.3 copy-start.64
  618.4 4.4 copy-start.40
  618.4 4.4 copy-start.63
  622.8 4.4 copy-start.66
  627.2 11.7 %copy-start.53 = (f32[40,40]{1,0:T(8,128)S(1)}, f32[40,40]{1,0:T(8,128)}, u32[]{:S(2)}) copy-start(f32[40,40]{1,0:T(8,128)} %fusion.89) | copy-start | bytes 19204
  640.9 7.6 copy-start.17
  640.9 7.6 copy-start.20
  640.9 7.6 copy-start.22
  640.9 7.6 copy-start.23
  640.9 7.6 copy-start.24
  640.9 7.6 copy-start.25
  640.9 8.3 copy-start.26
  649.2 3.5 copy-start.31
  649.2 4.7 copy-start.32
  653.9 5.6 copy-start.29
  653.9 5.6 copy-start.59
  653.9 5.6 copy-start.60
  660.8 375.2 %copy-start.6 = (f32[16,36,384]{2,1,0:T(8,128)S(1)}, f32[16,36,384]{2,1,0:T(8,128)}, u32[]{:S(2)}) copy-start(f32[16,36,384]{2,1,0:T(8,128)} %copy-done.5) | copy-start | bytes 2654212
  1036.0 3.2 copy-start.3
  1039.2 12.1 %copy-start.54 = (f32[36,384]{1,0:T(8,128)S(1)}, f32[36,384]{1,0:T(8,128)}, u32[]{:S(2)}) copy-start(f32[36,384]{1,0:T(8,128)} %get-tuple-element.38) | copy-start | bytes 165892
  1039.2 12.7 %copy-start.38 = (f32[3,128,1024]{2,1,0:T(8,128)S(1)}, f32[3,128,1024]{2,1,0:T(8,128)}, u32[]{:S(2)}) copy-start(f32[3,128,1024]{2,1,0:T(8,128)} %get-tuple-element.155) | copy-start | bytes 4718596
  1039.2 13.9 %copy-start.46 = (f32[128,1024]{1,0:T(8,128)S(1)}, f32[128,1024]{1,0:T(8,128)}, u32[]{:S(2)}) copy-start(f32[128,1024]{1,0:T(8,128)} %get-tuple-element.156) | copy-start | bytes 1572868
  1051.9 3.3 copy-start.36
  1053.1 4.1 copy-start.1
  (27 other events, 45.4 us)

commit v3 on v2

--- a/solution.py
+++ b/solution.py
@@ -17,6 +17,8 @@
 MIXH = 40
 WIDE = 128
 EPS = 1e-05
+AHEAD = 6
+CUTS = (1, 1, 2, 2)
 MESH = pl.DeviceIdType.MESH
 DMA = pltpu.SemaphoreType.DMA
 f32 = jnp.float32
@@ -61,6 +63,24 @@
     return ref.at[pl.ds(start, count), :]
 
 
+def cuts_of(shards, cuts):
+    pieces = []
+    for i, shard in enumerate(shards):
+        if len(shard.shape) == 3:
+            pieces += [(i, s, 0) for s in range(shard.shape[0])]
+        else:
+            wide = shard.shape[1] // cuts[i]
+            pieces += [(i, k * wide, wide) for k in range(cuts[i])]
+    return pieces
+
+
+def piece_of(refs, piece, start, count):
+    i, first, wide = piece
+    if wide == 0:
+        return refs[i].at[first, pl.ds(start, count), :]
+    return refs[i].at[pl.ds(start, count), pl.ds(first, wide)]
+
+
 class Ring:
     def __init__(self, n):
         self.n, self.ring = n, n // 2
@@ -75,17 +95,35 @@
 
 
 def forward_kernel(n, count, *refs):
-    hist, cot, mix, small = refs[:4]
-    shards = refs[4 : 4 + count]
-    inputs, mixes, smalls = refs[4 + count : 7 + count]
-    fulls = refs[7 + count : 7 + 2 * count]
+    hist, cot, mix, small, tables, docs_row, docs_col = refs[:7]
+    shards = refs[7 : 7 + count]
+    refs = refs[7 + count :]
+    inputs, mixes, smalls, normed_out, level, heads_out, attn_out, pre_out, hidden_out, total = refs[:10]
+    fulls = refs[10 : 10 + count]
     (
         hist_buf,
         slots,
+        streams,
+        normed,
+        tiles,
+        heads,
+        attn,
+        pre_buf,
+        hidden,
+        down_buf,
+        out_buf,
+        branch,
+        branch_land,
         hist_sem,
         cot_sem,
         own_sem,
         local_sem,
+        keep_sem,
+        tile_sem,
+        pre_sem,
+        row_sem,
+        swap_send,
+        swap_recv,
         mix_send,
         mix_recv,
         small_send,
@@ -98,49 +136,82 @@
         ring_recv,
         core_send,
         core_recv,
-    ) = refs[7 + 2 * count :]
+    ) = refs[10 + count :]
     where = Ring(n)
     me, ring, owner = where.me, where.ring, where.owner
     mp = lax.axis_index("mp")
     across = {"mp": 1 - mp}
     feat, tokens = hist.shape[1], mix.shape[1]
     h = feat // 2
+    width = n * feat
     size = shards[0].shape[-2]
     half = size // 2
+    w_qkv, w_out, w_up, w_down = fulls
     greet_plane(n, me, mp)
+
+    pieces = cuts_of(shards, CUTS)
+
+    def of(*arrays):
+        return [p for p, piece in enumerate(pieces) if piece[0] in arrays]
 
     def origin_rows(offset, way):
         return pl.multiple_of(owner(offset) * size + way * half, half)
 
-    def ring_copy(way, step, i, first=False):
-        there = rows_of(fulls[i], origin_rows(-step if way == 0 else step, way), half)
-        here = rows_of(shards[i], way * half, half) if first else there
-        return remote(
-            here, there, ring_send.at[way, step, i], ring_recv.at[way, step, i], where.next_of[way]
-        )
-
-    def ring_arrival(way, step, i):
-        there = rows_of(fulls[i], origin_rows(-step - 1 if way == 0 else step + 1, way), half)
-        return remote(
-            there, there, ring_send.at[way, step, i], ring_recv.at[way, step, i], where.next_of[way]
-        )
-
-    def core_copy(way, step, i, first=False):
-        there = rows_of(fulls[i], origin_rows(-step if way == 0 else step, way), half)
-        here = rows_of(shards[i], way * half, half) if first else there
-        return remote(
-            here, there, core_send.at[way, step, i], core_recv.at[way, step, i], {"dp": where.mate}
+    def ring_copy(way, step, p, first=False):
+        there = piece_of(fulls, pieces[p], origin_rows(-step if way == 0 else step, way), half)
+        here = piece_of(shards, pieces[p], way * half, half) if first else there
+        return remote(
+            here, there, ring_send.at[way, step, p], ring_recv.at[way, step, p], where.next_of[way]
+        )
+
+    def ring_arrival(way, step, p):
+        offset = -step - 1 if way == 0 else step + 1
+        there = piece_of(fulls, pieces[p], origin_rows(offset, way), half)
+        return remote(
+            there, there, ring_send.at[way, step, p], ring_recv.at[way, step, p], where.next_of[way]
+        )
+
+    def core_copy(way, step, p, first=False):
+        there = piece_of(fulls, pieces[p], origin_rows(-step if way == 0 else step, way), half)
+        here = piece_of(shards, pieces[p], way * half, half) if first else there
+        return remote(
+            here, there, core_send.at[way, step, p], core_recv.at[way, step, p], {"dp": where.mate}
         )
 
     def shard_copy(i):
         return pltpu.make_async_copy(shards[i], rows_of(fulls[i], me * size, size), local_sem.at[i])
 
-    def turn(q):
-        return (q + 1) % n
+    def ring_begin(some):
+        for p in some:
+            for way in range(2):
+                ring_copy(way, 0, p, True).start()
+
+    def ring_step(step, some):
+        for p in some:
+            for way in range(2):
+                ring_arrival(way, step - 1, p).wait_recv()
+                ring_copy(way, step, p).start()
+                core_copy(way, step, p).start()
+
+    def ring_end(some):
+        for p in some:
+            for way in range(2):
+                ring_arrival(way, ring - 2, p).wait_recv()
+                core_copy(way, ring - 1, p).start()
+
+    def ring_complete(*arrays):
+        for i in arrays:
+            shard_copy(i).wait()
+        for p in of(*arrays):
+
+            @pl.loop(0, ring)
+            def _(step):
+                for way in range(2):
+                    core_copy(way, step, p).wait_recv()
 
     def mix_copy(q):
         return remote(
-            mix, mixes.at[me], mix_send.at[q], mix_recv.at[q], {"dp": (me + turn(q)) % n}
+            mix, mixes.at[me], mix_send.at[q], mix_recv.at[q], {"dp": (me + q) % n}
         )
 
     def small_copy(q):
@@ -149,14 +220,14 @@
             smalls.at[pl.ds(pl.multiple_of(me * feat, feat), feat)],
             small_send.at[q],
             small_recv.at[q],
-            {"dp": (me + turn(q)) % n},
+            {"dp": (me + q) % n},
         )
 
     def lanes(peer):
         return pl.ds(pl.multiple_of(peer * tokens, 128), tokens)
 
     def hist_copy(q):
-        peer = (me + turn(q)) % n
+        peer = (me + q) % n
         return pltpu.make_async_copy(
             hist.at[:, pl.ds(pl.multiple_of(mp * h, h), h), lanes(peer)],
             hist_buf.at[q % 2],
@@ -164,7 +235,7 @@
         )
 
     def cot_copy(q):
-        peer = (me + turn(q)) % n
+        peer = (me + q) % n
         return pltpu.make_async_copy(
             cot.at[pl.ds(pl.multiple_of(mp * h, h), h), lanes(peer)],
             slots.at[q, STREAMS],
@@ -172,24 +243,24 @@
         )
 
     def features(source, plane):
-        return inputs.at[:, pl.ds(pl.multiple_of(source * feat + plane * h, h), h), :]
+        return streams.at[:, pl.ds(pl.multiple_of(source * feat + plane * h, h), h), :]
 
     def stream_copy(q):
         return remote(
-            slots.at[q], features(me, mp), a_send.at[q], a_recv.at[q], {"dp": (me + turn(q)) % n}
+            slots.at[q], features(me, mp), a_send.at[q], a_recv.at[q], {"dp": (me + q) % n}
         )
 
     def own_copy():
-        return pltpu.make_async_copy(slots.at[n - 1], features(me, mp), own_sem)
+        return pltpu.make_async_copy(slots.at[0], features(me, mp), own_sem)
 
     def across_copy(q, own=False):
-        there = features((me - turn(q) + n) % n, mp)
-        return remote(
-            slots.at[n - 1] if own else there, there, y_send.at[q], y_recv.at[q], across
+        there = features((me - q + n) % n, mp)
+        return remote(
+            slots.at[0] if own else there, there, y_send.at[q], y_recv.at[q], across
         )
 
     def mix_streams(q):
-        peer = (me + turn(q)) % n
+        peer = (me + q) % n
 
         @pl.loop(0, h // 16)
         def _(r):
@@ -203,124 +274,368 @@
             for s in range(STREAMS):
                 slots[q, s, rows, :] = sums[s].astype(bf16)
 
-    pieces = [(i, way) for i in range(count) for way in range(2)]
-
-    @pl.loop(0, n - 1)
+    def normalise():
+        level[...] = jnp.zeros_like(level)
+        for s in range(STREAMS):
+
+            def add(r, total):
+                part = streams[s, pl.ds(pl.multiple_of(r * 32, 32), 32), :].astype(f32)
+                part = part * part
+                return total + (part[0:8] + part[8:16]) + (part[16:24] + part[24:32])
+
+            squares = lax.fori_loop(0, width // 32, add, jnp.zeros((8, tokens), f32))
+            mean = jnp.sum(squares, axis=0, keepdims=True) * (1.0 / width)
+            level[pl.ds(s, 1), :] = lax.rsqrt(mean + EPS)
+
+        @pl.loop(0, width // 32)
+        def _(r):
+            rows = pl.ds(pl.multiple_of(r * 32, 32), 32)
+            gain = smalls[rows, :].astype(f32)
+            for s in range(STREAMS):
+                unit = streams[s, rows, :].astype(f32) * level[pl.ds(s, 1), :]
+                normed[s, rows, :] = (unit * gain[:, MIXH + s : MIXH + s + 1]).astype(bf16)
+
+    def head_tiles(pair, spot):
+        columns = pl.ds(pl.multiple_of(pair * 2 * HEAD, 2 * HEAD), 2 * HEAD)
+        return [
+            pltpu.make_async_copy(
+                w_qkv.at[s, :, columns], tiles.at[spot * 3 + s], tile_sem.at[spot * 3 + s]
+            )
+            for s in range(3)
+        ]
+
+    def first_dims(left, right):
+        return lax.dot_general(left, right, (((0,), (0,)), ((), ())), preferred_element_type=f32)
+
+    def last_dims(left, right):
+        return lax.dot_general(left, right, (((1,), (1,)), ((), ())), preferred_element_type=f32)
+
+    def attend(pair):
+        spot = pair % 2
+        for copy in head_tiles(pair, spot):
+            copy.wait()
+
+        @pl.when(pair < heads.shape[1] // 2 - 1)
+        def _():
+            for copy in head_tiles(pair + 1, 1 - spot):
+                copy.start()
+
+        for s in range(3):
+            both = first_dims(normed[s], tiles[spot * 3 + s])
+            for u in range(2):
+                one = both[:, u * HEAD : (u + 1) * HEAD]
+                if s < 2:
+                    one = (
+                        one * tables[0]
+                        + pltpu.roll(one, HEAD - ROT // 2, 1) * tables[1]
+                        + pltpu.roll(one, ROT // 2, 1) * tables[2]
+                    )
+                heads[s, pair * 2 + u] = one.astype(bf16)
+        place = lax.broadcasted_iota(jnp.int32, (tokens, tokens), 0)
+        other = lax.broadcasted_iota(jnp.int32, (tokens, tokens), 1)
+        allowed = (place >= other) & (docs_col[...] == docs_row[...])
+        for u in range(2):
+            scores = last_dims(heads[0, pair * 2 + u], heads[1, pair * 2 + u]) * HEAD ** (-0.5)
+            scores = jnp.where(allowed, scores, -1000000000.0)
+            weight = jnp.exp(scores - jnp.max(scores, axis=1, keepdims=True))
+            probs = weight * (1.0 / jnp.sum(weight, axis=1, keepdims=True))
+            value = jnp.dot(
+                probs.astype(bf16), heads[2, pair * 2 + u], preferred_element_type=f32
+            )
+            attn[:, pl.ds(pl.multiple_of((pair * 2 + u) * HEAD, HEAD), HEAD)] = value.astype(bf16)
+
+    chunk = 512
+    ups = hidden.shape[1] // chunk
+
+    def up_tile(c, spot):
+        return [
+            pltpu.make_async_copy(
+                w_up.at[:, pl.ds(pl.multiple_of(c * chunk + k * 256, 256), 256)],
+                tiles.at[spot * 2 + k],
+                tile_sem.at[spot * 2 + k],
+            )
+            for k in range(2)
+        ]
+
+    def pre_copy(c):
+        return pltpu.make_async_copy(
+            pre_buf.at[c % 2],
+            pre_out.at[:, pl.ds(pl.multiple_of(c * chunk, chunk), chunk)],
+            pre_sem.at[c % 2],
+        )
+
+    def feed(c, spot):
+        for copy in up_tile(c, spot):
+            copy.wait()
+
+        @pl.when(c < ups - 1)
+        def _():
+            for copy in up_tile(c + 1, 1 - spot):
+                copy.start()
+
+        @pl.when(c >= 2)
+        def _():
+            pre_copy(c - 2).wait()
+
+        for k in range(2):
+            pre = first_dims(normed[STREAMS - 1], tiles[spot * 2 + k])
+            pre_buf[c % 2, :, k * 256 : (k + 1) * 256] = pre
+            low = (0.5 * pre * (1.0 + lax.erf(pre * math.sqrt(0.5)))).astype(bf16)
+            hidden[:, pl.ds(pl.multiple_of(c * chunk + k * 256, 256), 256)] = low
+        pre_copy(c).start()
+
+    deep = down_buf.shape[1]
+
+    def row_tiles(c):
+        rows = pl.ds(c * deep, deep)
+        return [
+            pltpu.make_async_copy(w_down.at[rows, :], down_buf.at[c % 2], row_sem.at[c % 2, 0]),
+            pltpu.make_async_copy(w_out.at[rows, :], out_buf.at[c % 2], row_sem.at[c % 2, 1]),
+        ]
+
+    def swap_copy(c):
+        rows = pl.ds(c * deep, deep)
+        return remote(
+            branch.at[rows], branch_land.at[rows], swap_send.at[c], swap_recv.at[c], across
+        )
+
+    def keep(k):
+        pairs = [
+            (streams, inputs),
+            (normed, normed_out),
+            (heads, heads_out),
+            (attn, attn_out),
+            (hidden, hidden_out),
+        ]
+        return pltpu.make_async_copy(pairs[k][0], pairs[k][1], keep_sem.at[k])
+
+    def stream_turn(q):
+        hist_copy(q).wait()
+
+        @pl.when(q < n - 1)
+        def _():
+            hist_copy(q + 1).start()
+
+        mix_copy(n - q).wait_recv()
+        mix_streams(q)
+        cot_copy(q).wait()
+        stream_copy(q).start()
+
+    def forward_turn(q):
+        stream_copy(q).wait_recv()
+        across_copy(q).start()
+
+    @pl.loop(1, n)
     def _(q):
         mix_copy(q).start()
         small_copy(q).start()
+
+    @pl.loop(0, n)
+    def _(q):
         cot_copy(q).start()
 
-    cot_copy(n - 1).start()
     hist_copy(0).start()
-    for i, way in pieces:
-        ring_copy(way, 0, i, True).start()
+    ring_begin(of(0, 1))
     own_small = pltpu.make_async_copy(
         small, smalls.at[pl.ds(pl.multiple_of(me * feat, feat), feat)], local_sem.at[count]
     )
     own_small.start()
     mixes[me] = mix[...]
-
-    @pl.loop(0, n - 1)
+    hist_copy(0).wait()
+    hist_copy(1).start()
+    mix_streams(0)
+    cot_copy(0).wait()
+    own_copy().start()
+    across_copy(0, True).start()
+
+    @pl.loop(1, 4)
     def _(q):
-        hist_copy(q).wait()
-        hist_copy(q + 1).start()
-        mix_copy(n - 2 - q).wait_recv()
-        mix_streams(q)
-        cot_copy(q).wait()
-        stream_copy(q).start()
-
-    hist_copy(n - 1).wait()
-    mix_streams(n - 1)
-    cot_copy(n - 1).wait()
-    own_copy().start()
-    across_copy(n - 1, True).start()
-    for i, way in pieces:
-        core_copy(way, 0, i, True).start()
+        stream_turn(q)
+
+    for p in range(len(pieces)):
+        for way in range(2):
+            core_copy(way, 0, p, True).start()
     for i in range(count):
         shard_copy(i).start()
+    ring_begin(of(2))
 
     @pl.loop(1, ring - 1)
     def _(step):
-        for i, way in pieces:
-            ring_arrival(way, step - 1, i).wait_recv()
-            ring_copy(way, step, i).start()
-            core_copy(way, step, i).start()
-        for k in range(2):
-            q = (step - 1) * 2 + k
-            stream_copy(q).wait_recv()
-            across_copy(q).start()
-
-    @pl.loop((ring - 2) * 2, n - 1)
+        ring_step(step, of(0, 1))
+        for u in range(2):
+            stream_turn(2 + 2 * step + u)
+        for u in range(2):
+            forward_turn(2 * step - 1 + u)
+
+    ring_end(of(0, 1))
+    ring_begin(of(3))
+
+    @pl.loop(n - 3, n)
     def _(q):
-        stream_copy(q).wait_recv()
-        across_copy(q).start()
-
-    for i, way in pieces:
-        ring_arrival(way, ring - 2, i).wait_recv()
-        core_copy(way, ring - 1, i).start()
+        forward_turn(q)
 
     own_copy().wait()
     own_small.wait()
-    for i in range(count):
-        shard_copy(i).wait()
-
-    @pl.loop(0, n - 1)
+
+    @pl.loop(1, n)
+    def _(q):
+        small_copy(q).wait_recv()
+
+    @pl.loop(0, n)
+    def _(q):
+        across_copy(q).wait_recv()
+
+    keep(0).start()
+    ring_complete(0, 1)
+    for copy in head_tiles(0, 0):
+        copy.start()
+    normalise()
+    keep(1).start()
+    pairs = heads.shape[1] // 2
+
+    @pl.loop(1, ring - 1)
+    def _(step):
+        ring_step(step, of(2))
+
+        @pl.when(step <= pairs)
+        def _():
+            attend(step - 1)
+
+    keep(2).start()
+    keep(3).start()
+    ring_end(of(2))
+    ring_complete(2)
+    for copy in up_tile(0, 0):
+        copy.start()
+
+    @pl.loop(1, ring - 1)
+    def _(step):
+        ring_step(step, of(3))
+
+        @pl.when(step <= ups - 2)
+        def _():
+            feed(step - 1, (step - 1) % 2)
+
+    feed(ups - 2, (ups - 2) % 2)
+    feed(ups - 1, (ups - 1) % 2)
+    keep(4).start()
+    ring_end(of(3))
+    ring_complete(3)
+    rounds = width // deep
+    for copy in row_tiles(0):
+        copy.start()
+    for c in range(rounds):
+        if c < rounds - 1:
+            for copy in row_tiles(c + 1):
+                copy.start()
+        for copy in row_tiles(c):
+            copy.wait()
+        part = last_dims(down_buf[c % 2], hidden[...]) + last_dims(out_buf[c % 2], attn[...])
+        branch[pl.ds(c * deep, deep)] = part.astype(bf16)
+        swap_copy(c).start()
+    for c in range(rounds):
+        swap_copy(c).wait_recv()
+
+        @pl.loop(0, deep // 32)
+        def _(r):
+            rows = pl.ds(pl.multiple_of(c * deep + r * 32, 32), 32)
+            both = branch[rows, :].astype(f32) + branch_land[rows, :].astype(f32)
+            total[rows, :] = streams[STREAMS - 1, rows, :].astype(f32) + both
+
+    for c in range(ups - 2, ups):
+        pre_copy(c).wait()
+    for k in range(5):
+        keep(k).wait()
+    for c in range(rounds):
+        swap_copy(c).wait_send()
+
+    @pl.loop(1, n)
     def _(q):
         mix_copy(q).wait_send()
-        small_copy(q).wait()
+        small_copy(q).wait_send()
         stream_copy(q).wait_send()
 
     @pl.loop(0, n)
     def _(q):
-        across_copy(q).wait()
+        across_copy(q).wait_send()
 
     @pl.loop(0, ring)
     def _(step):
-        for i, way in pieces:
-            core_copy(way, step, i).wait()
+        for p in range(len(pieces)):
+            for way in range(2):
+                core_copy(way, step, p).wait_send()
 
     @pl.loop(0, ring - 1)
     def _(step):
-        for i, way in pieces:
-            ring_copy(way, step, i).wait_send()
-
-
-def forward_exchange(n, history, cot_out, mix, small, shards):
+        for p in range(len(pieces)):
+            for way in range(2):
+                ring_copy(way, step, p).wait_send()
+
+
+def forward_exchange(n, history, cot_out, mix, small, tables, docs, shards):
     count, ring = len(shards), n // 2
     feat, tokens = history.shape[1], mix.shape[1]
-    h = feat // 2
+    h, width = feat // 2, n * feat
     hbm = pl.BlockSpec(memory_space=pl.ANY)
     vmem = pl.BlockSpec(memory_space=pltpu.VMEM)
+    columns, units = shards[0].shape[2], shards[2].shape[1]
+    across = columns // HEAD
+    deep = 512
+    rounds = width // deep
+    travel = len(cuts_of(shards, CUTS))
     found = pl.pallas_call(
         functools.partial(forward_kernel, n, count),
         out_shape=[
-            jax.ShapeDtypeStruct((STREAMS + 1, n * feat, tokens), bf16),
+            jax.ShapeDtypeStruct((STREAMS + 1, width, tokens), bf16),
             jax.ShapeDtypeStruct((n,) + mix.shape, f32),
-            jax.ShapeDtypeStruct((n * feat, WIDE), bf16),
+            jax.ShapeDtypeStruct((width, WIDE), bf16),
+            jax.ShapeDtypeStruct((STREAMS, width, tokens), bf16),
+            jax.ShapeDtypeStruct((8, tokens), f32),
+            jax.ShapeDtypeStruct((3, across, tokens, HEAD), bf16),
+            jax.ShapeDtypeStruct((tokens, columns), bf16),
+            jax.ShapeDtypeStruct((tokens, units), f32),
+            jax.ShapeDtypeStruct((tokens, units), bf16),
+            jax.ShapeDtypeStruct((width, tokens), f32),
         ]
         + [
             jax.ShapeDtypeStruct(s.shape[:-2] + (s.shape[-2] * n, s.shape[-1]), s.dtype)
             for s in shards
         ],
-        in_specs=[hbm, hbm, vmem, hbm] + [hbm] * count,
-        out_specs=[hbm, vmem, hbm] + [hbm] * count,
+        in_specs=[hbm, hbm, vmem, hbm, vmem, vmem, vmem] + [hbm] * count,
+        out_specs=[hbm, vmem, vmem, hbm, vmem, hbm, hbm, hbm, hbm, vmem] + [hbm] * count,
         scratch_shapes=[
             pltpu.VMEM((2, HIST, h, tokens), bf16),
             pltpu.VMEM((n, STREAMS + 1, h, tokens), bf16),
+            pltpu.VMEM((STREAMS + 1, width, tokens), bf16),
+            pltpu.VMEM((STREAMS, width, tokens), bf16),
+            pltpu.VMEM((6, width, 2 * HEAD), bf16),
+            pltpu.VMEM((3, across, tokens, HEAD), bf16),
+            pltpu.VMEM((tokens, columns), bf16),
+            pltpu.VMEM((2, tokens, 512), f32),
+            pltpu.VMEM((tokens, units), bf16),
+            pltpu.VMEM((2, deep, units), bf16),
+            pltpu.VMEM((2, deep, columns), bf16),
+            pltpu.VMEM((width, tokens), bf16),
+            pltpu.VMEM((width, tokens), bf16),
             DMA((2,)),
             DMA((n,)),
             DMA,
             DMA((count + 1,)),
+            DMA((5,)),
+            DMA((6,)),
+            DMA((2,)),
+            DMA((2, 2)),
+            DMA((rounds,)),
+            DMA((rounds,)),
         ]
         + [DMA((n,)) for _ in range(8)]
-        + [DMA((2, ring - 1, count)) for _ in range(2)]
-        + [DMA((2, ring, count)) for _ in range(2)],
+        + [DMA((2, ring - 1, travel)) for _ in range(2)]
+        + [DMA((2, ring, travel)) for _ in range(2)],
         compiler_params=pltpu.CompilerParams(
-            collective_id=0, has_side_effects=True, vmem_limit_bytes=32 * 1024 * 1024
+            collective_id=0, has_side_effects=True, vmem_limit_bytes=60 * 1024 * 1024
         ),
-    )(history, cot_out, mix, small, *shards)
-    return found[0], found[1], found[2], found[3:]
+    )(history, cot_out, mix, small, tables, docs, docs.T, *shards)
+    return found[:10], found[10:]
 
 
 def backward_kernel(n, count, *refs):
@@ -453,14 +768,11 @@
                 else:
                     slot[at] = total.astype(bf16)
 
-    def turn(q):
-        return (q + 1) % n
-
     def span(peer, plane):
         return pl.ds(pl.multiple_of(peer * feat + plane * h, h), h)
 
     def sum_copy(q):
-        peer = (me + turn(q)) % n
+        peer = (me + q) % n
         return remote(
             grads.at[:, span(peer, 1 - mp), :],
             across_land.at[q],
@@ -473,7 +785,7 @@
         return remote(inner, inner_land, p_sem.at[0], p_sem.at[1], across)
 
     def loads(q):
-        rows = span((me + turn(q)) % n, mp)
+        rows = span((me + q) % n, mp)
         spot = q % 2
         return [
             pltpu.make_async_copy(grads.at[:, rows, :], d_buf.at[spot], load_sem.at[spot, 0]),
@@ -487,7 +799,7 @@
         ]
 
     def out_copy(q):
-        rows = span((me + turn(q)) % n, mp)
+        rows = span((me + q) % n, mp)
         return pltpu.make_async_copy(output.at[rows, :], g_slots.at[q, STREAMS], out_sem.at[q])
 
     def place(source, plane):
@@ -495,26 +807,26 @@
 
     def stream_copy(q):
         return remote(
-            g_slots.at[q], place(me, mp), a_send.at[q], a_recv.at[q], {"dp": (me + turn(q)) % n}
+            g_slots.at[q], place(me, mp), a_send.at[q], a_recv.at[q], {"dp": (me + q) % n}
         )
 
     def little_copy(q):
         return remote(
-            l_slots.at[q], l_land.at[q], l_send.at[q], l_recv.at[q], {"dp": (me + turn(q)) % n}
+            l_slots.at[q], l_land.at[q], l_send.at[q], l_recv.at[q], {"dp": (me + q) % n}
         )
 
     def second_copy(q):
         return remote(
-            second, second_land.at[me], w_send.at[q], w_recv.at[q], {"dp": (me + turn(q)) % n}
+            second, second_land.at[me], w_send.at[q], w_recv.at[q], {"dp": (me + q) % n}
         )
 
     def home_copy():
-        return pltpu.make_async_copy(g_slots.at[n - 1], place(me, mp), end_sem.at[0])
+        return pltpu.make_async_copy(g_slots.at[0], place(me, mp), end_sem.at[0])
 
     def across_copy(q, own=False):
-        there = place((me - turn(q) + n) % n, mp)
-        return remote(
-            g_slots.at[n - 1] if own else there, there, fy_send.at[q], fy_recv.at[q], across
+        there = place((me - q + n) % n, mp)
+        return remote(
+            g_slots.at[0] if own else there, there, fy_send.at[q], fy_recv.at[q], across
         )
 
     def start_loads(q):
@@ -547,20 +859,30 @@
                 tail = jnp.where(lane == MIXH + s, gain_grad, tail)
             l_slots[q, rows, :] = tail
 
-    def norm_turn(q, last=False):
-        if not last:
+    def norm_turn(q):
+        @pl.when(q < n - 1)
+        def _():
             start_loads(q + 1)
+
+        @pl.when(q < n - AHEAD)
+        def _():
+            sum_copy(q + AHEAD).start()
+
         norm_backward(q)
         out_copy(q).wait()
-        if last:
+
+        @pl.when(q == 0)
+        def _():
             home_copy().start()
             across_copy(q, True).start()
-        else:
+
+        @pl.when(q > 0)
+        def _():
             stream_copy(q).start()
             little_copy(q).start()
 
     def hist_load(q):
-        source = (me - turn(q) + n) % n
+        source = (me - q + n) % n
         return pltpu.make_async_copy(
             hist.at[
                 :,
@@ -572,7 +894,7 @@
         )
 
     def grad_load(q):
-        source = (me - turn(q) + n) % n
+        source = (me - q + n) % n
         return pltpu.make_async_copy(
             feature_side.at[source, pl.ds(0, STREAMS), pl.ds(pl.multiple_of(mp * h, h), h), :],
             f_buf,
@@ -585,7 +907,7 @@
             m_land.at[q],
             m_send.at[q],
             m_recv.at[q],
-            {"dp": (me - turn(q) + n) % n},
+            {"dp": (me - q + n) % n},
         )
 
     def mix_backward(q):
@@ -600,36 +922,47 @@
             for j in range(HIST):
                 m_slots[q, pl.ds(s * HIST + j, 1), :] = jnp.sum(totals[j], axis=0, keepdims=True)
 
-    def mix_turn(q, last=False):
-        if last:
+    def mix_turn(q):
+        @pl.when(q < n - 1)
+        def _():
+            hist_load(q + 1).start()
+
+        @pl.when(q == 0)
+        def _():
             home_copy().wait()
-        else:
-            hist_load(q + 1).start()
+
+        @pl.when(q > 0)
+        def _():
             stream_copy(q).wait_recv()
             across_copy(q).start()
+
         grad_load(q).start()
         grad_load(q).wait()
         hist_load(q).wait()
         mix_backward(q)
-        if not last:
+
+        @pl.when(q > 0)
+        def _():
             mix_copy(q).start()
 
     pieces = [(i, way) for i in range(count) for way in range(2)]
-    units = len(pieces)
 
     inner_copy().start()
     for step in range(2):
         for i, way in pieces:
             core_copy(way, step, i).start()
 
+    @pl.loop(0, AHEAD)
+    def _(q):
+        sum_copy(q).start()
+
     @pl.loop(0, n)
     def _(q):
-        sum_copy(q).start()
         out_copy(q).start()
 
     second_land[me] = second[...]
 
-    @pl.loop(0, n - 1)
+    @pl.loop(1, n)
     def _(q):
         second_copy(q).start()
 
@@ -654,58 +987,35 @@
         for i, way in pieces:
             core_copy(way, step + 1, i).start()
 
-    turns = n // units
-
-    @pl.loop(1, 1 + turns)
+    hist_load(0).start()
+
+    @pl.loop(1, ring - 1)
     def _(step):
         mates_ahead(step)
         for u, (i, way) in enumerate(pieces):
             ring_unit(step, i, way)
-            q = (step - 1) * units + u
-            if u < units - 1:
-                norm_turn(q)
+            if u % 2 == 0:
+
+                @pl.when(step <= n // 4)
+                def _():
+                    norm_turn(4 * (step - 1) + u // 2)
             else:
 
-                @pl.when(step < turns)
+                @pl.when((step >= 2) & (step <= n // 4 + 1))
                 def _():
-                    norm_turn(q)
-
-    norm_turn(n - 1, True)
-    hist_load(0).start()
-
-    @pl.loop(1 + turns, 1 + 2 * turns)
-    def _(step):
-        mates_ahead(step)
-        for u, (i, way) in enumerate(pieces):
-            ring_unit(step, i, way)
-            q = (step - 1 - turns) * units + u
-            if u < units - 1:
-                mix_turn(q)
-            else:
-
-                @pl.when(step < 2 * turns)
-                def _():
-                    mix_turn(q)
-
-    mix_turn(n - 1, True)
-
-    @pl.loop(1 + 2 * turns, ring - 1)
-    def _(step):
-        mates_ahead(step)
-        for i, way in pieces:
-            ring_unit(step, i, way)
-
-    @pl.loop(0, n - 1)
+                    mix_turn(4 * (step - 2) + u // 2)
+
+    @pl.loop(1, n)
     def _(q):
         little_copy(q).wait_recv()
         second_copy(q).wait_recv()
         mix_copy(q).wait_recv()
 
     def sum_over(land, mine):
-        return lax.fori_loop(0, n - 1, lambda q, total: total + land[q], mine)
-
-    l_sum[...] = sum_over(l_land, l_slots[n - 1])
-    m_mine[...] = sum_over(m_land, m_slots[n - 1])
+        return lax.fori_loop(1, n, lambda q, total: total + land[q], mine)
+
+    l_sum[...] = sum_over(l_land, l_slots[0])
+    m_mine[...] = sum_over(m_land, m_slots[0])
     second_sum[...] = lax.fori_loop(
         1, n, lambda q, total: total + second_land[q], second_land[0]
     )
@@ -733,7 +1043,7 @@
     for i in range(count):
         final_copy(1, i).wait()
 
-    @pl.loop(0, n - 1)
+    @pl.loop(1, n)
     def _(q):
         stream_copy(q).wait_send()
         little_copy(q).wait_send()
@@ -863,27 +1173,27 @@
     )(feature_side, mixes)
 
 
-def rotary(heads_in, angles):
-    halfway = ROT // 2
-    cosine = jnp.cos(angles)[:, None, :]
-    sine_part = jnp.sin(angles)[:, None, :]
-    first_half = heads_in[..., :halfway]
-    second_half = heads_in[..., halfway:ROT]
-    return jnp.concatenate(
-        [
-            first_half * cosine - second_half * sine_part,
-            second_half * cosine + first_half * sine_part,
-            heads_in[..., ROT:],
-        ],
-        axis=-1,
-    )
-
-
-def angle_table(length):
+def rotary(heads_in, tables):
+    ahead = jnp.roll(heads_in, -(ROT // 2), axis=-1)
+    behind = jnp.roll(heads_in, ROT // 2, axis=-1)
+    return heads_in * tables[0] + ahead * tables[1] + behind * tables[2]
+
+
+def angle_tables(length):
     halfway = ROT // 2
     frequency = jnp.exp(jnp.arange(halfway, dtype=f32) * (-2.0 * math.log(10000.0) / ROT))
     places = (jnp.arange(length) % TOK_DEV).astype(f32)
-    return places[:, None] * frequency[None, :]
+    angles = places[:, None] * frequency[None, :]
+    cosine, sine_part = jnp.cos(angles), jnp.sin(angles)
+    rest = jnp.zeros((length, HEAD - ROT), f32)
+    none = jnp.zeros((length, halfway), f32)
+    return jnp.stack(
+        [
+            jnp.concatenate([cosine, cosine, rest + 1.0], axis=1),
+            jnp.concatenate([-sine_part, none, rest], axis=1),
+            jnp.concatenate([none, sine_part, rest], axis=1),
+        ]
+    )
 
 
 def gelu_exact(inputs):
@@ -916,26 +1226,16 @@
     small = jnp.pad(
         jnp.concatenate([w_mix1, gains.T], axis=1), ((0, 0), (0, WIDE - MIXH - gains.shape[0]))
     )
-    inputs, mixes, smalls, (full_qkv, full_o, full_up, full_down) = forward_exchange(
-        n, history, cot_out, mix_in.T, small, (w_qkv, w_out, w_up, w_down)
-    )
+    tables = angle_tables(tokens_here)
+    kept, (full_qkv, full_o, full_up, full_down) = forward_exchange(
+        n, history, cot_out, mix_in.T, small, tables, doc_ids, (w_qkv, w_out, w_up, w_down)
+    )
+    inputs, mixes, smalls, normed, level, qkv_heads, attn_cat, up_pre, hidden, out_full = kept
+    queries, key_heads, values = qkv_heads[0], qkv_heads[1], qkv_heads[2]
+    heads_here = full_qkv.shape[2] // HEAD
+    width_here = heads_here * HEAD
     full_m1 = smalls[:, :MIXH]
     gain_f = smalls[:, MIXH : MIXH + STREAMS + 1].astype(f32)
-    heads_here = full_qkv.shape[2] // HEAD
-    width_here = heads_here * HEAD
-    streams = inputs[:STREAMS].astype(f32)
-    level = lax.rsqrt(jnp.mean(streams * streams, axis=1) + EPS)
-    normed = [
-        (streams[s] * level[s][None, :] * gain_f[:, s : s + 1]).astype(bf16) for s in range(STREAMS)
-    ]
-    angles = angle_table(tokens_here)
-
-    def project(s):
-        return product("dt,dn->tn", normed[s], full_qkv[s]).reshape(tokens_here, heads_here, HEAD)
-
-    queries = rotary(project(0), angles).astype(bf16).transpose(1, 0, 2)
-    key_heads = rotary(project(1), angles).astype(bf16).transpose(1, 0, 2)
-    values = project(2).astype(bf16).transpose(1, 0, 2)
     scale_qk = HEAD ** (-0.5)
     positions = jnp.arange(tokens_here)
     doc_row = doc_ids[0]
@@ -946,15 +1246,6 @@
     log_total = row_max + jnp.log(jnp.sum(jnp.exp(scores - row_max), axis=-1, keepdims=True))
     attn_probs = jnp.exp(scores - log_total)
     probs_low = attn_probs.astype(bf16)
-    attended = product("hqk,hkd->hqd", probs_low, values)
-    attn_cat = attended.astype(bf16).transpose(1, 0, 2).reshape(tokens_here, width_here)
-    up_pre = product("dt,dn->tn", normed[3], full_up)
-    hidden = gelu_exact(up_pre).astype(bf16)
-    branch_part = product("oi,ti->ot", full_o, attn_cat) + product("oi,ti->ot", full_down, hidden)
-    branch_low = branch_part.astype(bf16)
-    swap = [(0, 1), (1, 0)]
-    branch = branch_low.astype(f32) + lax.ppermute(branch_low, "mp", swap).astype(f32)
-    out_full = streams[3] + branch
     out_low = out_full.astype(bf16)
     mix_level = lax.rsqrt(jnp.mean(out_full * out_full, axis=0) + EPS)
     mix_unit = out_full * mix_level[None, :]
@@ -995,13 +1286,15 @@
     grad_q_rot = product("hqk,hkd->hqd", grad_scores, key_heads) * scale_qk
     grad_k_rot = product("hqk,hqd->hkd", grad_scores, queries) * scale_qk
 
+    back_tables = (tables[0], -tables[1], -tables[2])
+
     def flat(heads):
-        return heads.reshape(tokens_here, width_here).astype(bf16)
+        return heads.astype(bf16).transpose(1, 0, 2).reshape(tokens_here, width_here)
 
     grad_projs = (
-        flat(rotary(grad_q_rot.transpose(1, 0, 2), -angles)),
-        flat(rotary(grad_k_rot.transpose(1, 0, 2), -angles)),
-        flat(grad_values.transpose(1, 0, 2)),
+        flat(rotary(grad_q_rot, back_tables)),
+        flat(rotary(grad_k_rot, back_tables)),
+        flat(grad_values),
     )
     grad_qkv_part = jnp.stack(
         [product("dt,tn->dn", normed[s], grad_projs[s]).astype(bf16) for s in range(3)]
@@ -1010,7 +1303,7 @@
         [product("dn,tn->dt", full_qkv[s], grad_projs[s]).astype(bf16) for s in range(3)]
         + [grad_normed_ff.astype(bf16)]
     )
-    norm_inner = jnp.sum(jnp.stack(normed).astype(f32) * grad_normed.astype(f32), axis=1)
+    norm_inner = jnp.sum(normed.astype(f32) * grad_normed.astype(f32), axis=1)
 
     def eight(rows):
         return jnp.pad(rows, ((0, 8 - rows.shape[0]), (0, 0)))
@@ -1029,7 +1322,7 @@
         n,
         grad_normed,
         eight(norm_inner),
-        eight(level),
+        level,
         inputs,
         grad_out_full,
         out_low,

time: 1070 us -> 982 us (0.918)
  Pallas kernels: 749 us -> 814 us
  matrix products: 157 us -> 106 us
  local copies, waits for them, and re-layouts: 71.4 us -> 25.4 us
  waiting for transfers between devices: 34 us -> 0 us
  other arithmetic: 44.8 us -> 26.9 us
    pallas_call x1, Pallas kernels: 365 us -> 429 us  [forward_exchange(): pl.pallas_call(functools.partial(forward_kernel, n, count), out_shape=[ja...]
    dot_general x30 -> x23, matrix products: 157 us -> 106 us  [product(): return jnp.einsum(spec, left, right, preferred_element_type=f32)]
    ppermute x1 -> x0, waiting for transfers between devices: 34 us -> none  [body(): lax.ppermute(branch_low, 'mp', swap).astype(f32)]
    dot_general x4 -> x0, local copies, waits for them, and re-layouts: 28.8 us -> none  [product(): return jnp.einsum(spec, left, right, preferred_element_type=f32)]
    convert_element_type x5 -> x2, other arithmetic: 17.3 us -> 0.84 us  [the longest x1 0.84 us: flat(): heads.astype(bf16).transpose(1, 0, 2).reshape(tokens_here, width_here)]
    unnamed x156 -> x104, local copies, waits for them, and re-layouts: 31.1 us -> 15.2 us
  transfers between devices with their start and end apart: 1 -> 0, of which waited for: 1 -> 0; matrix products, arithmetic and copies ran while one was open for 0% -> 0% of each run, Pallas kernels for 0% -> 0%
where the time goes in v3:
time: 982 us; the launch traced here: 974 us
  Pallas kernels  814 us (83%)
  matrix products  106 us (11%)
  other arithmetic  26.9 us (3%)
  local copies, waits for them, and re-layouts  25.4 us (3%)
    pallas_call x1, Pallas kernels, forward_exchange(): pl.pallas_call(functools.partial(forward_kernel, n, count), out_shape=[ja...  429 us
    pallas_call x1, Pallas kernels, backward_exchange(): pl.pallas_call(functools.partial(backward_kernel, n, count), out_shape=[j...  373 us
    dot_general x23, matrix products, product(): return jnp.einsum(spec, left, right, preferred_element_type=f32)  106 us

profile of v3, /device:TPU:21, one launch (start us, length us, event | category | flops | bytes accessed | tf_op | source)
XLA Modules:
  0.0 974.2 jit_solution(4217471909238534753)
XLA Ops:
  2.2 0.8 multiply_cosine_fusion
  3.1 1.0 fusion.87
  4.1 0.9 pad_maximum_fusion.2.refs_4_
  4.9 1.5 copy.91.refs_6_
  6.4 429.1 %shard_map.221 = (bf16[5,2048,384]{2,1,0:T(8,128)(2,1)}, f32[16,36,384]{2,1,0:T(8,128)}, bf16[2048,128]{1,0:T(8,128)(2,1)}, bf16[4,2048,384]{2,1,0:T(8,128)(2,1)...) custom-call(bf16[9,128,6144]{2,1,0:T(8,128)(2,1)} %refs_9_.3, ...), custom_call_target="tpu_custom_call" | custom-call | tf_op jit(solution)/shard_map/pallas_call | solution.py:586
  435.6 2.4 multiply_reduce_fusion.4
  437.9 1.4 convert_reduce_fusion
  440.5 2.7 multiply_reduce_fusion.2
  443.3 4.2 fusion.101
  447.5 25.3 %fusion.4 = bf16[384,4096]{1,0:T(8,128)(2,1)} fusion(f32[384,4096]{1,0:T(8,128)} %get-tuple-element.42, bf16[2048,384]{1,0:T(8,128)(2,1)S(1)} %get-tuple-element.118, bf16[2048,4096]{1,0:T(8,128)(2,1)} %get-tuple-element.43), kind=kOutput, calls=%fused_computation.9 | convolution fusion | flops 6555697152 | bytes 27787264 | tf_op jit(solution)/shard_map/ot,oi->ti/dot_general | solution.py:1204
  472.8 12.5 %fusion.32 = bf16[1,2048,384]{2,1,0:T(8,128)(2,1)} fusion(bf16[2048,4096]{1,0:T(8,128)(2,1)S(1)} %bitcast.150, bf16[384,4096]{1,0:T(8,128)(2,1)} %fusion.4), kind=kOutput, calls=%fused_computation.55 | convolution fusion | flops 6443237376 | bytes 21495808 | tf_op jit(solution)/shard_map/dn,tn->dt/dot_general | solution.py:1204
  485.4 2.7 convolution_convert_fusion.4
  488.1 1.5 copy.113
  489.7 0.9 fusion.21
  490.7 1.0 exponential_reduce_fusion
  491.7 1.4 fusion.63
  493.1 0.9 copy-done.37
  494.0 5.7 fusion.33
  499.6 1.4 multiply_reduce_fusion.1
  501.1 1.3 multiply_convert_fusion
  502.3 3.0 broadcast_multiply_fusion.1
  505.3 0.8 fusion.103
  506.1 1.8 fusion.104
  507.9 0.8 copy.98
  508.7 0.8 copy.97
  509.6 2.0 broadcast_multiply_fusion
  512.0 1.1 copy-done.8
  514.1 0.8 fusion.51
  515.0 4.9 fusion.36
  519.9 4.7 fusion.39
  524.6 3.5 pad_maximum_fusion.1.refs_0_
  528.0 1.7 multiply_reduce_fusion
  531.5 1.3 maximum_maximum_fusion.refs_7_
  533.5 3.9 convert_bitcast_fusion
  537.5 2.4 convert_bitcast_fusion.1
  539.9 2.4 convert_bitcast_fusion.2
  542.3 5.4 pad_maximum_fusion.refs_11_
  547.7 4.4 convolution_convert_fusion.2.refs_12_
  552.1 11.7 %convolution_convert_fusion.1.refs_13_ = bf16[2048,4096]{1,0:T(8,128)(2,1)} fusion(bf16[384,4096]{1,0:T(8,128)(2,1)S(1)} %copy-done.39, bf16[4,2048,384]{2,1,0:T(8,128)(2,1)S(1)} %bitcast.135), kind=kOutput, calls=%fused_computation.1 | convolution fusion | flops 6450839552 | bytes 21495808 | tf_op jit(solution)/shard_map/dt,tn->dn/dot_general | solution.py:1204
  563.8 11.9 %convolution_convert_fusion.refs_14_ = bf16[2048,4096]{1,0:T(8,128)(2,1)} fusion(bf16[2048,384]{1,0:T(8,128)(2,1)S(1)} %copy-done.16, bf16[384,4096]{1,0:T(8,128)(2,1)S(1)} %copy-done.35), kind=kOutput, calls=%fused_computation | convolution fusion | flops 6450839552 | bytes 21495808 | tf_op jit(solution)/shard_map/ot,ti->oi/dot_general | solution.py:1204
  575.7 373.2 %shard_map.222 = (bf16[16,4,64,384]{3,2,1,0:T(8,128)(2,1)}, bf16[16,5,128,384]{3,2,1,0:T(8,128)(2,1)}, f32[36,384]{1,0:T(8,128)}, f32[128,128]{1,0:T(8,128)}, f3...) custom-call(bf16[4,2048,384]{2,1,0:T(8,128)(2,1)} %pad_maximum_fusio, ...), custom_call_target="tpu_custom_call" | custom-call | tf_op jit(solution)/shard_map/pallas_call | solution.py:1082
  948.9 3.2 copy-done.1
  952.2 12.1 %shard_map.223 = (bf16[9,128,6144]{2,1,0:T(8,128)(2,1)}, bf16[128,6144]{1,0:T(8,128)(2,1)}) custom-call(bf16[16,5,128,384]{3,2,1,0:T(8,128)(2,1)S(1)} %copy-done.1, f32[16,36,384]{2,1,0:T(8,128)S(1)} %copy-done.2), custom_call_target="tpu_custom_call" | custom-call | tf_op jit(solution)/shard_map/pallas_call | solution.py:1157
  964.3 0.8 fusion.109
  967.1 2.8 copy.121
  969.9 0.8 copy.122
  970.7 1.3 copy.123
  972.0 1.3 copy.124
  (133 shorter events, 9.6 us)
Async XLA Ops:
  0.6 439.7 %copy-start = (bf16[384,40]{0,1:T(8,128)(2,1)S(1)}, bf16[384,40]{0,1:T(8,128)(2,1)}, u32[]{:S(2)}) copy-start(bf16[384,40]{0,1:T(8,128)(2,1)} %param.27) | copy-start | bytes 92164
  435.6 3.8 copy-start.3
  435.6 4.2 copy-start.11
  437.9 2.4 copy-start.30
  439.8 3.4 copy-start.6
  440.3 2.9 copy-start.32
  440.3 2.9 copy-start.33
  443.3 29.5 %slice-start.4 = ((s8[16777216]{0:T(1024)(128)(4,1)}), s8[4194304]{0:T(1024)(128)(4,1)S(1)}, s32[]{:S(2)}) async-start(s8[16777216]{0:T(1024)(128)(4,1)} %bitcast.149), calls=%async_computation.4 | async-start | bytes 8388608
  447.5 37.8 %copy-start.15 = (bf16[2048,384]{1,0:T(8,128)(2,1)}, bf16[2048,384]{1,0:T(8,128)(2,1)S(1)}, u32[]{:S(2)}) copy-start(bf16[2048,384]{1,0:T(8,128)(2,1)S(1)} %get-tuple-element.118) | copy-start | bytes 4718596
  447.5 25.3 %slice-start.5 = ((s8[16777216]{0:T(1024)(128)(4,1)}), s8[4194304]{0:T(1024)(128)(4,1)S(1)}, s32[]{:S(2)}) async-start(s8[16777216]{0:T(1024)(128)(4,1)} %bitcast.149), calls=%async_computation.5 | async-start | bytes 8388608
  447.5 25.3 %slice-start.6 = ((s8[16777216]{0:T(1024)(128)(4,1)}), s8[4194304]{0:T(1024)(128)(4,1)S(1)}, s32[]{:S(2)}) async-start(s8[16777216]{0:T(1024)(128)(4,1)} %bitcast.149), calls=%async_computation.6 | async-start | bytes 8388608
  447.5 25.3 %slice-start.7 = ((s8[16777216]{0:T(1024)(128)(4,1)}), s8[4194304]{0:T(1024)(128)(4,1)S(1)}, s32[]{:S(2)}) async-start(s8[16777216]{0:T(1024)(128)(4,1)} %bitcast.149), calls=%async_computation.7 | async-start | bytes 8388608
  472.8 12.5 %copy-start.34 = (bf16[2048,1024]{1,0:T(8,128)(2,1)S(1)}, bf16[2048,1024]{1,0:T(8,128)(2,1)}, u32[]{:S(2)}) copy-start(bf16[2048,1024]{1,0:T(8,128)(2,1)} %get-tuple-element.40) | copy-start | bytes 12582916
  485.4 4.2 copy-start.29
  485.4 4.4 copy-start.12
  493.1 0.9 copy-start.37
  505.3 2.6 copy-start.20
  505.3 3.4 copy-start.19
  511.7 1.4 copy-start.8
  511.7 1.8 copy-start.9
  511.7 2.2 copy-start.10
  511.7 2.2 copy-start.21
  511.7 2.2 copy-start.22
  511.7 2.3 copy-start.23
  511.7 2.3 copy-start.24
  514.9 4.9 copy-start.17
  514.9 13.1 %slice-start = ((s8[6291456]{0:T(1024)(128)(4,1)}), s8[4194304]{0:T(1024)(128)(4,1)S(1)}, s32[]{:S(2)}) async-start(s8[6291456]{0:T(1024)(128)(4,1)} %bitcast.132), calls=%async_computation | async-start | bytes 8388608
  519.8 4.7 copy-start.4
  519.8 4.7 copy-start.5
  519.9 8.2 slice-start.1
  528.0 2.7 copy-start.7
  530.7 2.8 copy-start.38
  530.7 6.7 slice-start.2
  533.5 4.0 slice-start.3
  533.5 4.0 copy-start.18
  542.3 5.4 copy-start.16
  542.3 5.4 copy-start.36
  547.7 4.4 copy-start.39
  552.1 11.7 %copy-start.35 = (bf16[384,4096]{1,0:T(8,128)(2,1)S(1)}, bf16[384,4096]{1,0:T(8,128)(2,1)}, u32[]{:S(2)}) copy-start(bf16[384,4096]{1,0:T(8,128)(2,1)} %get-tuple-element.48) | copy-start | bytes 9437188
  575.7 373.2 %copy-start.2 = (f32[16,36,384]{2,1,0:T(8,128)S(1)}, f32[16,36,384]{2,1,0:T(8,128)}, u32[]{:S(2)}) copy-start(f32[16,36,384]{2,1,0:T(8,128)} %get-tuple-element.46.refs_10_.mixes) | copy-start | bytes 2654212
  948.9 3.2 copy-start.1
  952.1 12.1 %copy-start.31 = (bf16[40,40]{1,0:T(8,128)(2,1)S(1)}, bf16[40,40]{1,0:T(8,128)(2,1)}, u32[]{:S(2)}) copy-start(bf16[40,40]{1,0:T(8,128)(2,1)} %param.24) | copy-start | bytes 9604
  952.2 12.9 %copy-start.26 = (f32[128,128]{1,0:T(8,128)S(1)}, f32[128,128]{1,0:T(8,128)}, u32[]{:S(2)}) copy-start(f32[128,128]{1,0:T(8,128)} %get-tuple-element.57) | copy-start | bytes 196612
  952.2 14.4 %copy-start.27 = (f32[36,384]{1,0:T(8,128)S(1)}, f32[36,384]{1,0:T(8,128)}, u32[]{:S(2)}) copy-start(f32[36,384]{1,0:T(8,128)} %get-tuple-element.52) | copy-start | bytes 165892
  952.2 17.7 %copy-start.25 = (f32[128,1024]{1,0:T(8,128)S(1)}, f32[128,1024]{1,0:T(8,128)}, u32[]{:S(2)}) copy-start(f32[128,1024]{1,0:T(8,128)} %get-tuple-element.170) | copy-start | bytes 1572868
  964.3 7.8 copy-start.13
  966.5 4.2 copy-start.14
  969.9 3.4 copy-start.28

commit v4 on v3

--- a/solution.py
+++ b/solution.py
@@ -16,9 +16,9 @@
 TOK_DEV = 384
 MIXH = 40
 WIDE = 128
+MIXED = 48
 EPS = 1e-05
-AHEAD = 6
-CUTS = (1, 1, 2, 2)
+CUTS = (1, 1, 2, 2, 1)
 MESH = pl.DeviceIdType.MESH
 DMA = pltpu.SemaphoreType.DMA
 f32 = jnp.float32
@@ -95,11 +95,11 @@
 
 
 def forward_kernel(n, count, *refs):
-    hist, cot, mix, small, tables, docs_row, docs_col = refs[:7]
-    shards = refs[7 : 7 + count]
-    refs = refs[7 + count :]
-    inputs, mixes, smalls, normed_out, level, heads_out, attn_out, pre_out, hidden_out, total = refs[:10]
-    fulls = refs[10 : 10 + count]
+    hist, cot, mix, tables, docs_row, docs_col = refs[:6]
+    shards = refs[6 : 6 + count]
+    refs = refs[6 + count :]
+    inputs, mixes, normed_out, level, heads_out, attn_out, slope_out, hidden_out, total = refs[:9]
+    fulls = refs[9 : 9 + count]
     (
         hist_buf,
         slots,
@@ -108,26 +108,25 @@
         tiles,
         heads,
         attn,
-        pre_buf,
+        slope_buf,
         hidden,
         down_buf,
         out_buf,
         branch,
         branch_land,
+        smalls,
         hist_sem,
         cot_sem,
         own_sem,
         local_sem,
         keep_sem,
         tile_sem,
-        pre_sem,
+        slope_sem,
         row_sem,
         swap_send,
         swap_recv,
         mix_send,
         mix_recv,
-        small_send,
-        small_recv,
         a_send,
         a_recv,
         y_send,
@@ -136,7 +135,7 @@
         ring_recv,
         core_send,
         core_recv,
-    ) = refs[10 + count :]
+    ) = refs[9 + count :]
     where = Ring(n)
     me, ring, owner = where.me, where.ring, where.owner
     mp = lax.axis_index("mp")
@@ -146,7 +145,7 @@
     width = n * feat
     size = shards[0].shape[-2]
     half = size // 2
-    w_qkv, w_out, w_up, w_down = fulls
+    w_qkv, w_out, w_up, w_down, all_small = fulls
     greet_plane(n, me, mp)
 
     pieces = cuts_of(shards, CUTS)
@@ -212,15 +211,6 @@
     def mix_copy(q):
         return remote(
             mix, mixes.at[me], mix_send.at[q], mix_recv.at[q], {"dp": (me + q) % n}
-        )
-
-    def small_copy(q):
-        return remote(
-            small,
-            smalls.at[pl.ds(pl.multiple_of(me * feat, feat), feat)],
-            small_send.at[q],
-            small_recv.at[q],
-            {"dp": (me + q) % n},
         )
 
     def lanes(peer):
@@ -357,11 +347,11 @@
             for k in range(2)
         ]
 
-    def pre_copy(c):
+    def slope_copy(c):
         return pltpu.make_async_copy(
-            pre_buf.at[c % 2],
-            pre_out.at[:, pl.ds(pl.multiple_of(c * chunk, chunk), chunk)],
-            pre_sem.at[c % 2],
+            slope_buf.at[c % 2],
+            slope_out.at[:, pl.ds(pl.multiple_of(c * chunk, chunk), chunk)],
+            slope_sem.at[c % 2],
         )
 
     def feed(c, spot):
@@ -375,14 +365,16 @@
 
         @pl.when(c >= 2)
         def _():
-            pre_copy(c - 2).wait()
+            slope_copy(c - 2).wait()
 
         for k in range(2):
             pre = first_dims(normed[STREAMS - 1], tiles[spot * 2 + k])
-            pre_buf[c % 2, :, k * 256 : (k + 1) * 256] = pre
-            low = (0.5 * pre * (1.0 + lax.erf(pre * math.sqrt(0.5)))).astype(bf16)
+            below = 0.5 + 0.5 * lax.erf(pre * math.sqrt(0.5))
+            bell = jnp.exp(-0.5 * pre * pre) * (1.0 / math.sqrt(2.0 * math.pi))
+            slope_buf[c % 2, :, k * 256 : (k + 1) * 256] = below + pre * bell
+            low = (pre * below).astype(bf16)
             hidden[:, pl.ds(pl.multiple_of(c * chunk + k * 256, 256), 256)] = low
-        pre_copy(c).start()
+        slope_copy(c).start()
 
     deep = down_buf.shape[1]
 
@@ -428,18 +420,13 @@
     @pl.loop(1, n)
     def _(q):
         mix_copy(q).start()
-        small_copy(q).start()
 
     @pl.loop(0, n)
     def _(q):
         cot_copy(q).start()
 
     hist_copy(0).start()
-    ring_begin(of(0, 1))
-    own_small = pltpu.make_async_copy(
-        small, smalls.at[pl.ds(pl.multiple_of(me * feat, feat), feat)], local_sem.at[count]
-    )
-    own_small.start()
+    ring_begin(of(0, 1, 4))
     mixes[me] = mix[...]
     hist_copy(0).wait()
     hist_copy(1).start()
@@ -461,45 +448,56 @@
 
     @pl.loop(1, ring - 1)
     def _(step):
-        ring_step(step, of(0, 1))
+        ring_step(step, of(0, 1, 4))
         for u in range(2):
             stream_turn(2 + 2 * step + u)
         for u in range(2):
             forward_turn(2 * step - 1 + u)
 
-    ring_end(of(0, 1))
+    ring_end(of(0, 1, 4))
     ring_begin(of(3))
-
-    @pl.loop(n - 3, n)
-    def _(q):
-        forward_turn(q)
-
-    own_copy().wait()
-    own_small.wait()
-
-    @pl.loop(1, n)
-    def _(q):
-        small_copy(q).wait_recv()
-
-    @pl.loop(0, n)
-    def _(q):
-        across_copy(q).wait_recv()
-
-    keep(0).start()
-    ring_complete(0, 1)
-    for copy in head_tiles(0, 0):
-        copy.start()
-    normalise()
-    keep(1).start()
     pairs = heads.shape[1] // 2
+    last = ring - 2
+    early = 3
+
+    def streams_here():
+        ring_complete(0, 1, 4)
+        gains_copy = pltpu.make_async_copy(all_small, smalls, local_sem.at[count])
+        gains_copy.start()
+        for copy in head_tiles(0, 0):
+            copy.start()
+        own_copy().wait()
+
+        @pl.loop(0, n)
+        def _(q):
+            across_copy(q).wait_recv()
+
+        keep(0).start()
+        gains_copy.wait()
+        normalise()
+        keep(1).start()
 
     @pl.loop(1, ring - 1)
     def _(step):
         ring_step(step, of(2))
 
-        @pl.when(step <= pairs)
-        def _():
-            attend(step - 1)
+        @pl.when(step == 1)
+        def _():
+            @pl.loop(n - 3, n)
+            def _(q):
+                forward_turn(q)
+
+        @pl.when(step > last - early)
+        def _():
+            ring_step(step - (last - early), of(3))
+
+        @pl.when(step == last - pairs)
+        def _():
+            streams_here()
+
+        @pl.when(step > last - pairs)
+        def _():
+            attend(step - (last - pairs) - 1)
 
     keep(2).start()
     keep(3).start()
@@ -508,16 +506,17 @@
     for copy in up_tile(0, 0):
         copy.start()
 
-    @pl.loop(1, ring - 1)
+    @pl.loop(early + 1, ring - 1)
     def _(step):
         ring_step(step, of(3))
 
-        @pl.when(step <= ups - 2)
-        def _():
-            feed(step - 1, (step - 1) % 2)
-
-    feed(ups - 2, (ups - 2) % 2)
-    feed(ups - 1, (ups - 1) % 2)
+        @pl.when(2 * (step - early) <= ups - 2)
+        def _():
+            for u in range(2):
+                feed(2 * (step - early - 1) + u, u)
+
+    for c in range(ups - 2, ups):
+        feed(c, c % 2)
     keep(4).start()
     ring_end(of(3))
     ring_complete(3)
@@ -543,7 +542,7 @@
             total[rows, :] = streams[STREAMS - 1, rows, :].astype(f32) + both
 
     for c in range(ups - 2, ups):
-        pre_copy(c).wait()
+        slope_copy(c).wait()
     for k in range(5):
         keep(k).wait()
     for c in range(rounds):
@@ -552,7 +551,6 @@
     @pl.loop(1, n)
     def _(q):
         mix_copy(q).wait_send()
-        small_copy(q).wait_send()
         stream_copy(q).wait_send()
 
     @pl.loop(0, n)
@@ -572,7 +570,7 @@
                 ring_copy(way, step, p).wait_send()
 
 
-def forward_exchange(n, history, cot_out, mix, small, tables, docs, shards):
+def forward_exchange(n, history, cot_out, mix, tables, docs, shards):
     count, ring = len(shards), n // 2
     feat, tokens = history.shape[1], mix.shape[1]
     h, width = feat // 2, n * feat
@@ -588,7 +586,6 @@
         out_shape=[
             jax.ShapeDtypeStruct((STREAMS + 1, width, tokens), bf16),
             jax.ShapeDtypeStruct((n,) + mix.shape, f32),
-            jax.ShapeDtypeStruct((width, WIDE), bf16),
             jax.ShapeDtypeStruct((STREAMS, width, tokens), bf16),
             jax.ShapeDtypeStruct((8, tokens), f32),
             jax.ShapeDtypeStruct((3, across, tokens, HEAD), bf16),
@@ -601,8 +598,8 @@
             jax.ShapeDtypeStruct(s.shape[:-2] + (s.shape[-2] * n, s.shape[-1]), s.dtype)
             for s in shards
         ],
-        in_specs=[hbm, hbm, vmem, hbm, vmem, vmem, vmem] + [hbm] * count,
-        out_specs=[hbm, vmem, vmem, hbm, vmem, hbm, hbm, hbm, hbm, vmem] + [hbm] * count,
+        in_specs=[hbm, hbm, vmem, vmem, vmem, vmem] + [hbm] * count,
+        out_specs=[hbm, vmem, hbm, vmem, hbm, hbm, hbm, hbm, vmem] + [hbm] * count,
         scratch_shapes=[
             pltpu.VMEM((2, HIST, h, tokens), bf16),
             pltpu.VMEM((n, STREAMS + 1, h, tokens), bf16),
@@ -617,6 +614,7 @@
             pltpu.VMEM((2, deep, columns), bf16),
             pltpu.VMEM((width, tokens), bf16),
             pltpu.VMEM((width, tokens), bf16),
+            pltpu.VMEM((width, WIDE), bf16),
             DMA((2,)),
             DMA((n,)),
             DMA,
@@ -628,27 +626,53 @@
             DMA((rounds,)),
             DMA((rounds,)),
         ]
-        + [DMA((n,)) for _ in range(8)]
+        + [DMA((n,)) for _ in range(6)]
         + [DMA((2, ring - 1, travel)) for _ in range(2)]
         + [DMA((2, ring, travel)) for _ in range(2)],
         compiler_params=pltpu.CompilerParams(
             collective_id=0, has_side_effects=True, vmem_limit_bytes=60 * 1024 * 1024
         ),
-    )(history, cot_out, mix, small, tables, docs, docs.T, *shards)
-    return found[:10], found[10:]
+    )(history, cot_out, mix, tables, docs, docs.T, *shards)
+    return found[:9], found[9:]
 
 
 def backward_kernel(n, count, *refs):
-    grads, inner, scale, inputs, direct, output, smalls, little, second, hist, mixes = refs[:11]
-    parts = refs[11 : 11 + count]
-    refs = refs[11 + count :]
-    across_land, feature_side, mix_sum, little_sum, second_sum = refs[:5]
-    sums, mates = refs[5 : 5 + count], refs[5 + count : 5 + 2 * count]
-    refs = refs[5 + 2 * count :]
-    slots, own, other, final = (refs[k * count : (k + 1) * count] for k in range(4))
     (
+        normed,
+        grad_branch,
+        hidden,
+        attn,
+        grad_up,
+        heads,
+        grad_attended,
+        w_qkv,
+        w_up,
+        tables,
+        docs_row,
+        docs_col,
+        level,
+        inputs,
+        direct,
+        output,
+        smalls,
+        little,
+        second,
+        hist,
+        mixes,
+    ) = refs[:21]
+    across_land, feature_side, mix_sum, little_sum, second_sum = refs[21:26]
+    sums, mates = refs[26 : 26 + count], refs[26 + count : 26 + 2 * count]
+    refs = refs[26 + 2 * count :]
+    slots, other, mine, final = (refs[k * count : (k + 1) * count] for k in range(4))
+    (
+        rows_buf,
+        projs,
+        grads,
+        qkv_tile,
+        up_tile,
+        n_tile,
+        inner,
         inner_land,
-        d_buf,
         e_buf,
         x_buf,
         go_buf,
@@ -658,17 +682,20 @@
         l_slots,
         l_land,
         second_land,
+        second_own,
         f_buf,
         h_buf,
+        m_wide,
         m_slots,
         m_land,
         m_mine,
         m_other,
         l_sum,
+        rows_sem,
+        tile_sem,
         load_sem,
         out_sem,
         back_sem,
-        own_sem,
         other_sem,
         final_sem,
         y_send,
@@ -694,43 +721,79 @@
     me, ring, owner = where.me, where.ring, where.owner
     mp = lax.axis_index("mp")
     across = {"mp": 1 - mp}
-    feat, tokens = hist.shape[1], inner.shape[1]
+    feat, tokens = hist.shape[1], level.shape[1]
     h = feat // 2
+    width = n * feat
     size = sums[0].shape[-2]
     half = size // 2
     greet_plane(n, me, mp)
 
+    def first_dims(left, right):
+        return lax.dot_general(left, right, (((0,), (0,)), ((), ())), preferred_element_type=f32)
+
+    def last_dims(left, right):
+        return lax.dot_general(left, right, (((1,), (1,)), ((), ())), preferred_element_type=f32)
+
     def target(way, step):
         return -1 - step if way == 0 else 1 + step
 
+    def rows_load(way, step):
+        spot = step % 3
+        copies = []
+        for which in range(2):
+            shard = owner(target(way, step)) + which * (where.mate - me)
+            rows = pl.ds(pl.multiple_of(shard * size + way * half, half), half)
+            copies += [
+                pltpu.make_async_copy(
+                    normed.at[:, rows, :],
+                    rows_buf.at[way, spot, which, pl.ds(0, STREAMS)],
+                    rows_sem.at[way, spot, 2 * which],
+                ),
+                pltpu.make_async_copy(
+                    grad_branch.at[rows, :],
+                    rows_buf.at[way, spot, which, STREAMS],
+                    rows_sem.at[way, spot, 2 * which + 1],
+                ),
+            ]
+        return copies
+
+    def part(way, step, i, which, k, columns):
+        source = (k, STREAMS, STREAMS - 1, STREAMS)[i]
+        left = rows_buf[way, step % 3, which, source]
+        right = (projs, attn, grad_up, hidden)[i]
+        right = right[k, :, columns] if i == 0 else right[:, columns]
+        return jnp.dot(left, right, preferred_element_type=f32)
+
+    strip = 1024
+
+    def strips(i, work):
+        deep = len(sums[i].shape) == 3
+        for k in range(sums[i].shape[0] if deep else 1):
+
+            @pl.loop(0, sums[i].shape[-1] // strip)
+            def _(c):
+                columns = pl.ds(pl.multiple_of(c * strip, strip), strip)
+                at = (k, slice(None), columns) if deep else (slice(None), columns)
+                work(k, columns, at)
+
     def core_copy(way, step, i):
-        theirs = owner(target(way, step)) + (where.mate - me)
-        start = pl.multiple_of(theirs * size + way * half, half)
         return remote(
-            rows_of(parts[i], start, half),
+            mine[i].at[way],
             mates[i].at[way, step],
             core_send.at[way, step, i],
             core_recv.at[way, step, i],
             {"dp": where.mate},
         )
 
-    def own_copy(way, step, i):
-        start = pl.multiple_of(owner(target(way, step)) * size + way * half, half)
-        spot = step % 2
+    def other_copy(way, step, i):
         return pltpu.make_async_copy(
-            rows_of(parts[i], start, half), own[i].at[way, spot], own_sem.at[way, spot, i]
-        )
-
-    def other_copy(way, step, i):
-        spot = step % 2
-        return pltpu.make_async_copy(
-            mates[i].at[way, step], other[i].at[way, spot], other_sem.at[way, spot, i]
+            mates[i].at[way, step], other[i].at[way], other_sem.at[way, i]
         )
 
     def ring_copy(way, step, i):
         return remote(
-            slots[i].at[way, step],
-            slots[i].at[way, step + 1],
+            slots[i].at[way, step % 4],
+            slots[i].at[way, (step + 1) % 4],
             ring_send.at[way, step, i],
             ring_recv.at[way, step, i],
             where.next_of[way],
@@ -741,32 +804,101 @@
             final[i], rows_of(sums[i], way * half, half), final_sem.at[i]
         )
 
+    def give(way, step, i):
+        def work(k, columns, at):
+            mine[i][(way,) + at] = part(way, step, i, 1, k, columns).astype(bf16)
+
+        strips(i, work)
+        core_copy(way, step, i).start()
+
     def stage(way, step, i):
-        own_copy(way, step, i).start()
         core_copy(way, step, i).wait_recv()
         other_copy(way, step, i).start()
 
-    def staged(way, step, i):
-        own_copy(way, step, i).wait()
+    def add(way, step, i, first=False, last=False):
+        def work(k, columns, at):
+            total = part(way, step, i, 0, k, columns) + other[i][(way,) + at].astype(f32)
+            place = (way, step % 4) + at
+            if not first:
+                total = total + slots[i][place].astype(f32)
+            if last:
+                final[i][at] = total
+            else:
+                slots[i][place] = total.astype(bf16)
+
+        strips(i, work)
+
+    def ring_unit(step, i, way):
         other_copy(way, step, i).wait()
-
-    def add(way, step, i, first=False, last=False):
-        spot = step % 2
-        deep = len(parts[i].shape) == 3
-        slot, mine, theirs = slots[i].at[way, step], own[i].at[way, spot], other[i].at[way, spot]
-        for k in range(parts[i].shape[0] if deep else 1):
-
-            @pl.loop(0, half // 16)
-            def _(r):
-                rows = pl.ds(pl.multiple_of(r * 16, 16), 16)
-                at = (k, rows) if deep else (rows,)
-                total = mine[at].astype(f32) + theirs[at].astype(f32)
-                if not first:
-                    total = total + slot[at].astype(f32)
-                if last:
-                    final[i][at] = total
-                else:
-                    slot[at] = total.astype(bf16)
+        ring_copy(way, step - 1, i).wait_recv()
+        add(way, step, i)
+        ring_copy(way, step, i).start()
+        core_copy(way, step, i).wait_send()
+        give(way, step + 1, i)
+
+    def attend_back(head):
+        lane = pl.ds(pl.multiple_of(head * HEAD, HEAD), HEAD)
+        query, key, value = heads[0, head], heads[1, head], heads[2, head]
+        grad = grad_attended[:, lane]
+        place = lax.broadcasted_iota(jnp.int32, (tokens, tokens), 0)
+        behind = lax.broadcasted_iota(jnp.int32, (tokens, tokens), 1)
+        allowed = (place >= behind) & (docs_col[...] == docs_row[...])
+        scores = jnp.where(allowed, last_dims(query, key) * HEAD ** (-0.5), -1000000000.0)
+        weight = jnp.exp(scores - jnp.max(scores, axis=1, keepdims=True))
+        probs = weight * (1.0 / jnp.sum(weight, axis=1, keepdims=True))
+        grad_probs = last_dims(grad, value)
+        inside = jnp.sum(probs * grad_probs, axis=1, keepdims=True)
+        grad_scores = (probs * (grad_probs - inside)).astype(bf16)
+        grad_value = first_dims(probs.astype(bf16), grad)
+        grad_query = jnp.dot(grad_scores, key, preferred_element_type=f32) * HEAD ** (-0.5)
+        grad_key = first_dims(grad_scores, query) * HEAD ** (-0.5)
+
+        def turn_back(one):
+            return (
+                one * tables[0]
+                - pltpu.roll(one, HEAD - ROT // 2, 1) * tables[1]
+                - pltpu.roll(one, ROT // 2, 1) * tables[2]
+            )
+
+        projs[0, :, lane] = turn_back(grad_query).astype(bf16)
+        projs[1, :, lane] = turn_back(grad_key).astype(bf16)
+        projs[2, :, lane] = grad_value.astype(bf16)
+
+    tall = n_tile.shape[2]
+    tiles = width // tall
+    per = tall // feat
+
+    def tile_loads(t):
+        rows = pl.ds(pl.multiple_of(((me // per + t) % tiles) * tall, tall), tall)
+        spot = t % 2
+        return [
+            pltpu.make_async_copy(w_qkv.at[:, rows, :], qkv_tile.at[spot], tile_sem.at[spot, 0]),
+            pltpu.make_async_copy(w_up.at[rows, :], up_tile.at[spot], tile_sem.at[spot, 1]),
+            pltpu.make_async_copy(normed.at[:, rows, :], n_tile.at[spot], tile_sem.at[spot, 2]),
+        ]
+
+    def tile_turn(t):
+        spot = t % 2
+        for copy in tile_loads(t):
+            copy.wait()
+
+        @pl.when(t < tiles - 1)
+        def _():
+            for copy in tile_loads(t + 1):
+                copy.start()
+
+        base = ((me // per + t) % tiles) * per
+        rows = pl.ds(pl.multiple_of(base * feat, tall), tall)
+        for s in range(STREAMS):
+            if s < 3:
+                grad = last_dims(qkv_tile[spot, s], projs[s])
+            else:
+                grad = last_dims(up_tile[spot], grad_up[...])
+            grads[s, rows, :] = grad.astype(bf16)
+            products = jnp.sum(n_tile[spot, s].astype(f32) * grad, axis=0, keepdims=True)
+            inner[pl.ds(s, 1), :] = inner[pl.ds(s, 1), :] + products
+        for e in range(per):
+            sum_copy((base + e - me + n) % n).start()
 
     def span(peer, plane):
         return pl.ds(pl.multiple_of(peer * feat + plane * h, h), h)
@@ -788,26 +920,29 @@
         rows = span((me + q) % n, mp)
         spot = q % 2
         return [
-            pltpu.make_async_copy(grads.at[:, rows, :], d_buf.at[spot], load_sem.at[spot, 0]),
-            pltpu.make_async_copy(across_land.at[q], e_buf.at[spot], load_sem.at[spot, 1]),
+            pltpu.make_async_copy(across_land.at[q], e_buf.at[spot], load_sem.at[spot, 0]),
             pltpu.make_async_copy(
-                inputs.at[pl.ds(0, STREAMS), rows, :], x_buf.at[spot], load_sem.at[spot, 2]
+                inputs.at[pl.ds(0, STREAMS), rows, :], x_buf.at[spot], load_sem.at[spot, 1]
             ),
-            pltpu.make_async_copy(direct.at[rows, :], go_buf.at[spot], load_sem.at[spot, 3]),
-            pltpu.make_async_copy(smalls.at[rows, :], g_buf.at[spot], load_sem.at[spot, 4]),
-            pltpu.make_async_copy(little.at[rows, :], l_buf.at[spot], load_sem.at[spot, 5]),
+            pltpu.make_async_copy(direct.at[rows, :], go_buf.at[spot], load_sem.at[spot, 2]),
+            pltpu.make_async_copy(smalls.at[rows, :], g_buf.at[spot], load_sem.at[spot, 3]),
+            pltpu.make_async_copy(little.at[rows, :], l_buf.at[spot], load_sem.at[spot, 4]),
         ]
 
     def out_copy(q):
         rows = span((me + q) % n, mp)
         return pltpu.make_async_copy(output.at[rows, :], g_slots.at[q, STREAMS], out_sem.at[q])
 
-    def place(source, plane):
+    def place_of_source(source, plane):
         return feature_side.at[source, :, pl.ds(pl.multiple_of(plane * h, h), h), :]
 
     def stream_copy(q):
         return remote(
-            g_slots.at[q], place(me, mp), a_send.at[q], a_recv.at[q], {"dp": (me + q) % n}
+            g_slots.at[q],
+            place_of_source(me, mp),
+            a_send.at[q],
+            a_recv.at[q],
+            {"dp": (me + q) % n},
         )
 
     def little_copy(q):
@@ -815,16 +950,27 @@
             l_slots.at[q], l_land.at[q], l_send.at[q], l_recv.at[q], {"dp": (me + q) % n}
         )
 
-    def second_copy(q):
+    bits = second_land.shape[0]
+
+    def second_copy(b):
+        bit = (me // 2**b) % 2
         return remote(
-            second, second_land.at[me], w_send.at[q], w_recv.at[q], {"dp": (me + q) % n}
-        )
+            second_own,
+            second_land.at[b],
+            w_send.at[b],
+            w_recv.at[b],
+            {"dp": me + 2**b * (1 - 2 * bit)},
+        )
+
+    def second_turn(b):
+        second_copy(b).wait()
+        second_own[...] = second_own[...] + second_land[b]
 
     def home_copy():
-        return pltpu.make_async_copy(g_slots.at[0], place(me, mp), end_sem.at[0])
+        return pltpu.make_async_copy(g_slots.at[0], place_of_source(me, mp), end_sem.at[0])
 
     def across_copy(q, own=False):
-        there = place((me - q + n) % n, mp)
+        there = place_of_source((me - q + n) % n, mp)
         return remote(
             g_slots.at[0] if own else there, there, fy_send.at[q], fy_recv.at[q], across
         )
@@ -836,37 +982,35 @@
 
     def norm_backward(q):
         spot = q % 2
+        peer = (me + q) % n
         for copy in loads(q):
             copy.wait()
 
         @pl.loop(0, h // 16)
         def _(r):
             rows = pl.ds(pl.multiple_of(r * 16, 16), 16)
+            full = pl.ds(pl.multiple_of(peer * feat + mp * h + r * 16, 16), 16)
             tail = l_buf[spot, rows, :]
             lane = lax.broadcasted_iota(jnp.int32, tail.shape, 1)
             for s in range(STREAMS):
-                dy = d_buf[spot, s, rows, :].astype(f32) + e_buf[spot, s, rows, :].astype(f32)
-                level = scale[pl.ds(s, 1), :]
-                common = (inner[pl.ds(s, 1), :] + inner_land[pl.ds(s, 1), :]) * level
-                common = common * (1.0 / (n * feat))
-                unit = x_buf[spot, s, rows, :].astype(f32) * level
+                dy = grads[s, full, :].astype(f32) + e_buf[spot, s, rows, :].astype(f32)
+                scale = level[pl.ds(s, 1), :]
+                common = (inner[pl.ds(s, 1), :] + inner_land[pl.ds(s, 1), :]) * scale
+                common = common * (1.0 / width)
+                unit = x_buf[spot, s, rows, :].astype(f32) * scale
                 gain = g_buf[spot, rows, :].astype(f32)[:, MIXH + s : MIXH + s + 1]
-                grad = level * (gain * dy) - unit * common
+                grad = scale * (gain * dy) - unit * common
                 if s == STREAMS - 1:
                     grad = grad + go_buf[spot, rows, :]
                 g_slots[q, s, rows, :] = grad.astype(bf16)
                 gain_grad = jnp.sum(unit * dy, axis=1, keepdims=True)
                 tail = jnp.where(lane == MIXH + s, gain_grad, tail)
-            l_slots[q, rows, :] = tail
+            l_slots[q, rows, :] = tail.astype(bf16)
 
     def norm_turn(q):
         @pl.when(q < n - 1)
         def _():
             start_loads(q + 1)
-
-        @pl.when(q < n - AHEAD)
-        def _():
-            sum_copy(q + AHEAD).start()
 
         norm_backward(q)
         out_copy(q).wait()
@@ -903,11 +1047,7 @@
 
     def mix_copy(q):
         return remote(
-            m_slots.at[q],
-            m_land.at[q],
-            m_send.at[q],
-            m_recv.at[q],
-            {"dp": (me - q + n) % n},
+            m_slots.at[q], m_land.at[q], m_send.at[q], m_recv.at[q], {"dp": (me - q + n) % n}
         )
 
     def mix_backward(q):
@@ -920,7 +1060,8 @@
                     both = both[0:8] + both[8:16]
                     totals[j] = both if r == 0 else totals[j] + both
             for j in range(HIST):
-                m_slots[q, pl.ds(s * HIST + j, 1), :] = jnp.sum(totals[j], axis=0, keepdims=True)
+                m_wide[pl.ds(s * HIST + j, 1), :] = jnp.sum(totals[j], axis=0, keepdims=True)
+        m_slots[q] = m_wide[...].astype(bf16)
 
     def mix_turn(q):
         @pl.when(q < n - 1)
@@ -945,80 +1086,136 @@
         def _():
             mix_copy(q).start()
 
-    pieces = [(i, way) for i in range(count) for way in range(2)]
-
-    inner_copy().start()
-    for step in range(2):
-        for i, way in pieces:
-            core_copy(way, step, i).start()
-
-    @pl.loop(0, AHEAD)
-    def _(q):
-        sum_copy(q).start()
+    early = [(i, way) for i in (3, 2, 1) for way in range(2)]
+    late = [(0, way) for way in range(2)]
+
+    for way in range(2):
+        for step in range(3):
+            for copy in rows_load(way, step):
+                copy.start()
 
     @pl.loop(0, n)
     def _(q):
         out_copy(q).start()
 
-    second_land[me] = second[...]
-
-    @pl.loop(1, n)
-    def _(q):
-        second_copy(q).start()
-
-    for i, way in pieces:
+    second_own[...] = second[...]
+    for copy in tile_loads(0):
+        copy.start()
+    inner[...] = jnp.zeros_like(inner)
+    m_wide[...] = jnp.zeros_like(m_wide)
+    for way in range(2):
+        slots[0][way, 0] = jnp.zeros_like(slots[0][way, 0])
+        for copy in rows_load(way, 0) + rows_load(way, 1):
+            copy.wait()
+    for i, way in early:
+        give(way, 0, i)
+    for i, way in early:
         stage(way, 0, i)
-    for i, way in pieces:
-        staged(way, 0, i)
+    for i, way in early:
+        other_copy(way, 0, i).wait()
         add(way, 0, i, first=True)
         ring_copy(way, 0, i).start()
+        core_copy(way, 0, i).wait_send()
+        give(way, 1, i)
+    for i, way in early:
         stage(way, 1, i)
-    inner_copy().wait()
-    start_loads(0)
-
-    def ring_unit(step, i, way):
-        staged(way, step, i)
-        ring_copy(way, step - 1, i).wait_recv()
-        add(way, step, i)
-        ring_copy(way, step, i).start()
-        stage(way, step + 1, i)
-
-    def mates_ahead(step):
-        for i, way in pieces:
-            core_copy(way, step + 1, i).start()
-
+
+    @pl.loop(0, heads.shape[1])
+    def _(head):
+        attend_back(head)
+
+    for i, way in late:
+        give(way, 0, i)
+    for i, way in late:
+        stage(way, 0, i)
     hist_load(0).start()
+
+    opening = 2
 
     @pl.loop(1, ring - 1)
     def _(step):
-        mates_ahead(step)
-        for u, (i, way) in enumerate(pieces):
-            ring_unit(step, i, way)
+        for way in range(2):
+            for copy in rows_load(way, step + 1):
+                copy.wait()
+
+        for b in range(bits):
+
+            @pl.when(step == b + 1)
+            def _():
+                if b > 0:
+                    second_turn(b - 1)
+                second_copy(b).start()
+
+        @pl.when(step == opening)
+        def _():
+            inner_copy().start()
+            start_loads(0)
+            inner_copy().wait()
+
+        for u, (i, way) in enumerate(early + late):
+            if i == 0:
+
+                @pl.when(step > 1)
+                def _():
+                    if way == 0:
+                        for w in range(2):
+                            ring_copy(w, step - 2, i).wait_send()
+
+                other_copy(way, step - 1, i).wait()
+
+                @pl.when(step > 1)
+                def _():
+                    ring_copy(way, step - 2, i).wait_recv()
+
+                add(way, step - 1, i)
+                ring_copy(way, step - 1, i).start()
+                core_copy(way, step - 1, i).wait_send()
+                give(way, step, i)
+            else:
+                if way == 0:
+                    for w in range(2):
+                        ring_copy(w, step - 1, i).wait_send()
+                ring_unit(step, i, way)
             if u % 2 == 0:
 
-                @pl.when(step <= n // 4)
+                @pl.when((step >= opening) & (step < opening + n // 4))
                 def _():
-                    norm_turn(4 * (step - 1) + u // 2)
+                    norm_turn(4 * (step - opening) + u // 2)
             else:
 
-                @pl.when((step >= 2) & (step <= n // 4 + 1))
+                @pl.when((step > opening) & (step <= opening + n // 4))
                 def _():
-                    mix_turn(4 * (step - 2) + u // 2)
+                    mix_turn(4 * (step - opening - 1) + u // 2)
+
+            @pl.when(step == 1)
+            def _():
+                tile_turn(u)
+
+            if u > 0:
+                before, w = (early + late)[u - 1]
+                stage(w, step if before == 0 else step + 1, before)
+        stage(1, step, 0)
+
+        @pl.when(step < ring - 2)
+        def _():
+            for way in range(2):
+                for copy in rows_load(way, step + 2):
+                    copy.start()
 
     @pl.loop(1, n)
     def _(q):
         little_copy(q).wait_recv()
-        second_copy(q).wait_recv()
         mix_copy(q).wait_recv()
 
-    def sum_over(land, mine):
-        return lax.fori_loop(1, n, lambda q, total: total + land[q], mine)
+    def sum_over(land, own):
+        return lax.fori_loop(
+            1, n, lambda q, total: total + land[q].astype(f32), own.astype(f32)
+        )
 
     l_sum[...] = sum_over(l_land, l_slots[0])
     m_mine[...] = sum_over(m_land, m_slots[0])
-    second_sum[...] = lax.fori_loop(
-        1, n, lambda q, total: total + second_land[q], second_land[0]
-    )
+    second_turn(bits - 1)
+    second_sum[...] = second_own[...]
     here = pl.ds(pl.multiple_of(mp * h, h), h)
     little_home = pltpu.make_async_copy(l_sum, little_sum.at[here], end_sem.at[1])
     little_across = remote(l_sum, little_sum.at[here], end_sem.at[2], end_sem.at[3], across)
@@ -1027,14 +1224,21 @@
     little_across.start()
     mix_across.start()
 
-    for way in range(2):
-        for i in range(count):
-            staged(way, ring - 1, i)
-            ring_copy(way, ring - 2, i).wait_recv()
-            if way == 1:
-                final_copy(0, i).wait()
-            add(way, ring - 1, i, last=True)
-            final_copy(way, i).start()
+    for i, way in late:
+        if way == 0:
+            for w in range(2):
+                ring_copy(w, ring - 3, i).wait_send()
+        ring_unit(ring - 2, i, way)
+    for i, way in late:
+        stage(way, ring - 1, i)
+
+    for i, way in early + late:
+        other_copy(way, ring - 1, i).wait()
+        ring_copy(way, ring - 2, i).wait_recv()
+        if way == 1:
+            final_copy(0, i).wait()
+        add(way, ring - 1, i, last=True)
+        final_copy(way, i).start()
 
     mix_across.wait()
     mix_sum[...] = m_mine[...] + m_other[...]
@@ -1047,7 +1251,6 @@
     def _(q):
         stream_copy(q).wait_send()
         little_copy(q).wait_send()
-        second_copy(q).wait_send()
         mix_copy(q).wait_send()
 
     @pl.loop(0, n)
@@ -1055,71 +1258,100 @@
         sum_copy(q).wait_send()
         across_copy(q).wait()
 
-    @pl.loop(0, ring - 1)
-    def _(step):
-        for i, way in pieces:
-            ring_copy(way, step, i).wait_send()
-
-    @pl.loop(0, ring)
-    def _(step):
-        for i, way in pieces:
-            core_copy(way, step, i).wait_send()
+    for i, way in early + late:
+        ring_copy(way, ring - 2, i).wait_send()
+        core_copy(way, ring - 1, i).wait_send()
 
 
 def backward_exchange(
-    n, grads, inner, scale, inputs, direct, output, smalls, little, second, history, mixes, parts
+    n,
+    normed,
+    grad_branch,
+    hidden,
+    attn,
+    grad_up,
+    heads,
+    grad_attended,
+    w_qkv,
+    w_up,
+    tables,
+    docs,
+    level,
+    inputs,
+    direct,
+    output,
+    smalls,
+    little,
+    second,
+    history,
+    mixes,
+    shards,
 ):
-    count, ring = len(parts), n // 2
-    feat, tokens = history.shape[1], grads.shape[2]
-    h = feat // 2
+    count, ring = len(shards), n // 2
+    feat, tokens = history.shape[1], level.shape[1]
+    h, width = feat // 2, n * feat
+    units = grad_up.shape[1]
     hbm = pl.BlockSpec(memory_space=pl.ANY)
     vmem = pl.BlockSpec(memory_space=pltpu.VMEM)
 
     def cut(s, rows):
         return s.shape[:-2] + (rows, s.shape[-1])
 
-    half = parts[0].shape[-2] // n // 2
+    half = shards[0].shape[-2] // 2
+    tall = 256
+    columns = attn.shape[1]
+    places = [hbm, hbm, vmem, vmem, vmem, vmem, vmem, hbm, hbm, vmem, vmem, vmem, vmem]
+    places += [hbm, hbm, hbm, hbm, hbm, vmem, hbm, hbm]
     found = pl.pallas_call(
         functools.partial(backward_kernel, n, count),
         out_shape=[
             jax.ShapeDtypeStruct((n, STREAMS, h, tokens), bf16),
             jax.ShapeDtypeStruct((n, STREAMS + 1, feat, tokens), bf16),
-            jax.ShapeDtypeStruct((STREAMS * HIST, tokens), f32),
+            jax.ShapeDtypeStruct((MIXED, tokens), f32),
             jax.ShapeDtypeStruct((feat, WIDE), f32),
             jax.ShapeDtypeStruct(second.shape, f32),
         ]
-        + [jax.ShapeDtypeStruct(cut(s, 2 * half), f32) for s in parts]
-        + [jax.ShapeDtypeStruct((2, ring) + cut(s, half), bf16) for s in parts],
-        in_specs=[hbm, vmem, vmem, hbm, hbm, hbm, hbm, hbm, vmem, hbm, hbm] + [hbm] * count,
+        + [jax.ShapeDtypeStruct(s.shape, f32) for s in shards]
+        + [jax.ShapeDtypeStruct((2, ring) + cut(s, half), bf16) for s in shards],
+        in_specs=places,
         out_specs=[hbm, hbm, vmem, hbm, vmem] + [hbm] * (2 * count),
-        scratch_shapes=[pltpu.VMEM((2, ring) + cut(s, half), bf16) for s in parts]
-        + [pltpu.VMEM((2, 2) + cut(s, half), bf16) for s in parts]
-        + [pltpu.VMEM((2, 2) + cut(s, half), bf16) for s in parts]
-        + [pltpu.VMEM(cut(s, half), f32) for s in parts]
+        scratch_shapes=[pltpu.VMEM((2, 4) + cut(s, half), bf16) for s in shards]
+        + [pltpu.VMEM((2,) + cut(s, half), bf16) for s in shards]
+        + [pltpu.VMEM((2,) + cut(s, half), bf16) for s in shards]
+        + [pltpu.VMEM(cut(s, half), f32) for s in shards]
         + [
-            pltpu.VMEM(inner.shape, f32),
-            pltpu.VMEM((2, STREAMS, h, tokens), bf16),
+            pltpu.VMEM((2, 3, 2, STREAMS + 1, half, tokens), bf16),
+            pltpu.VMEM((3, tokens, columns), bf16),
+            pltpu.VMEM((STREAMS, width, tokens), bf16),
+            pltpu.VMEM((2, 3, tall, columns), bf16),
+            pltpu.VMEM((2, tall, units), bf16),
+            pltpu.VMEM((2, STREAMS, tall, tokens), bf16),
+            pltpu.VMEM((8, tokens), f32),
+            pltpu.VMEM((8, tokens), f32),
             pltpu.VMEM((2, STREAMS, h, tokens), bf16),
             pltpu.VMEM((2, STREAMS, h, tokens), bf16),
             pltpu.VMEM((2, h, tokens), f32),
             pltpu.VMEM((2, h, WIDE), bf16),
             pltpu.VMEM((2, h, WIDE), f32),
             pltpu.VMEM((n, STREAMS + 1, h, tokens), bf16),
-            pltpu.VMEM((n, h, WIDE), f32),
-            pltpu.VMEM((n, h, WIDE), f32),
-            pltpu.VMEM((n,) + second.shape, f32),
+            pltpu.VMEM((n, h, WIDE), bf16),
+            pltpu.VMEM((n, h, WIDE), bf16),
+            pltpu.VMEM((n.bit_length() - 1,) + second.shape, f32),
+            pltpu.VMEM(second.shape, f32),
             pltpu.VMEM((STREAMS, h, tokens), bf16),
             pltpu.VMEM((2, HIST, h, tokens), bf16),
-            pltpu.VMEM((n, STREAMS * HIST, tokens), f32),
-            pltpu.VMEM((n, STREAMS * HIST, tokens), f32),
-            pltpu.VMEM((STREAMS * HIST, tokens), f32),
-            pltpu.VMEM((STREAMS * HIST, tokens), f32),
+            pltpu.VMEM((MIXED, tokens), f32),
+            pltpu.VMEM((n, MIXED, tokens), bf16),
+            pltpu.VMEM((n, MIXED, tokens), bf16),
+            pltpu.VMEM((MIXED, tokens), f32),
+            pltpu.VMEM((MIXED, tokens), f32),
             pltpu.VMEM((h, WIDE), f32),
-            DMA((2, 6)),
+            DMA((2, 3, 4)),
+            DMA((2, 3)),
+            DMA((2, 5)),
             DMA((n,)),
             DMA((2, 2)),
-            DMA((2, 2, count)),
-            DMA((2, 2, count)),
+            DMA((2, count)),
             DMA((count,)),
             DMA((n,)),
             DMA((n,)),
@@ -1130,9 +1362,31 @@
         + [DMA((2, ring - 1, count)) for _ in range(2)]
         + [DMA((2, ring, count)) for _ in range(2)],
         compiler_params=pltpu.CompilerParams(
-            collective_id=1, has_side_effects=True, vmem_limit_bytes=60 * 1024 * 1024
+            collective_id=1, has_side_effects=True, vmem_limit_bytes=62 * 1024 * 1024
         ),
-    )(grads, inner, scale, inputs, direct, output, smalls, little, second, history, mixes, *parts)
+    )(
+        normed,
+        grad_branch,
+        hidden,
+        attn,
+        grad_up,
+        heads,
+        grad_attended,
+        w_qkv,
+        w_up,
+        tables,
+        docs,
+        docs.T,
+        level,
+        inputs,
+        direct,
+        output,
+        smalls,
+        little,
+        second,
+        history,
+        mixes,
+    )
     return found[1], found[2], found[3], found[4], found[5 : 5 + count]
 
 
@@ -1171,12 +1425,6 @@
         ],
         compiler_params=pltpu.CompilerParams(vmem_limit_bytes=32 * 1024 * 1024),
     )(feature_side, mixes)
-
-
-def rotary(heads_in, tables):
-    ahead = jnp.roll(heads_in, -(ROT // 2), axis=-1)
-    behind = jnp.roll(heads_in, ROT // 2, axis=-1)
-    return heads_in * tables[0] + ahead * tables[1] + behind * tables[2]
 
 
 def angle_tables(length):
@@ -1227,25 +1475,12 @@
         jnp.concatenate([w_mix1, gains.T], axis=1), ((0, 0), (0, WIDE - MIXH - gains.shape[0]))
     )
     tables = angle_tables(tokens_here)
-    kept, (full_qkv, full_o, full_up, full_down) = forward_exchange(
-        n, history, cot_out, mix_in.T, small, tables, doc_ids, (w_qkv, w_out, w_up, w_down)
+    kept, (full_qkv, full_o, full_up, full_down, smalls) = forward_exchange(
+        n, history, cot_out, mix_in.T, tables, doc_ids, (w_qkv, w_out, w_up, w_down, small)
     )
-    inputs, mixes, smalls, normed, level, qkv_heads, attn_cat, up_pre, hidden, out_full = kept
-    queries, key_heads, values = qkv_heads[0], qkv_heads[1], qkv_heads[2]
-    heads_here = full_qkv.shape[2] // HEAD
-    width_here = heads_here * HEAD
+    inputs, mixes, normed, level, qkv_heads, attn_cat, slope, hidden, out_full = kept
     full_m1 = smalls[:, :MIXH]
     gain_f = smalls[:, MIXH : MIXH + STREAMS + 1].astype(f32)
-    scale_qk = HEAD ** (-0.5)
-    positions = jnp.arange(tokens_here)
-    doc_row = doc_ids[0]
-    allowed = (positions[:, None] >= positions[None, :]) & (doc_row[:, None] == doc_row[None, :])
-    scores = product("hqd,hkd->hqk", queries, key_heads) * scale_qk
-    scores = jnp.where(allowed[None], scores, -1000000000.0)
-    row_max = jnp.max(scores, axis=-1, keepdims=True)
-    log_total = row_max + jnp.log(jnp.sum(jnp.exp(scores - row_max), axis=-1, keepdims=True))
-    attn_probs = jnp.exp(scores - log_total)
-    probs_low = attn_probs.astype(bf16)
     out_low = out_full.astype(bf16)
     mix_level = lax.rsqrt(jnp.mean(out_full * out_full, axis=0) + EPS)
     mix_unit = out_full * mix_level[None, :]
@@ -1271,42 +1506,9 @@
         mix_gain * grad_mix_normed - mix_unit * mix_inner[None, :]
     )
     grad_branch = grad_out_full.astype(bf16)
-    grad_o_part = product("ot,ti->oi", grad_branch, attn_cat).astype(bf16)
-    grad_down_part = product("ot,ti->oi", grad_branch, hidden).astype(bf16)
     grad_attended = product("ot,oi->ti", grad_branch, full_o).astype(bf16)
-    grad_attended = grad_attended.reshape(tokens_here, heads_here, HEAD).transpose(1, 0, 2)
     grad_hidden = product("ot,oi->ti", grad_branch, full_down)
-    grad_up_pre = jax.vjp(gelu_exact, up_pre)[1](grad_hidden)[0].astype(bf16)
-    grad_up_part = product("dt,tn->dn", normed[3], grad_up_pre).astype(bf16)
-    grad_normed_ff = product("dn,tn->dt", full_up, grad_up_pre)
-    grad_probs = product("hqd,hkd->hqk", grad_attended, values)
-    grad_values = product("hqk,hqd->hkd", probs_low, grad_attended)
-    inner = jnp.sum(attn_probs * grad_probs, axis=-1, keepdims=True)
-    grad_scores = (attn_probs * (grad_probs - inner)).astype(bf16)
-    grad_q_rot = product("hqk,hkd->hqd", grad_scores, key_heads) * scale_qk
-    grad_k_rot = product("hqk,hqd->hkd", grad_scores, queries) * scale_qk
-
-    back_tables = (tables[0], -tables[1], -tables[2])
-
-    def flat(heads):
-        return heads.astype(bf16).transpose(1, 0, 2).reshape(tokens_here, width_here)
-
-    grad_projs = (
-        flat(rotary(grad_q_rot, back_tables)),
-        flat(rotary(grad_k_rot, back_tables)),
-        flat(grad_values),
-    )
-    grad_qkv_part = jnp.stack(
-        [product("dt,tn->dn", normed[s], grad_projs[s]).astype(bf16) for s in range(3)]
-    )
-    grad_normed = jnp.stack(
-        [product("dn,tn->dt", full_qkv[s], grad_projs[s]).astype(bf16) for s in range(3)]
-        + [grad_normed_ff.astype(bf16)]
-    )
-    norm_inner = jnp.sum(normed.astype(f32) * grad_normed.astype(f32), axis=1)
-
-    def eight(rows):
-        return jnp.pad(rows, ((0, 8 - rows.shape[0]), (0, 0)))
+    grad_up_pre = (slope * grad_hidden).astype(bf16)
 
     little = jnp.concatenate(
         [
@@ -1320,8 +1522,17 @@
     second = jnp.pad(grad_mix2_part, ((0, 0), (0, WIDE - MIXH)))
     feature_side, mix_sum, little_sum, second_sum, sums = backward_exchange(
         n,
-        grad_normed,
-        eight(norm_inner),
+        normed,
+        grad_branch,
+        hidden,
+        attn_cat,
+        grad_up_pre,
+        qkv_heads,
+        grad_attended,
+        full_qkv,
+        full_up,
+        tables,
+        doc_ids,
         level,
         inputs,
         grad_out_full,
@@ -1331,7 +1542,7 @@
         second,
         history,
         mixes,
-        (grad_qkv_part, grad_o_part, grad_up_part, grad_down_part),
+        (w_qkv, w_out, w_up, w_down),
     )
     grad_history, block_out = history_gradient(feature_side, mixes)
     grad_qkv, grad_w_out, grad_w_up, grad_w_down = sums
@@ -1339,7 +1550,7 @@
         block_out,
         mix_out,
         grad_history,
-        mix_sum.T,
+        mix_sum[: STREAMS * HIST].T,
         grad_qkv,
         grad_w_out,
         grad_w_up,

time: 982 us -> 888 us (0.904)
  matrix products: 106 us -> 23.2 us
  other arithmetic: 26.9 us -> 13.5 us
  Pallas kernels: 814 us -> 824 us
    dot_general x23 -> x8, matrix products: 106 us -> 23.2 us  [product(): return jnp.einsum(spec, left, right, preferred_element_type=f32)]
    pallas_call x1, Pallas kernels: 373 us -> 408 us  [backward_exchange(): pl.pallas_call(functools.partial(backward_kernel, n, count), out_shape=[j...]
    pallas_call x1, Pallas kernels: 429 us -> 404 us  [forward_exchange(): pl.pallas_call(functools.partial(forward_kernel, n, count), out_shape=[ja...]
where the time goes in v4:
time: 888 us; the launch traced here: 879 us
  Pallas kernels  824 us (93%)
  matrix products  23.2 us (3%)
  local copies, waits for them, and re-layouts  16.8 us (2%)
  other arithmetic  13.5 us (2%)
    pallas_call x1, Pallas kernels, backward_exchange(): pl.pallas_call(functools.partial(backward_kernel, n, count), out_shape=[j...  408 us
    pallas_call x1, Pallas kernels, forward_exchange(): pl.pallas_call(functools.partial(forward_kernel, n, count), out_shape=[ja...  404 us
    dot_general x8, matrix products, product(): return jnp.einsum(spec, left, right, preferred_element_type=f32)  23.2 us

profile of v4, /device:TPU:21, one launch (start us, length us, event | category | flops | bytes accessed | tf_op | source)
XLA Modules:
  0.0 878.8 jit_solution(17124283546418888667)
XLA Ops:
  0.6 0.0 copy-start
  0.7 0.0 copy-start.13
  0.7 0.8 multiply_cosine_fusion
  1.5 0.1 pad.24.clone
  1.6 0.1 pad.27.clone
  1.7 0.2 maximum_bitcast_fusion.1
  1.9 0.9 pad_maximum_fusion.refs_3_.refs_9_
  2.8 0.8 copy.54.refs_5_.refs_11_
  3.6 0.0 copy-done.16
  3.6 0.1 copy.53
  3.8 0.6 pad.8.refs_10_
  4.4 404.1 %shard_map.221 = (bf16[5,2048,384]{2,1,0:T(8,128)(2,1)}, f32[16,36,384]{2,1,0:T(8,128)}, bf16[4,2048,384]{2,1,0:T(8,128)(2,1)}, f32[8,384]{1,0:T(8,128)}, bf16[3...) custom-call(bf16[9,128,6144]{2,1,0:T(8,128)(2,1)} %refs_19_.1, ...), custom_call_target="tpu_custom_call" | custom-call | tf_op jit(solution)/shard_map/pallas_call | solution.py:584
  408.6 1.6 convert_reduce_fusion
  410.1 2.2 multiply_reduce_fusion.2
  412.4 0.4 multiply_convert_fusion.1
  412.7 0.6 copy-done.6
  413.4 0.5 multiply_convert_fusion.2
  413.9 0.2 copy-done.14
  414.1 0.1 add_convert_fusion
  414.2 1.5 fusion.15
  415.7 2.7 multiply_reduce_fusion
  418.5 1.3 copy.56
  419.8 0.1 pad.11.clone
  419.9 0.1 pad.13.clone
  420.0 2.9 maximum_maximum_fusion.refs_17_
  422.8 0.1 select_reduce_fusion
  422.9 4.5 fusion.13
  427.5 2.7 convolution_convert_fusion.refs_6_
  430.2 14.7 %multiply_convert_fusion.refs_4_ = bf16[384,4096]{1,0:T(8,128)(2,1)} fusion(f32[384,4096]{1,0:T(8,128)} %get-tuple-element.41, bf16[2048,384]{1,0:T(8,128)(2,1)S(1)} %get-tuple-element.118.refs_1_, bf16[2048,4096]{1,0:T(8,128)(2,1)} %get-tuple-element.42), kind=kOutput, calls=%fused_computation | convolution fusion | flops 6445596672 | bytes 27787264 | tf_op jit(solution)/shard_map/ot,oi->ti/dot_general | solution.py:1452
  444.8 0.1 fusion.16
  445.0 0.6 pad.9.refs_18_
  445.6 408.0 %shard_map.222 = (bf16[16,4,64,384]{3,2,1,0:T(8,128)(2,1)}, bf16[16,5,128,384]{3,2,1,0:T(8,128)(2,1)}, f32[48,384]{1,0:T(8,128)}, f32[128,128]{1,0:T(8,128)}, f3...) custom-call(bf16[4,2048,384]{2,1,0:T(8,128)(2,1)} %get-tuple-element, ...), custom_call_target="tpu_custom_call" | custom-call | tf_op jit(solution)/shard_map/pallas_call | solution.py:1305
  853.6 0.0 copy-done.3
  853.6 0.0 copy-start.2
  853.6 3.2 copy-done.2
  856.8 12.1 %shard_map.223 = (bf16[9,128,6144]{2,1,0:T(8,128)(2,1)}, bf16[128,6144]{1,0:T(8,128)(2,1)}) custom-call(bf16[16,5,128,384]{3,2,1,0:T(8,128)(2,1)S(1)} %copy-done.2, f32[16,36,384]{2,1,0:T(8,128)S(1)} %copy-done.3), custom_call_target="tpu_custom_call" | custom-call | tf_op jit(solution)/shard_map/pallas_call | solution.py:1411
  868.9 0.0 copy-done.10
  868.9 0.1 slice_bitcast_fusion
  869.0 0.7 copy.59
  869.7 0.0 copy-done.11
  869.7 0.6 slice_bitcast_fusion.1
  870.3 0.7 copy.58
  871.0 0.8 fusion.17
  871.8 2.7 copy.66
  874.5 0.8 copy.67
  875.3 1.3 copy.68
  876.7 1.3 copy.69
  878.0 0.6 copy.70
  (41 shorter events, 0.1 us)
Async XLA Ops:
  0.6 413.3 %copy-start = (bf16[384,40]{0,1:T(8,128)(2,1)S(1)}, bf16[384,40]{0,1:T(8,128)(2,1)}, u32[]{:S(2)}) copy-start(bf16[384,40]{0,1:T(8,128)(2,1)} %param.27) | copy-start | bytes 92164
  0.7 2.1 copy-start.13
  0.7 3.0 copy-start.16
  0.7 2.9 copy-start.15
  408.5 3.8 copy-start.4
  412.3 1.0 copy-start.6
  413.4 0.7 copy-start.14
  418.4 4.4 copy-start.17
  418.4 4.4 copy-start.18
  422.9 4.5 copy-start.19
  427.5 2.7 copy-start.5
  445.6 408.0 %copy-start.3 = (f32[16,36,384]{2,1,0:T(8,128)S(1)}, f32[16,36,384]{2,1,0:T(8,128)}, u32[]{:S(2)}) copy-start(f32[16,36,384]{2,1,0:T(8,128)} %get-tuple-element.48.refs_20_.mixes) | copy-start | bytes 2654212
  853.6 3.2 copy-start.2
  856.8 12.1 %copy-start.10 = (f32[128,128]{1,0:T(8,128)S(1)}, f32[128,128]{1,0:T(8,128)}, u32[]{:S(2)}) copy-start(f32[128,128]{1,0:T(8,128)} %get-tuple-element.57) | copy-start | bytes 196612
  856.8 12.8 %copy-start.11 = (f32[48,384]{1,0:T(8,128)S(1)}, f32[48,384]{1,0:T(8,128)}, u32[]{:S(2)}) copy-start(f32[48,384]{1,0:T(8,128)} %get-tuple-element.52) | copy-start | bytes 221188
  868.9 5.6 copy-start.9
  868.9 6.4 copy-start.8
  874.5 2.1 copy-start.7
  875.3 3.3 copy-start.1
  876.7 1.3 copy-start.12

commit v5 on v4

--- a/solution.py
+++ b/solution.py
@@ -376,19 +376,48 @@
             hidden[:, pl.ds(pl.multiple_of(c * chunk + k * 256, 256), 256)] = low
         slope_copy(c).start()
 
-    deep = down_buf.shape[1]
+    def blocks(c):
+        starts = []
+        for way in range(2):
+            shard = owner(-c if way == 0 else c)
+            for which in range(2):
+                row = (shard + which * (where.mate - me)) * size + way * half
+                starts.append(pl.multiple_of(row, half))
+        return starts
 
     def row_tiles(c):
-        rows = pl.ds(c * deep, deep)
-        return [
-            pltpu.make_async_copy(w_down.at[rows, :], down_buf.at[c % 2], row_sem.at[c % 2, 0]),
-            pltpu.make_async_copy(w_out.at[rows, :], out_buf.at[c % 2], row_sem.at[c % 2, 1]),
-        ]
+        copies = []
+        for b, start in enumerate(blocks(c)):
+            rows, there = pl.ds(start, half), pl.ds(b * half, half)
+            copies.append(
+                pltpu.make_async_copy(
+                    w_down.at[rows, :], down_buf.at[c % 2, there], row_sem.at[c % 2, b]
+                )
+            )
+            copies.append(
+                pltpu.make_async_copy(
+                    w_out.at[rows, :], out_buf.at[c % 2, there], row_sem.at[c % 2, 4 + b]
+                )
+            )
+        return copies
+
+    def rows_begin(c):
+        for p in of(3):
+            for way in range(2):
+                core_copy(way, c, p).wait_recv()
+        for copy in row_tiles(c):
+            copy.start()
+
+    def rows_product(c):
+        for copy in row_tiles(c):
+            copy.wait()
+        part = last_dims(down_buf[c % 2], hidden[...]) + last_dims(out_buf[c % 2], attn[...])
+        branch[c] = part.astype(bf16)
+        swap_copy(c).start()
 
     def swap_copy(c):
-        rows = pl.ds(c * deep, deep)
         return remote(
-            branch.at[rows], branch_land.at[rows], swap_send.at[c], swap_recv.at[c], across
+            branch.at[c], branch_land.at[c], swap_send.at[c], swap_recv.at[c], across
         )
 
     def keep(k):
@@ -426,7 +455,7 @@
         cot_copy(q).start()
 
     hist_copy(0).start()
-    ring_begin(of(0, 1, 4))
+    ring_begin(of(2, 4))
     mixes[me] = mix[...]
     hist_copy(0).wait()
     hist_copy(1).start()
@@ -444,27 +473,27 @@
             core_copy(way, 0, p, True).start()
     for i in range(count):
         shard_copy(i).start()
-    ring_begin(of(2))
+    ring_begin(of(0, 1))
 
     @pl.loop(1, ring - 1)
     def _(step):
-        ring_step(step, of(0, 1, 4))
+        ring_step(step, of(2, 4))
         for u in range(2):
             stream_turn(2 + 2 * step + u)
         for u in range(2):
             forward_turn(2 * step - 1 + u)
 
-    ring_end(of(0, 1, 4))
+    ring_end(of(2, 4))
     ring_begin(of(3))
     pairs = heads.shape[1] // 2
     last = ring - 2
-    early = 3
+    early = 2
 
     def streams_here():
-        ring_complete(0, 1, 4)
+        ring_complete(2, 4)
         gains_copy = pltpu.make_async_copy(all_small, smalls, local_sem.at[count])
         gains_copy.start()
-        for copy in head_tiles(0, 0):
+        for copy in up_tile(0, 0):
             copy.start()
         own_copy().wait()
 
@@ -479,7 +508,7 @@
 
     @pl.loop(1, ring - 1)
     def _(step):
-        ring_step(step, of(2))
+        ring_step(step, of(0, 1))
 
         @pl.when(step == 1)
         def _():
@@ -491,61 +520,75 @@
         def _():
             ring_step(step - (last - early), of(3))
 
-        @pl.when(step == last - pairs)
+        @pl.when(step == last - ups // 2)
         def _():
             streams_here()
 
-        @pl.when(step > last - pairs)
-        def _():
-            attend(step - (last - pairs) - 1)
-
-    keep(2).start()
-    keep(3).start()
-    ring_end(of(2))
-    ring_complete(2)
-    for copy in up_tile(0, 0):
+        @pl.when(step > last - ups // 2)
+        def _():
+            for u in range(2):
+                feed(2 * (step - (last - ups // 2) - 1) + u, u)
+
+    keep(4).start()
+    ring_end(of(0, 1))
+    ring_complete(0, 1)
+    shard_copy(3).wait()
+    for copy in head_tiles(0, 0):
         copy.start()
 
     @pl.loop(early + 1, ring - 1)
     def _(step):
         ring_step(step, of(3))
 
-        @pl.when(2 * (step - early) <= ups - 2)
+        @pl.when(step <= early + pairs // 2)
         def _():
             for u in range(2):
-                feed(2 * (step - early - 1) + u, u)
-
-    for c in range(ups - 2, ups):
-        feed(c, c % 2)
-    keep(4).start()
+                attend(2 * (step - early - 1) + u)
+
+        @pl.when(step == early + pairs // 2)
+        def _():
+            for c in range(2):
+                rows_begin(c)
+
+        for ahead in range(1, 3):
+
+            @pl.when(step == early + pairs // 2 + ahead)
+            def _():
+                for u in range(2):
+                    c = 2 * (ahead - 1) + u
+                    rows_product(c)
+                    rows_begin(c + 2)
+
+    keep(2).start()
+    keep(3).start()
+
+    @pl.loop(4, ring - 3)
+    def _(c):
+        rows_product(c)
+        rows_begin(c + 2)
+
+    rows_product(ring - 3)
     ring_end(of(3))
-    ring_complete(3)
-    rounds = width // deep
-    for copy in row_tiles(0):
-        copy.start()
-    for c in range(rounds):
-        if c < rounds - 1:
-            for copy in row_tiles(c + 1):
-                copy.start()
-        for copy in row_tiles(c):
-            copy.wait()
-        part = last_dims(down_buf[c % 2], hidden[...]) + last_dims(out_buf[c % 2], attn[...])
-        branch[pl.ds(c * deep, deep)] = part.astype(bf16)
-        swap_copy(c).start()
-    for c in range(rounds):
+    rows_begin(ring - 1)
+    rows_product(ring - 2)
+    rows_product(ring - 1)
+
+    @pl.loop(0, ring)
+    def _(c):
         swap_copy(c).wait_recv()
-
-        @pl.loop(0, deep // 32)
-        def _(r):
-            rows = pl.ds(pl.multiple_of(c * deep + r * 32, 32), 32)
-            both = branch[rows, :].astype(f32) + branch_land[rows, :].astype(f32)
+        for b, start in enumerate(blocks(c)):
+            both = branch[c, b * half : (b + 1) * half].astype(f32)
+            both = both + branch_land[c, b * half : (b + 1) * half].astype(f32)
+            rows = pl.ds(start, half)
             total[rows, :] = streams[STREAMS - 1, rows, :].astype(f32) + both
 
     for c in range(ups - 2, ups):
         slope_copy(c).wait()
     for k in range(5):
         keep(k).wait()
-    for c in range(rounds):
+
+    @pl.loop(0, ring)
+    def _(c):
         swap_copy(c).wait_send()
 
     @pl.loop(1, n)
@@ -578,8 +621,7 @@
     vmem = pl.BlockSpec(memory_space=pltpu.VMEM)
     columns, units = shards[0].shape[2], shards[2].shape[1]
     across = columns // HEAD
-    deep = 512
-    rounds = width // deep
+    deep = 2 * shards[0].shape[1]
     travel = len(cuts_of(shards, CUTS))
     found = pl.pallas_call(
         functools.partial(forward_kernel, n, count),
@@ -612,8 +654,8 @@
             pltpu.VMEM((tokens, units), bf16),
             pltpu.VMEM((2, deep, units), bf16),
             pltpu.VMEM((2, deep, columns), bf16),
-            pltpu.VMEM((width, tokens), bf16),
-            pltpu.VMEM((width, tokens), bf16),
+            pltpu.VMEM((ring, deep, tokens), bf16),
+            pltpu.VMEM((ring, deep, tokens), bf16),
             pltpu.VMEM((width, WIDE), bf16),
             DMA((2,)),
             DMA((n,)),
@@ -622,9 +664,9 @@
             DMA((5,)),
             DMA((6,)),
             DMA((2,)),
-            DMA((2, 2)),
-            DMA((rounds,)),
-            DMA((rounds,)),
+            DMA((2, 8)),
+            DMA((ring,)),
+            DMA((ring,)),
         ]
         + [DMA((n,)) for _ in range(6)]
         + [DMA((2, ring - 1, travel)) for _ in range(2)]
@@ -694,13 +736,14 @@
         rows_sem,
         tile_sem,
         load_sem,
-        out_sem,
         back_sem,
         other_sem,
         final_sem,
         y_send,
         y_recv,
         p_sem,
+        o_send,
+        o_recv,
         a_send,
         a_recv,
         l_send,
@@ -929,20 +972,29 @@
             pltpu.make_async_copy(little.at[rows, :], l_buf.at[spot], load_sem.at[spot, 4]),
         ]
 
-    def out_copy(q):
-        rows = span((me + q) % n, mp)
-        return pltpu.make_async_copy(output.at[rows, :], g_slots.at[q, STREAMS], out_sem.at[q])
-
     def place_of_source(source, plane):
         return feature_side.at[source, :, pl.ds(pl.multiple_of(plane * h, h), h), :]
 
+    def grads_of_source(source, plane):
+        rows = pl.ds(pl.multiple_of(plane * h, h), h)
+        return feature_side.at[source, pl.ds(0, STREAMS), rows, :]
+
+    def output_of_source(source, plane):
+        return feature_side.at[source, STREAMS, pl.ds(pl.multiple_of(plane * h, h), h), :]
+
+    def out_copy(q):
+        peer = (me + q) % n
+        return remote(
+            output.at[span(peer, mp), :],
+            output_of_source(me, mp),
+            o_send.at[q],
+            o_recv.at[q],
+            {"dp": peer},
+        )
+
     def stream_copy(q):
         return remote(
-            g_slots.at[q],
-            place_of_source(me, mp),
-            a_send.at[q],
-            a_recv.at[q],
-            {"dp": (me + q) % n},
+            g_slots.at[q], grads_of_source(me, mp), a_send.at[q], a_recv.at[q], {"dp": (me + q) % n}
         )
 
     def little_copy(q):
@@ -967,13 +1019,16 @@
         second_own[...] = second_own[...] + second_land[b]
 
     def home_copy():
-        return pltpu.make_async_copy(g_slots.at[0], place_of_source(me, mp), end_sem.at[0])
-
-    def across_copy(q, own=False):
+        return pltpu.make_async_copy(g_slots.at[0], grads_of_source(me, mp), end_sem.at[0])
+
+    def home_output():
+        return pltpu.make_async_copy(
+            output.at[span(me, mp), :], output_of_source(me, mp), end_sem.at[6]
+        )
+
+    def across_copy(q):
         there = place_of_source((me - q + n) % n, mp)
-        return remote(
-            g_slots.at[0] if own else there, there, fy_send.at[q], fy_recv.at[q], across
-        )
+        return remote(there, there, fy_send.at[q], fy_recv.at[q], across)
 
     def start_loads(q):
         sum_copy(q).wait_recv()
@@ -1013,12 +1068,10 @@
             start_loads(q + 1)
 
         norm_backward(q)
-        out_copy(q).wait()
 
         @pl.when(q == 0)
         def _():
             home_copy().start()
-            across_copy(q, True).start()
 
         @pl.when(q > 0)
         def _():
@@ -1071,12 +1124,14 @@
         @pl.when(q == 0)
         def _():
             home_copy().wait()
+            home_output().wait()
 
         @pl.when(q > 0)
         def _():
             stream_copy(q).wait_recv()
-            across_copy(q).start()
-
+            out_copy(q).wait_recv()
+
+        across_copy(q).start()
         grad_load(q).start()
         grad_load(q).wait()
         hist_load(q).wait()
@@ -1094,7 +1149,9 @@
             for copy in rows_load(way, step):
                 copy.start()
 
-    @pl.loop(0, n)
+    home_output().start()
+
+    @pl.loop(1, n)
     def _(q):
         out_copy(q).start()
 
@@ -1107,14 +1164,16 @@
         slots[0][way, 0] = jnp.zeros_like(slots[0][way, 0])
         for copy in rows_load(way, 0) + rows_load(way, 1):
             copy.wait()
-    for i, way in early:
+    for i, way in early[:2]:
         give(way, 0, i)
-    for i, way in early:
+    for u, (i, way) in enumerate(early):
+        if u + 2 < len(early):
+            give(early[u + 2][1], 0, early[u + 2][0])
         stage(way, 0, i)
-    for i, way in early:
         other_copy(way, 0, i).wait()
         add(way, 0, i, first=True)
         ring_copy(way, 0, i).start()
+    for i, way in early:
         core_copy(way, 0, i).wait_send()
         give(way, 1, i)
     for i, way in early:
@@ -1250,6 +1309,7 @@
     @pl.loop(1, n)
     def _(q):
         stream_copy(q).wait_send()
+        out_copy(q).wait_send()
         little_copy(q).wait_send()
         mix_copy(q).wait_send()
 
@@ -1333,7 +1393,7 @@
             pltpu.VMEM((2, h, tokens), f32),
             pltpu.VMEM((2, h, WIDE), bf16),
             pltpu.VMEM((2, h, WIDE), f32),
-            pltpu.VMEM((n, STREAMS + 1, h, tokens), bf16),
+            pltpu.VMEM((n, STREAMS, h, tokens), bf16),
             pltpu.VMEM((n, h, WIDE), bf16),
             pltpu.VMEM((n, h, WIDE), bf16),
             pltpu.VMEM((n.bit_length() - 1,) + second.shape, f32),
@@ -1349,7 +1409,6 @@
             DMA((2, 3, 4)),
             DMA((2, 3)),
             DMA((2, 5)),
-            DMA((n,)),
             DMA((2, 2)),
             DMA((2, count)),
             DMA((count,)),
@@ -1357,8 +1416,8 @@
             DMA((n,)),
             DMA((2,)),
         ]
-        + [DMA((n,)) for _ in range(10)]
-        + [DMA((6,))]
+        + [DMA((n,)) for _ in range(12)]
+        + [DMA((7,))]
         + [DMA((2, ring - 1, count)) for _ in range(2)]
         + [DMA((2, ring, count)) for _ in range(2)],
         compiler_params=pltpu.CompilerParams(

time: 888 us -> 848 us (0.955)
  Pallas kernels: 824 us -> 787 us
    pallas_call x1, Pallas kernels: 404 us -> 378 us  [forward_exchange(): pl.pallas_call(functools.partial(forward_kernel, n, count), out_shape=[ja...]
    pallas_call x1, Pallas kernels: 408 us -> 397 us  [backward_exchange(): pl.pallas_call(functools.partial(backward_kernel, n, count), out_shape=[j...]
where the time goes in v5:
time: 848 us; the launch traced here: 842 us
  Pallas kernels  787 us (93%)
  matrix products  23.2 us (3%)
  local copies, waits for them, and re-layouts  17.4 us (2%)
  other arithmetic  13.1 us (2%)
    pallas_call x1, Pallas kernels, backward_exchange(): pl.pallas_call(functools.partial(backward_kernel, n, count), out_shape=[j...  397 us
    pallas_call x1, Pallas kernels, forward_exchange(): pl.pallas_call(functools.partial(forward_kernel, n, count), out_shape=[ja...  378 us
    dot_general x8, matrix products, product(): return jnp.einsum(spec, left, right, preferred_element_type=f32)  23.2 us

profile of v5, /device:TPU:21, one launch (start us, length us, event | category | flops | bytes accessed | tf_op | source)
XLA Modules:
  0.0 842.0 jit_solution(3924882330663959721)
XLA Ops:
  0.6 0.0 copy-start
  0.7 0.0 copy-start.13
  0.7 0.8 multiply_cosine_fusion
  1.5 0.1 pad.24.clone
  1.6 0.1 pad.27.clone
  1.7 0.2 maximum_bitcast_fusion.1
  1.9 0.9 pad_maximum_fusion.refs_3_.refs_9_
  2.8 0.8 copy.54.refs_5_.refs_11_
  3.6 0.1 copy.53
  3.8 0.6 pad.8.refs_10_
  4.4 378.2 %shard_map.221 = (bf16[5,2048,384]{2,1,0:T(8,128)(2,1)}, f32[16,36,384]{2,1,0:T(8,128)}, bf16[4,2048,384]{2,1,0:T(8,128)(2,1)}, f32[8,384]{1,0:T(8,128)}, bf16[3...) custom-call(bf16[9,128,6144]{2,1,0:T(8,128)(2,1)} %refs_19_.1, ...), custom_call_target="tpu_custom_call" | custom-call | tf_op jit(solution)/shard_map/pallas_call | solution.py:626
  382.6 0.0 copy-start.4
  382.7 1.6 convert_reduce_fusion
  384.2 2.2 multiply_reduce_fusion.2
  386.5 0.0 copy-done.4
  386.5 0.4 multiply_convert_fusion.1
  386.8 0.6 copy-done.6
  387.5 0.5 multiply_convert_fusion.2
  388.0 0.0 copy-done
  388.0 0.2 copy-done.14
  388.2 0.1 add_convert_fusion
  388.3 1.5 fusion.15
  389.9 2.7 multiply_reduce_fusion
  392.6 1.3 copy.56
  393.9 0.1 pad.11.clone
  394.0 0.1 pad.13.clone
  394.1 2.9 maximum_maximum_fusion.refs_17_
  396.9 0.0 copy-done.17
  396.9 0.1 select_reduce_fusion
  397.0 4.1 fusion.13
  401.1 0.6 copy-done.19
  401.7 2.7 convolution_convert_fusion.refs_6_
  404.4 14.7 %multiply_convert_fusion.refs_4_ = bf16[384,4096]{1,0:T(8,128)(2,1)} fusion(f32[384,4096]{1,0:T(8,128)} %get-tuple-element.41, bf16[2048,384]{1,0:T(8,128)(2,1)S(1)} %get-tuple-element.118.refs_1_, bf16[2048,4096]{1,0:T(8,128)(2,1)} %get-tuple-element.42), kind=kOutput, calls=%fused_computation | convolution fusion | flops 6445596672 | bytes 27787264 | tf_op jit(solution)/shard_map/ot,oi->ti/dot_general | solution.py:1511
  419.1 0.1 fusion.16
  419.2 0.6 pad.9.refs_18_
  419.9 396.9 %shard_map.222 = (bf16[16,4,64,384]{3,2,1,0:T(8,128)(2,1)}, bf16[16,5,128,384]{3,2,1,0:T(8,128)(2,1)}, f32[48,384]{1,0:T(8,128)}, f32[128,128]{1,0:T(8,128)}, f3...) custom-call(bf16[4,2048,384]{2,1,0:T(8,128)(2,1)} %get-tuple-element, ...), custom_call_target="tpu_custom_call" | custom-call | tf_op jit(solution)/shard_map/pallas_call | solution.py:1365
  816.8 3.2 copy-done.2
  820.0 12.1 %shard_map.223 = (bf16[9,128,6144]{2,1,0:T(8,128)(2,1)}, bf16[128,6144]{1,0:T(8,128)(2,1)}) custom-call(bf16[16,5,128,384]{3,2,1,0:T(8,128)(2,1)S(1)} %copy-done.2, f32[16,36,384]{2,1,0:T(8,128)S(1)} %copy-done.3), custom_call_target="tpu_custom_call" | custom-call | tf_op jit(solution)/shard_map/pallas_call | solution.py:1470
  832.1 0.1 slice_bitcast_fusion
  832.2 0.7 copy.59
  832.8 0.6 slice_bitcast_fusion.1
  833.5 0.7 copy.58
  834.1 0.8 fusion.17
  835.0 2.7 copy.66
  837.7 0.8 copy.67
  838.5 1.3 copy.68
  839.8 1.3 copy.69
  841.1 0.6 copy.70
  (41 shorter events, 0.1 us)
Async XLA Ops:
  0.6 387.4 %copy-start = (bf16[384,40]{0,1:T(8,128)(2,1)S(1)}, bf16[384,40]{0,1:T(8,128)(2,1)}, u32[]{:S(2)}) copy-start(bf16[384,40]{0,1:T(8,128)(2,1)} %param.27) | copy-start | bytes 92164
  0.7 2.1 copy-start.13
  0.7 3.0 copy-start.16
  0.7 2.9 copy-start.15
  382.6 3.8 copy-start.4
  386.4 1.0 copy-start.6
  387.5 0.7 copy-start.14
  392.6 4.4 copy-start.17
  392.6 4.4 copy-start.18
  397.0 4.7 copy-start.19
  401.1 3.3 copy-start.5
  419.9 396.9 %copy-start.3 = (f32[16,36,384]{2,1,0:T(8,128)S(1)}, f32[16,36,384]{2,1,0:T(8,128)}, u32[]{:S(2)}) copy-start(f32[16,36,384]{2,1,0:T(8,128)} %get-tuple-element.48.refs_20_.mixes) | copy-start | bytes 2654212
  816.8 3.2 copy-start.2
  820.0 12.1 %copy-start.10 = (f32[128,128]{1,0:T(8,128)S(1)}, f32[128,128]{1,0:T(8,128)}, u32[]{:S(2)}) copy-start(f32[128,128]{1,0:T(8,128)} %get-tuple-element.57) | copy-start | bytes 196612
  820.0 12.8 %copy-start.11 = (f32[48,384]{1,0:T(8,128)S(1)}, f32[48,384]{1,0:T(8,128)}, u32[]{:S(2)}) copy-start(f32[48,384]{1,0:T(8,128)} %get-tuple-element.52) | copy-start | bytes 221188
  832.1 5.6 copy-start.9
  832.1 6.4 copy-start.8
  837.7 2.1 copy-start.7
  838.5 3.3 copy-start.1
  839.8 1.3 copy-start.12

commit v6 on v5

--- a/solution.py
+++ b/solution.py
@@ -3,6 +3,7 @@
 
 import jax
 import jax.numpy as jnp
+import numpy as np
 from jax import lax
 from jax.experimental import pallas as pl
 from jax.experimental.pallas import tpu as pltpu
@@ -95,11 +96,12 @@
 
 
 def forward_kernel(n, count, *refs):
-    hist, cot, mix, tables, docs_row, docs_col = refs[:6]
-    shards = refs[6 : 6 + count]
-    refs = refs[6 + count :]
-    inputs, mixes, normed_out, level, heads_out, attn_out, slope_out, hidden_out, total = refs[:9]
-    fulls = refs[9 : 9 + count]
+    hist, cot, mix, tables, docs_row, docs_col, groups, weights, cot_in, mix2_in = refs[:10]
+    shards = refs[10 : 10 + count]
+    refs = refs[10 + count :]
+    inputs, mixes, normed_out, level, heads_out, attn_out, slope_out, hidden_out = refs[:8]
+    direct, grad_branch, out_low, little, mix_out, second = refs[8:14]
+    fulls = refs[14 : 14 + count]
     (
         hist_buf,
         slots,
@@ -115,6 +117,10 @@
         branch,
         branch_land,
         smalls,
+        total,
+        token_scale,
+        cot_mix,
+        w_mix2,
         hist_sem,
         cot_sem,
         own_sem,
@@ -135,7 +141,7 @@
         ring_recv,
         core_send,
         core_recv,
-    ) = refs[9 + count :]
+    ) = refs[14 + count :]
     where = Ring(n)
     me, ring, owner = where.me, where.ring, where.owner
     mp = lax.axis_index("mp")
@@ -371,7 +377,7 @@
             pre = first_dims(normed[STREAMS - 1], tiles[spot * 2 + k])
             below = 0.5 + 0.5 * lax.erf(pre * math.sqrt(0.5))
             bell = jnp.exp(-0.5 * pre * pre) * (1.0 / math.sqrt(2.0 * math.pi))
-            slope_buf[c % 2, :, k * 256 : (k + 1) * 256] = below + pre * bell
+            slope_buf[c % 2, :, k * 256 : (k + 1) * 256] = (below + pre * bell).astype(bf16)
             low = (pre * below).astype(bf16)
             hidden[:, pl.ds(pl.multiple_of(c * chunk + k * 256, 256), 256)] = low
         slope_copy(c).start()
@@ -420,6 +426,49 @@
             branch.at[c], branch_land.at[c], swap_send.at[c], swap_recv.at[c], across
         )
 
+    def mixing_network(squares):
+        columns = lax.broadcasted_iota(jnp.int32, (tokens, WIDE), 1)
+        plain = normed.at[0]
+        gain_at = slice(MIXH + STREAMS, MIXH + STREAMS + 1)
+        scale = lax.rsqrt(jnp.sum(squares, axis=0, keepdims=True) * (1.0 / width) + EPS)
+
+        @pl.loop(0, width // 64)
+        def _(r):
+            rows = pl.ds(pl.multiple_of(r * 64, 64), 64)
+            value = total[rows, :]
+            out_low[rows, :] = value.astype(bf16)
+            plain[rows, :] = (value * scale * smalls[rows, :].astype(f32)[:, gain_at]).astype(bf16)
+
+        pre = first_dims(plain[...], smalls[...])
+        below = 0.5 + 0.5 * lax.erf(pre * math.sqrt(0.5))
+        bell = jnp.exp(-0.5 * pre * pre) * (1.0 / math.sqrt(2.0 * math.pi))
+        low = jnp.where(columns < MIXH, pre * below, 0.0).astype(bf16)
+        mix_out[...] = jnp.dot(low, w_mix2[...], preferred_element_type=f32)[:, :MIXH]
+        grad = last_dims(cot_mix[...], w_mix2[...])
+        grad = jnp.where(columns < MIXH, (below + pre * bell) * grad, 0.0).astype(bf16)
+        second[...] = first_dims(low, cot_mix[...])[:MIXH]
+        product = grad.astype(f32) * pre
+        high = product.astype(bf16)
+        ones = jnp.ones((8, WIDE), bf16)
+        inner = last_dims(ones, high) + last_dims(ones, (product - high.astype(f32)).astype(bf16))
+        inner = inner[0:1] * (1.0 / width)
+        step = 256
+
+        @pl.loop(0, width // step)
+        def _(r):
+            rows = pl.ds(pl.multiple_of(r * step, step), step)
+            first = smalls[rows, :]
+            gain = first.astype(f32)[:, gain_at]
+            sums = jnp.dot(plain[rows, :], grad, preferred_element_type=f32)
+            lane = lax.broadcasted_iota(jnp.int32, sums.shape, 1)
+            gain_grad = jnp.sum(first.astype(f32) * sums, axis=1, keepdims=True) / gain
+            little[rows, :] = jnp.where(lane == MIXH + STREAMS, gain_grad, sums)
+            grad_normed = last_dims(first, grad)
+            seed = streams[STREAMS, rows, :].astype(f32) * token_scale[0:1, :]
+            value = seed + scale * (gain * grad_normed - total[rows, :] * (scale * inner))
+            direct[rows, :] = value
+            grad_branch[rows, :] = value.astype(bf16)
+
     def keep(k):
         pairs = [
             (streams, inputs),
@@ -457,6 +506,14 @@
     hist_copy(0).start()
     ring_begin(of(2, 4))
     mixes[me] = mix[...]
+    row = jnp.zeros((1, tokens), f32)
+    for g in range(GROUPS):
+        row = row + jnp.where(groups[...] == g, weights[g], 0.0)
+    token_scale[...] = jnp.broadcast_to(row, token_scale.shape)
+    cot_mix[...] = jnp.zeros_like(cot_mix)
+    cot_mix[:, 0:MIXH] = cot_in[...]
+    w_mix2[...] = jnp.zeros_like(w_mix2)
+    w_mix2[0:MIXH, 0:MIXH] = mix2_in[...]
     hist_copy(0).wait()
     hist_copy(1).start()
     mix_streams(0)
@@ -573,19 +630,26 @@
     rows_product(ring - 2)
     rows_product(ring - 1)
 
-    @pl.loop(0, ring)
-    def _(c):
+    def add_up(c, squares):
         swap_copy(c).wait_recv()
         for b, start in enumerate(blocks(c)):
             both = branch[c, b * half : (b + 1) * half].astype(f32)
             both = both + branch_land[c, b * half : (b + 1) * half].astype(f32)
             rows = pl.ds(start, half)
-            total[rows, :] = streams[STREAMS - 1, rows, :].astype(f32) + both
+            value = streams[STREAMS - 1, rows, :].astype(f32) + both
+            total[rows, :] = value
+            value = value * value
+            for k in range(half // 8):
+                squares = squares + value[k * 8 : (k + 1) * 8]
+        return squares
+
+    squares = lax.fori_loop(0, ring, add_up, jnp.zeros((8, tokens), f32))
 
     for c in range(ups - 2, ups):
         slope_copy(c).wait()
     for k in range(5):
         keep(k).wait()
+    mixing_network(squares)
 
     @pl.loop(0, ring)
     def _(c):
@@ -613,12 +677,15 @@
                 ring_copy(way, step, p).wait_send()
 
 
-def forward_exchange(n, history, cot_out, mix, tables, docs, shards):
+def forward_exchange(
+    n, history, cot_out, mix, tables, docs, groups, weights, cot_mix, w_mix2, shards
+):
     count, ring = len(shards), n // 2
     feat, tokens = history.shape[1], mix.shape[1]
     h, width = feat // 2, n * feat
     hbm = pl.BlockSpec(memory_space=pl.ANY)
     vmem = pl.BlockSpec(memory_space=pltpu.VMEM)
+    smem = pl.BlockSpec(memory_space=pltpu.SMEM)
     columns, units = shards[0].shape[2], shards[2].shape[1]
     across = columns // HEAD
     deep = 2 * shards[0].shape[1]
@@ -632,16 +699,21 @@
             jax.ShapeDtypeStruct((8, tokens), f32),
             jax.ShapeDtypeStruct((3, across, tokens, HEAD), bf16),
             jax.ShapeDtypeStruct((tokens, columns), bf16),
-            jax.ShapeDtypeStruct((tokens, units), f32),
+            jax.ShapeDtypeStruct((tokens, units), bf16),
             jax.ShapeDtypeStruct((tokens, units), bf16),
             jax.ShapeDtypeStruct((width, tokens), f32),
+            jax.ShapeDtypeStruct((width, tokens), bf16),
+            jax.ShapeDtypeStruct((width, tokens), bf16),
+            jax.ShapeDtypeStruct((width, WIDE), f32),
+            jax.ShapeDtypeStruct((tokens, MIXH), f32),
+            jax.ShapeDtypeStruct((MIXH, WIDE), f32),
         ]
         + [
             jax.ShapeDtypeStruct(s.shape[:-2] + (s.shape[-2] * n, s.shape[-1]), s.dtype)
             for s in shards
         ],
-        in_specs=[hbm, hbm, vmem, vmem, vmem, vmem] + [hbm] * count,
-        out_specs=[hbm, vmem, hbm, vmem, hbm, hbm, hbm, hbm, vmem] + [hbm] * count,
+        in_specs=[hbm, hbm] + [vmem] * 5 + [smem] + [vmem] * 2 + [hbm] * count,
+        out_specs=[hbm, vmem, hbm, vmem, hbm, hbm, hbm, hbm] + [vmem] * 6 + [hbm] * count,
         scratch_shapes=[
             pltpu.VMEM((2, HIST, h, tokens), bf16),
             pltpu.VMEM((n, STREAMS + 1, h, tokens), bf16),
@@ -650,13 +722,17 @@
             pltpu.VMEM((6, width, 2 * HEAD), bf16),
             pltpu.VMEM((3, across, tokens, HEAD), bf16),
             pltpu.VMEM((tokens, columns), bf16),
-            pltpu.VMEM((2, tokens, 512), f32),
+            pltpu.VMEM((2, tokens, 512), bf16),
             pltpu.VMEM((tokens, units), bf16),
             pltpu.VMEM((2, deep, units), bf16),
             pltpu.VMEM((2, deep, columns), bf16),
             pltpu.VMEM((ring, deep, tokens), bf16),
             pltpu.VMEM((ring, deep, tokens), bf16),
             pltpu.VMEM((width, WIDE), bf16),
+            pltpu.VMEM((width, tokens), f32),
+            pltpu.VMEM((8, tokens), f32),
+            pltpu.VMEM((tokens, WIDE), bf16),
+            pltpu.VMEM((WIDE, WIDE), bf16),
             DMA((2,)),
             DMA((n,)),
             DMA,
@@ -674,8 +750,8 @@
         compiler_params=pltpu.CompilerParams(
             collective_id=0, has_side_effects=True, vmem_limit_bytes=60 * 1024 * 1024
         ),
-    )(history, cot_out, mix, tables, docs, docs.T, *shards)
-    return found[:9], found[9:]
+    )(history, cot_out, mix, tables, docs, docs.T, groups, weights, cot_mix, w_mix2, *shards)
+    return found[:14], found[14:]
 
 
 def backward_kernel(n, count, *refs):
@@ -684,11 +760,12 @@
         grad_branch,
         hidden,
         attn,
-        grad_up,
+        slope,
         heads,
-        grad_attended,
         w_qkv,
+        w_out,
         w_up,
+        w_down,
         tables,
         docs_row,
         docs_col,
@@ -701,13 +778,16 @@
         second,
         hist,
         mixes,
-    ) = refs[:21]
-    across_land, feature_side, mix_sum, little_sum, second_sum = refs[21:26]
-    sums, mates = refs[26 : 26 + count], refs[26 + count : 26 + 2 * count]
-    refs = refs[26 + 2 * count :]
+    ) = refs[:22]
+    across_land, feature_side, mix_sum, little_sum, second_sum = refs[22:27]
+    sums, mates = refs[27 : 27 + count], refs[27 + count : 27 + 2 * count]
+    refs = refs[27 + 2 * count :]
     slots, other, mine, final = (refs[k * count : (k + 1) * count] for k in range(4))
     (
         rows_buf,
+        branch_buf,
+        grad_up,
+        grad_attended,
         projs,
         grads,
         qkv_tile,
@@ -734,6 +814,8 @@
         m_other,
         l_sum,
         rows_sem,
+        branch_sem,
+        back_tile,
         tile_sem,
         load_sem,
         back_sem,
@@ -780,29 +862,36 @@
     def target(way, step):
         return -1 - step if way == 0 else 1 + step
 
-    def rows_load(way, step):
+    def rows_load(way, step, branch):
         spot = step % 3
         copies = []
         for which in range(2):
             shard = owner(target(way, step)) + which * (where.mate - me)
             rows = pl.ds(pl.multiple_of(shard * size + way * half, half), half)
-            copies += [
-                pltpu.make_async_copy(
-                    normed.at[:, rows, :],
-                    rows_buf.at[way, spot, which, pl.ds(0, STREAMS)],
-                    rows_sem.at[way, spot, 2 * which],
-                ),
-                pltpu.make_async_copy(
-                    grad_branch.at[rows, :],
-                    rows_buf.at[way, spot, which, STREAMS],
-                    rows_sem.at[way, spot, 2 * which + 1],
-                ),
-            ]
+            if branch:
+                here, there, sem = grad_branch.at[rows, :], branch_buf, branch_sem
+            else:
+                here, there, sem = normed.at[:, rows, :], rows_buf, rows_sem
+            copies.append(
+                pltpu.make_async_copy(here, there.at[way, spot, which], sem.at[way, spot, which])
+            )
         return copies
 
+    def rows_begin(step, branch):
+        for way in range(2):
+            for copy in rows_load(way, step, branch):
+                copy.start()
+
+    def rows_wait(step, branch):
+        for way in range(2):
+            for copy in rows_load(way, step, branch):
+                copy.wait()
+
     def part(way, step, i, which, k, columns):
-        source = (k, STREAMS, STREAMS - 1, STREAMS)[i]
-        left = rows_buf[way, step % 3, which, source]
+        if i in (1, 3):
+            left = branch_buf[way, step % 3, which]
+        else:
+            left = rows_buf[way, step % 3, which, k if i == 0 else STREAMS - 1]
         right = (projs, attn, grad_up, hidden)[i]
         right = right[k, :, columns] if i == 0 else right[:, columns]
         return jnp.dot(left, right, preferred_element_type=f32)
@@ -878,6 +967,57 @@
         ring_copy(way, step, i).start()
         core_copy(way, step, i).wait_send()
         give(way, step + 1, i)
+
+    broad = tokens
+
+    def back_loads(c, wide, source, sloped):
+        columns = pl.ds(pl.multiple_of(c * broad, 128), wide)
+        spot = c % 2
+        copies = [
+            pltpu.make_async_copy(
+                source.at[:, columns], grads.at[1 + spot, :, pl.ds(0, wide)], back_tile.at[spot, 0]
+            )
+        ]
+        if sloped:
+            copies.append(
+                pltpu.make_async_copy(
+                    slope.at[:, columns],
+                    grads.at[3, pl.ds(pl.multiple_of(spot * tokens, 128), tokens), pl.ds(0, wide)],
+                    back_tile.at[spot, 1],
+                )
+            )
+        return copies
+
+    def back_turn(c, wide, source, sloped):
+        columns = pl.ds(pl.multiple_of(c * broad, 128), wide)
+        spot = c % 2
+        for copy in back_loads(c, wide, source, sloped):
+            copy.wait()
+        value = first_dims(grads[0], grads[1 + spot, :, 0:wide])
+        if sloped:
+            rows = pl.ds(pl.multiple_of(spot * tokens, 128), tokens)
+            value = value * grads[3, rows, 0:wide].astype(f32)
+            grad_up[:, columns] = value.astype(bf16)
+        else:
+            grad_attended[:, columns] = value.astype(bf16)
+
+    def back_all(source, units, sloped):
+        full, rest = units // broad, units % broad
+        for copy in back_loads(0, broad, source, sloped):
+            copy.start()
+
+        @pl.loop(0, full - 1)
+        def _(c):
+            for copy in back_loads(c + 1, broad, source, sloped):
+                copy.start()
+            back_turn(c, broad, source, sloped)
+
+        if rest:
+            for copy in back_loads(full, rest, source, sloped):
+                copy.start()
+        back_turn(full - 1, broad, source, sloped)
+        if rest:
+            back_turn(full, rest, source, sloped)
 
     def attend_back(head):
         lane = pl.ds(pl.multiple_of(head * HEAD, HEAD), HEAD)
@@ -1094,8 +1234,8 @@
         source = (me - q + n) % n
         return pltpu.make_async_copy(
             feature_side.at[source, pl.ds(0, STREAMS), pl.ds(pl.multiple_of(mp * h, h), h), :],
-            f_buf,
-            back_sem.at[0, 1],
+            f_buf.at[q % 2],
+            back_sem.at[q % 2, 1],
         )
 
     def mix_copy(q):
@@ -1107,7 +1247,7 @@
         for s in range(STREAMS):
             totals = [None] * HIST
             for r in range(h // 16):
-                grad = f_buf[s, r * 16 : r * 16 + 16, :].astype(f32)
+                grad = f_buf[q % 2, s, r * 16 : r * 16 + 16, :].astype(f32)
                 for j in range(HIST):
                     both = h_buf[q % 2, j, r * 16 : r * 16 + 16, :].astype(f32) * grad
                     both = both[0:8] + both[8:16]
@@ -1116,11 +1256,7 @@
                 m_wide[pl.ds(s * HIST + j, 1), :] = jnp.sum(totals[j], axis=0, keepdims=True)
         m_slots[q] = m_wide[...].astype(bf16)
 
-    def mix_turn(q):
-        @pl.when(q < n - 1)
-        def _():
-            hist_load(q + 1).start()
-
+    def arrive(q):
         @pl.when(q == 0)
         def _():
             home_copy().wait()
@@ -1133,6 +1269,17 @@
 
         across_copy(q).start()
         grad_load(q).start()
+        hist_load(q).start()
+
+    def mix_turn(q):
+        @pl.when(q == 0)
+        def _():
+            arrive(q)
+
+        @pl.when(q < n - 1)
+        def _():
+            arrive(q + 1)
+
         grad_load(q).wait()
         hist_load(q).wait()
         mix_backward(q)
@@ -1141,14 +1288,52 @@
         def _():
             mix_copy(q).start()
 
-    early = [(i, way) for i in (3, 2, 1) for way in range(2)]
+    ahead = [(i, way) for i in (3, 1) for way in range(2)]
+    middle = [(2, way) for way in range(2)]
     late = [(0, way) for way in range(2)]
-
-    for way in range(2):
-        for step in range(3):
-            for copy in rows_load(way, step):
-                copy.start()
-
+    lead = 3
+
+    def unit(step, i, way):
+        if way == 0:
+            for w in range(2):
+                ring_copy(w, step - 1, i).wait_send()
+        ring_unit(step, i, way)
+
+    def first_blocks(some):
+        for i, way in some:
+            give(way, 0, i)
+        for i, way in some:
+            stage(way, 0, i)
+            other_copy(way, 0, i).wait()
+            add(way, 0, i, first=True)
+            ring_copy(way, 0, i).start()
+        for i, way in some:
+            core_copy(way, 0, i).wait_send()
+            give(way, 1, i)
+        for i, way in some:
+            stage(way, 1, i)
+
+    def ahead_units(step):
+        for i, way in ahead:
+            unit(step, i, way)
+        for i, way in ahead:
+            stage(way, step + 1, i)
+
+    def finish(i, way):
+        other_copy(way, ring - 1, i).wait()
+        ring_copy(way, ring - 2, i).wait_recv()
+        if way == 1:
+            final_copy(0, i).wait()
+        add(way, ring - 1, i, last=True)
+        final_copy(way, i).start()
+
+    branch_copy = pltpu.make_async_copy(grad_branch, grads.at[0], end_sem.at[7])
+    for step in range(2):
+        rows_begin(step, True)
+    branch_copy.start()
+    for step in range(3):
+        rows_begin(step, False)
+    rows_begin(2, True)
     home_output().start()
 
     @pl.loop(1, n)
@@ -1162,24 +1347,33 @@
     m_wide[...] = jnp.zeros_like(m_wide)
     for way in range(2):
         slots[0][way, 0] = jnp.zeros_like(slots[0][way, 0])
-        for copy in rows_load(way, 0) + rows_load(way, 1):
-            copy.wait()
-    for i, way in early[:2]:
-        give(way, 0, i)
-    for u, (i, way) in enumerate(early):
-        if u + 2 < len(early):
-            give(early[u + 2][1], 0, early[u + 2][0])
-        stage(way, 0, i)
-        other_copy(way, 0, i).wait()
-        add(way, 0, i, first=True)
-        ring_copy(way, 0, i).start()
-    for i, way in early:
-        core_copy(way, 0, i).wait_send()
-        give(way, 1, i)
-    for i, way in early:
-        stage(way, 1, i)
-
-    @pl.loop(0, heads.shape[1])
+    rows_wait(0, True)
+    rows_wait(1, True)
+    first_blocks(ahead[:2])
+    first_blocks(ahead[2:])
+    branch_copy.wait()
+    back_all(w_down, grad_up.shape[1], True)
+    rows_wait(2, True)
+    ahead_units(1)
+    rows_begin(3, True)
+    rows_wait(0, False)
+    rows_wait(1, False)
+    first_blocks(middle)
+    rows_wait(3, True)
+    ahead_units(2)
+    rows_begin(4, True)
+    back_all(w_out, grad_attended.shape[1], False)
+    heads_here = heads.shape[1]
+
+    @pl.loop(0, heads_here // 2)
+    def _(head):
+        attend_back(head)
+
+    rows_wait(4, True)
+    ahead_units(3)
+    rows_begin(5, True)
+
+    @pl.loop(heads_here // 2, heads_here)
     def _(head):
         attend_back(head)
 
@@ -1187,15 +1381,17 @@
         give(way, 0, i)
     for i, way in late:
         stage(way, 0, i)
-    hist_load(0).start()
 
     opening = 2
+    order = middle + ahead + late
 
     @pl.loop(1, ring - 1)
     def _(step):
-        for way in range(2):
-            for copy in rows_load(way, step + 1):
-                copy.wait()
+        rows_wait(step + 1, False)
+
+        @pl.when(step + lead <= ring - 2)
+        def _():
+            rows_wait(step + lead + 1, True)
 
         for b in range(bits):
 
@@ -1211,7 +1407,7 @@
             start_loads(0)
             inner_copy().wait()
 
-        for u, (i, way) in enumerate(early + late):
+        for u, (i, way) in enumerate(order):
             if i == 0:
 
                 @pl.when(step > 1)
@@ -1230,11 +1426,18 @@
                 ring_copy(way, step - 1, i).start()
                 core_copy(way, step - 1, i).wait_send()
                 give(way, step, i)
+            elif i == 2:
+                unit(step, i, way)
             else:
-                if way == 0:
-                    for w in range(2):
-                        ring_copy(w, step - 1, i).wait_send()
-                ring_unit(step, i, way)
+
+                @pl.when(step + lead <= ring - 2)
+                def _():
+                    unit(step + lead, i, way)
+
+                @pl.when(step == ring - 1 - lead)
+                def _():
+                    finish(i, way)
+
             if u % 2 == 0:
 
                 @pl.when((step >= opening) & (step < opening + n // 4))
@@ -1251,15 +1454,23 @@
                 tile_turn(u)
 
             if u > 0:
-                before, w = (early + late)[u - 1]
-                stage(w, step if before == 0 else step + 1, before)
+                before, w = order[u - 1]
+                if before in (1, 3):
+
+                    @pl.when(step + lead <= ring - 2)
+                    def _():
+                        stage(w, step + lead + 1, before)
+                else:
+                    stage(w, step if before == 0 else step + 1, before)
         stage(1, step, 0)
 
         @pl.when(step < ring - 2)
         def _():
-            for way in range(2):
-                for copy in rows_load(way, step + 2):
-                    copy.start()
+            rows_begin(step + 2, False)
+
+        @pl.when(step + lead < ring - 2)
+        def _():
+            rows_begin(step + lead + 2, True)
 
     @pl.loop(1, n)
     def _(q):
@@ -1284,20 +1495,11 @@
     mix_across.start()
 
     for i, way in late:
-        if way == 0:
-            for w in range(2):
-                ring_copy(w, ring - 3, i).wait_send()
-        ring_unit(ring - 2, i, way)
+        unit(ring - 2, i, way)
     for i, way in late:
         stage(way, ring - 1, i)
-
-    for i, way in early + late:
-        other_copy(way, ring - 1, i).wait()
-        ring_copy(way, ring - 2, i).wait_recv()
-        if way == 1:
-            final_copy(0, i).wait()
-        add(way, ring - 1, i, last=True)
-        final_copy(way, i).start()
+    for i, way in middle + late:
+        finish(i, way)
 
     mix_across.wait()
     mix_sum[...] = m_mine[...] + m_other[...]
@@ -1318,7 +1520,7 @@
         sum_copy(q).wait_send()
         across_copy(q).wait()
 
-    for i, way in early + late:
+    for i, way in order:
         ring_copy(way, ring - 2, i).wait_send()
         core_copy(way, ring - 1, i).wait_send()
 
@@ -1329,11 +1531,12 @@
     grad_branch,
     hidden,
     attn,
-    grad_up,
+    slope,
     heads,
-    grad_attended,
     w_qkv,
+    w_out,
     w_up,
+    w_down,
     tables,
     docs,
     level,
@@ -1350,7 +1553,7 @@
     count, ring = len(shards), n // 2
     feat, tokens = history.shape[1], level.shape[1]
     h, width = feat // 2, n * feat
-    units = grad_up.shape[1]
+    units = slope.shape[1]
     hbm = pl.BlockSpec(memory_space=pl.ANY)
     vmem = pl.BlockSpec(memory_space=pltpu.VMEM)
 
@@ -1360,7 +1563,7 @@
     half = shards[0].shape[-2] // 2
     tall = 256
     columns = attn.shape[1]
-    places = [hbm, hbm, vmem, vmem, vmem, vmem, vmem, hbm, hbm, vmem, vmem, vmem, vmem]
+    places = [hbm, hbm, vmem, vmem, hbm, vmem, hbm, hbm, hbm, hbm, vmem, vmem, vmem, vmem]
     places += [hbm, hbm, hbm, hbm, hbm, vmem, hbm, hbm]
     found = pl.pallas_call(
         functools.partial(backward_kernel, n, count),
@@ -1380,7 +1583,10 @@
         + [pltpu.VMEM((2,) + cut(s, half), bf16) for s in shards]
         + [pltpu.VMEM(cut(s, half), f32) for s in shards]
         + [
-            pltpu.VMEM((2, 3, 2, STREAMS + 1, half, tokens), bf16),
+            pltpu.VMEM((2, 3, 2, STREAMS, half, tokens), bf16),
+            pltpu.VMEM((2, 3, 2, half, tokens), bf16),
+            pltpu.VMEM((tokens, units), bf16),
+            pltpu.VMEM((tokens, columns), bf16),
             pltpu.VMEM((3, tokens, columns), bf16),
             pltpu.VMEM((STREAMS, width, tokens), bf16),
             pltpu.VMEM((2, 3, tall, columns), bf16),
@@ -1398,7 +1604,7 @@
             pltpu.VMEM((n, h, WIDE), bf16),
             pltpu.VMEM((n.bit_length() - 1,) + second.shape, f32),
             pltpu.VMEM(second.shape, f32),
-            pltpu.VMEM((STREAMS, h, tokens), bf16),
+            pltpu.VMEM((2, STREAMS, h, tokens), bf16),
             pltpu.VMEM((2, HIST, h, tokens), bf16),
             pltpu.VMEM((MIXED, tokens), f32),
             pltpu.VMEM((n, MIXED, tokens), bf16),
@@ -1406,7 +1612,9 @@
             pltpu.VMEM((MIXED, tokens), f32),
             pltpu.VMEM((MIXED, tokens), f32),
             pltpu.VMEM((h, WIDE), f32),
-            DMA((2, 3, 4)),
+            DMA((2, 3, 2)),
+            DMA((2, 3, 2)),
+            DMA((2, 2)),
             DMA((2, 3)),
             DMA((2, 5)),
             DMA((2, 2)),
@@ -1417,7 +1625,7 @@
             DMA((2,)),
         ]
         + [DMA((n,)) for _ in range(12)]
-        + [DMA((7,))]
+        + [DMA((8,))]
         + [DMA((2, ring - 1, count)) for _ in range(2)]
         + [DMA((2, ring, count)) for _ in range(2)],
         compiler_params=pltpu.CompilerParams(
@@ -1428,11 +1636,12 @@
         grad_branch,
         hidden,
         attn,
-        grad_up,
+        slope,
         heads,
-        grad_attended,
         w_qkv,
+        w_out,
         w_up,
+        w_down,
         tables,
         docs,
         docs.T,
@@ -1449,66 +1658,88 @@
     return found[1], found[2], found[3], found[4], found[5 : 5 + count]
 
 
-def history_kernel(grads, mixes, grad_history, block_out):
+def history_kernel(count, *refs):
+    grads, mixes = refs[:2]
+    sums = refs[2 : 2 + count]
+    grad_history, block_out = refs[2 + count : 4 + count]
+    outs, kept = refs[4 + count : 4 + 2 * count], refs[4 + 2 * count : 4 + 3 * count]
+    sems = refs[4 + 3 * count]
     feat = grads.shape[2]
-
-    @pl.loop(0, feat // 16)
-    def _(r):
-        rows = pl.ds(pl.multiple_of(r * 16, 16), 16)
-        each = [grads[0, s, rows, :].astype(f32) for s in range(STREAMS)]
-        for j in range(HIST):
-            total = mixes[0, pl.ds(j, 1), :] * each[0]
-            for s in range(1, STREAMS):
-                total = total + mixes[0, pl.ds(s * HIST + j, 1), :] * each[s]
-            grad_history[j, rows, :] = total.astype(bf16)
-
-    block_out[...] = grads[0, STREAMS]
-
-
-def history_gradient(feature_side, mixes):
+    came = [pltpu.make_async_copy(sums[i], kept[i], sems.at[0, i]) for i in range(count)]
+    left = [pltpu.make_async_copy(kept[i], outs[i], sems.at[1, i]) for i in range(count)]
+
+    @pl.when(pl.program_id(0) == 0)
+    def _():
+        for copy in came:
+            copy.start()
+
+    @pl.when(pl.program_id(0) == pl.num_programs(0) // 2)
+    def _():
+        for copy in came:
+            copy.wait()
+        for copy in left:
+            copy.start()
+
+    tokens = grads.shape[3]
+    for i in range(grads.shape[0]):
+        lanes = pl.ds(i * tokens, tokens)
+
+        @pl.loop(0, feat // 32)
+        def _(r):
+            rows = pl.ds(pl.multiple_of(r * 32, 32), 32)
+            each = [grads[i, s, rows, :].astype(f32) for s in range(STREAMS)]
+            for j in range(HIST):
+                total = mixes[i, pl.ds(j, 1), :] * each[0]
+                for s in range(1, STREAMS):
+                    total = total + mixes[i, pl.ds(s * HIST + j, 1), :] * each[s]
+                grad_history[j, rows, lanes] = total.astype(bf16)
+
+        block_out[:, lanes] = grads[i, STREAMS]
+
+    @pl.when(pl.program_id(0) == pl.num_programs(0) - 1)
+    def _():
+        for copy in left:
+            copy.wait()
+
+
+def history_gradient(feature_side, mixes, sums):
     n, streams, feat, tokens = feature_side.shape
-    return pl.pallas_call(
-        history_kernel,
-        grid=(n,),
+    count, group = len(sums), 4
+    hbm = pl.BlockSpec(memory_space=pl.ANY)
+    found = pl.pallas_call(
+        functools.partial(history_kernel, count),
+        grid=(n // group,),
         out_shape=[
             jax.ShapeDtypeStruct((HIST, feat, n * tokens), bf16),
             jax.ShapeDtypeStruct((feat, n * tokens), bf16),
-        ],
+        ]
+        + [jax.ShapeDtypeStruct(s.shape, s.dtype) for s in sums],
         in_specs=[
-            pl.BlockSpec((1, streams, feat, tokens), lambda i: (i, 0, 0, 0)),
-            pl.BlockSpec((1,) + mixes.shape[1:], lambda i: (i, 0, 0)),
-        ],
+            pl.BlockSpec((group, streams, feat, tokens), lambda i: (i, 0, 0, 0)),
+            pl.BlockSpec((group,) + mixes.shape[1:], lambda i: (i, 0, 0)),
+        ]
+        + [hbm] * count,
         out_specs=[
-            pl.BlockSpec((HIST, feat, tokens), lambda i: (0, 0, i)),
-            pl.BlockSpec((feat, tokens), lambda i: (0, i)),
-        ],
-        compiler_params=pltpu.CompilerParams(vmem_limit_bytes=32 * 1024 * 1024),
-    )(feature_side, mixes)
+            pl.BlockSpec((HIST, feat, group * tokens), lambda i: (0, 0, i)),
+            pl.BlockSpec((feat, group * tokens), lambda i: (0, i)),
+        ]
+        + [hbm] * count,
+        scratch_shapes=[pltpu.VMEM(s.shape, s.dtype) for s in sums] + [DMA((2, count))],
+        compiler_params=pltpu.CompilerParams(vmem_limit_bytes=62 * 1024 * 1024),
+    )(feature_side, mixes, *sums)
+    return found[0], found[1], found[2:]
 
 
 def angle_tables(length):
     halfway = ROT // 2
-    frequency = jnp.exp(jnp.arange(halfway, dtype=f32) * (-2.0 * math.log(10000.0) / ROT))
-    places = (jnp.arange(length) % TOK_DEV).astype(f32)
-    angles = places[:, None] * frequency[None, :]
-    cosine, sine_part = jnp.cos(angles), jnp.sin(angles)
-    rest = jnp.zeros((length, HEAD - ROT), f32)
-    none = jnp.zeros((length, halfway), f32)
-    return jnp.stack(
-        [
-            jnp.concatenate([cosine, cosine, rest + 1.0], axis=1),
-            jnp.concatenate([-sine_part, none, rest], axis=1),
-            jnp.concatenate([none, sine_part, rest], axis=1),
-        ]
-    )
-
-
-def gelu_exact(inputs):
-    return jax.nn.gelu(inputs, approximate=False)
-
-
-def product(spec, left, right):
-    return jnp.einsum(spec, left, right, preferred_element_type=f32)
+    frequency = np.exp(np.arange(halfway) * (-2.0 * math.log(10000.0) / ROT))
+    angles = (np.arange(length) % TOK_DEV)[:, None] * frequency[None, :]
+    tables = np.zeros((3, length, HEAD), np.float32)
+    tables[0] = 1.0
+    tables[0, :, :halfway] = tables[0, :, halfway:ROT] = np.cos(angles)
+    tables[1, :, :halfway] = -np.sin(angles)
+    tables[2, :, halfway:ROT] = np.sin(angles)
+    return jnp.asarray(tables)
 
 
 def body(
@@ -1529,67 +1760,37 @@
 ):
     n = lax.axis_size("dp")
     tokens_here = mix_in.shape[0]
-    width = n * history.shape[1]
     small = jnp.pad(
         jnp.concatenate([w_mix1, gains.T], axis=1), ((0, 0), (0, WIDE - MIXH - gains.shape[0]))
     )
     tables = angle_tables(tokens_here)
     kept, (full_qkv, full_o, full_up, full_down, smalls) = forward_exchange(
-        n, history, cot_out, mix_in.T, tables, doc_ids, (w_qkv, w_out, w_up, w_down, small)
+        n,
+        history,
+        cot_out,
+        mix_in.T,
+        tables,
+        doc_ids,
+        group_ids,
+        group_scale,
+        cot_mix,
+        w_mix2,
+        (w_qkv, w_out, w_up, w_down, small),
     )
-    inputs, mixes, normed, level, qkv_heads, attn_cat, slope, hidden, out_full = kept
-    full_m1 = smalls[:, :MIXH]
-    gain_f = smalls[:, MIXH : MIXH + STREAMS + 1].astype(f32)
-    out_low = out_full.astype(bf16)
-    mix_level = lax.rsqrt(jnp.mean(out_full * out_full, axis=0) + EPS)
-    mix_unit = out_full * mix_level[None, :]
-    mix_gain = gain_f[:, STREAMS : STREAMS + 1]
-    mix_normed = (mix_unit * mix_gain).astype(bf16)
-    mix_pre = product("dt,dm->tm", mix_normed, full_m1)
-    mix_hidden = gelu_exact(mix_pre).astype(bf16)
-    mix_out = product("tm,mo->to", mix_hidden, w_mix2)
-
-    row_scale = jnp.sum(
-        jnp.where(group_ids[0][:, None] == jnp.arange(GROUPS)[None, :], group_scale[None, :], 0.0),
-        axis=1,
-    )
-    seed = inputs[STREAMS].astype(f32) * row_scale[None, :]
-    grad_mix2_part = product("tm,to->mo", mix_hidden, cot_mix)
-    grad_mix_hidden = product("to,mo->tm", cot_mix, w_mix2)
-    grad_mix_pre = jax.vjp(gelu_exact, mix_pre)[1](grad_mix_hidden)[0].astype(bf16)
-    grad_m1_part = product("dt,tm->dm", mix_normed, grad_mix_pre)
-    grad_mix_normed = product("dm,tm->dt", full_m1, grad_mix_pre)
-    grad_gain_mix = jnp.sum(mix_unit * grad_mix_normed, axis=1)
-    mix_inner = jnp.mean(mix_unit * mix_gain * grad_mix_normed, axis=0)
-    grad_out_full = seed + mix_level[None, :] * (
-        mix_gain * grad_mix_normed - mix_unit * mix_inner[None, :]
-    )
-    grad_branch = grad_out_full.astype(bf16)
-    grad_attended = product("ot,oi->ti", grad_branch, full_o).astype(bf16)
-    grad_hidden = product("ot,oi->ti", grad_branch, full_down)
-    grad_up_pre = (slope * grad_hidden).astype(bf16)
-
-    little = jnp.concatenate(
-        [
-            grad_m1_part,
-            jnp.zeros((width, STREAMS), f32),
-            grad_gain_mix[:, None],
-            jnp.zeros((width, WIDE - MIXH - STREAMS - 1), f32),
-        ],
-        axis=1,
-    )
-    second = jnp.pad(grad_mix2_part, ((0, 0), (0, WIDE - MIXH)))
+    inputs, mixes, normed, level, qkv_heads, attn_cat, slope, hidden = kept[:8]
+    grad_out_full, grad_branch, out_low, little, mix_out, second = kept[8:]
     feature_side, mix_sum, little_sum, second_sum, sums = backward_exchange(
         n,
         normed,
         grad_branch,
         hidden,
         attn_cat,
-        grad_up_pre,
+        slope,
         qkv_heads,
-        grad_attended,
         full_qkv,
+        full_o,
         full_up,
+        full_down,
         tables,
         doc_ids,
         level,
@@ -1603,7 +1804,7 @@
         mixes,
         (w_qkv, w_out, w_up, w_down),
     )
-    grad_history, block_out = history_gradient(feature_side, mixes)
+    grad_history, block_out, sums = history_gradient(feature_side, mixes, sums)
     grad_qkv, grad_w_out, grad_w_up, grad_w_down = sums
     return (
         block_out,

time: 848 us -> 818 us (0.965)
  matrix products: 23.2 us -> 0 us
  other arithmetic: 13.1 us -> 0.73 us
  Pallas kernels: 787 us -> 798 us
    dot_general x8 -> x0, matrix products: 23.2 us -> none  [product(): return jnp.einsum(spec, left, right, preferred_element_type=f32)]
    pallas_call x1, Pallas kernels: 378 us -> 387 us  [forward_exchange(): pl.pallas_call(functools.partial(forward_kernel, n, count), out_shape=[ja...]
where the time goes in v6:
time: 818 us; the launch traced here: 809 us
  Pallas kernels  798 us (98%)
  local copies, waits for them, and re-layouts  9.67 us (1%)
    pallas_call x1, Pallas kernels, backward_exchange(): pl.pallas_call(functools.partial(backward_kernel, n, count), out_shape=[j...  398 us
    pallas_call x1, Pallas kernels, forward_exchange(): pl.pallas_call(functools.partial(forward_kernel, n, count), out_shape=[ja...  387 us

profile of v6, /device:TPU:21, one launch (start us, length us, event | category | flops | bytes accessed | tf_op | source)
XLA Modules:
  0.0 809.4 jit_solution(11952200321093866779)
XLA Ops:
  0.6 0.7 pad_maximum_fusion
  1.4 0.1 copy.40
  1.5 0.6 pad.4.refs_14_
  2.1 1.5 copy.42.refs_8_
  3.6 1.5 copy.41.refs_5_.refs_12_
  5.1 386.7 %shard_map.230 = (bf16[5,2048,384]{2,1,0:T(8,128)(2,1)}, f32[16,36,384]{2,1,0:T(8,128)}, bf16[4,2048,384]{2,1,0:T(8,128)(2,1)}, f32[8,384]{1,0:T(8,128)}, bf16[3...) custom-call(bf16[9,128,6144]{2,1,0:T(8,128)(2,1)} %refs_20_.1, ...), custom_call_target="tpu_custom_call" | custom-call | tf_op jit(solution)/shard_map/pallas_call | solution.py:693
  391.9 0.0 copy-start
  391.9 398.4 %shard_map.231 = (bf16[16,4,64,384]{3,2,1,0:T(8,128)(2,1)}, bf16[16,5,128,384]{3,2,1,0:T(8,128)(2,1)}, f32[48,384]{1,0:T(8,128)}, f32[128,128]{1,0:T(8,128)}, f3...) custom-call(bf16[4,2048,384]{2,1,0:T(8,128)(2,1)} %get-tuple-element, ...), custom_call_target="tpu_custom_call" | custom-call | tf_op jit(solution)/shard_map/pallas_call | solution.py:1568
  790.3 1.5 copy.45
  791.8 1.5 slice_bitcast_fusion.1
  793.2 0.0 copy-done
  793.2 0.7 copy.44
  794.0 0.9 slice_bitcast_fusion
  794.9 0.7 copy.46
  795.6 0.0 copy-start.1
  795.6 12.9 %shard_map.232 = (bf16[9,128,6144]{2,1,0:T(8,128)(2,1)}, bf16[128,6144]{1,0:T(8,128)(2,1)}, f32[3,128,1024]{2,1,0:T(8,128)}, f32[128,1024]{1,0:T(8,128)}, f32[128,4096]{1,0:T(8,128)}, /*index=5*/f32[128,4096]{1,0:T(8,128)}) custom-call(bf16[16,5,128,384]{3,2,1,0:T(8,128)(2,1)} %get-tuple-element.62.refs_0_, ...), custom_call_target="tpu_custom_call" | custom-call | tf_op jit(solution)/shard_map/pallas_call | solution.py:1709
  808.5 0.0 copy-done.1
  808.5 0.6 copy.48
Async XLA Ops:
  391.9 401.4 %copy-start = (f32[384,40]{1,0:T(8,128)S(1)}, f32[384,40]{1,0:T(8,128)}, u32[]{:S(2)}) copy-start(f32[384,40]{1,0:T(8,128)} %get-tuple-element.100) | copy-start | bytes 184324
  795.6 12.9 %copy-start.1 = (f32[40,128]{1,0:T(8,128)S(1)}, f32[40,128]{1,0:T(8,128)}, u32[]{:S(2)}) copy-start(f32[40,128]{1,0:T(8,128)} %get-tuple-element.76) | copy-start | bytes 61444

commit v7 on v6

--- a/solution.py
+++ b/solution.py
@@ -544,7 +544,7 @@
     ring_begin(of(3))
     pairs = heads.shape[1] // 2
     last = ring - 2
-    early = 2
+    early = 1
 
     def streams_here():
         ring_complete(2, 4)
@@ -1383,7 +1383,7 @@
         stage(way, 0, i)
 
     opening = 2
-    order = middle + ahead + late
+    order = ahead + middle + late
 
     @pl.loop(1, ring - 1)
     def _(step):

time: 818 us -> 812 us (level)
  no operation moved by 1% of the time
where the time goes in v7:
time: 812 us; the launch traced here: 805 us
  Pallas kernels  794 us (98%)
  local copies, waits for them, and re-layouts  9.67 us (1%)
    pallas_call x1, Pallas kernels, backward_exchange(): pl.pallas_call(functools.partial(backward_kernel, n, count), out_shape=[j...  397 us
    pallas_call x1, Pallas kernels, forward_exchange(): pl.pallas_call(functools.partial(forward_kernel, n, count), out_shape=[ja...  383 us

profile of v7, /device:TPU:21, one launch (start us, length us, event | category | flops | bytes accessed | tf_op | source)
XLA Modules:
  0.0 804.9 jit_solution(12307864380480995192)
XLA Ops:
  0.6 0.7 pad_maximum_fusion
  1.4 0.1 copy.40
  1.5 0.6 pad.4.refs_14_
  2.1 1.5 copy.42.refs_8_
  3.6 1.5 copy.41.refs_5_.refs_12_
  5.1 383.4 %shard_map.230 = (bf16[5,2048,384]{2,1,0:T(8,128)(2,1)}, f32[16,36,384]{2,1,0:T(8,128)}, bf16[4,2048,384]{2,1,0:T(8,128)(2,1)}, f32[8,384]{1,0:T(8,128)}, bf16[3...) custom-call(bf16[9,128,6144]{2,1,0:T(8,128)(2,1)} %refs_20_.1, ...), custom_call_target="tpu_custom_call" | custom-call | tf_op jit(solution)/shard_map/pallas_call | solution.py:693
  388.6 0.0 copy-start
  388.6 397.2 %shard_map.231 = (bf16[16,4,64,384]{3,2,1,0:T(8,128)(2,1)}, bf16[16,5,128,384]{3,2,1,0:T(8,128)(2,1)}, f32[48,384]{1,0:T(8,128)}, f32[128,128]{1,0:T(8,128)}, f3...) custom-call(bf16[4,2048,384]{2,1,0:T(8,128)(2,1)} %get-tuple-element, ...), custom_call_target="tpu_custom_call" | custom-call | tf_op jit(solution)/shard_map/pallas_call | solution.py:1568
  785.8 1.5 copy.45
  787.3 1.5 slice_bitcast_fusion.1
  788.8 0.0 copy-done
  788.8 0.7 copy.44
  789.5 0.9 slice_bitcast_fusion
  790.4 0.7 copy.46
  791.1 0.0 copy-start.1
  791.1 12.9 %shard_map.232 = (bf16[9,128,6144]{2,1,0:T(8,128)(2,1)}, bf16[128,6144]{1,0:T(8,128)(2,1)}, f32[3,128,1024]{2,1,0:T(8,128)}, f32[128,1024]{1,0:T(8,128)}, f32[128,4096]{1,0:T(8,128)}, /*index=5*/f32[128,4096]{1,0:T(8,128)}) custom-call(bf16[16,5,128,384]{3,2,1,0:T(8,128)(2,1)} %get-tuple-element.62.refs_0_, ...), custom_call_target="tpu_custom_call" | custom-call | tf_op jit(solution)/shard_map/pallas_call | solution.py:1709
  804.0 0.0 copy-done.1
  804.0 0.6 copy.48
Async XLA Ops:
  388.6 400.2 %copy-start = (f32[384,40]{1,0:T(8,128)S(1)}, f32[384,40]{1,0:T(8,128)}, u32[]{:S(2)}) copy-start(f32[384,40]{1,0:T(8,128)} %get-tuple-element.100) | copy-start | bytes 184324
  791.1 12.9 %copy-start.1 = (f32[40,128]{1,0:T(8,128)S(1)}, f32[40,128]{1,0:T(8,128)}, u32[]{:S(2)}) copy-start(f32[40,128]{1,0:T(8,128)} %get-tuple-element.76) | copy-start | bytes 61444

commit v8 on v7

--- a/solution.py
+++ b/solution.py
@@ -133,6 +133,8 @@
         swap_recv,
         mix_send,
         mix_recv,
+        half_send,
+        half_recv,
         a_send,
         a_recv,
         y_send,
@@ -214,10 +216,25 @@
                 for way in range(2):
                     core_copy(way, step, p).wait_recv()
 
+    def mix_half():
+        return pl.ds(pl.multiple_of(mp * (MIXED // 2), 8), MIXED // 2)
+
     def mix_copy(q):
         return remote(
-            mix, mixes.at[me], mix_send.at[q], mix_recv.at[q], {"dp": (me + q) % n}
-        )
+            mix.at[mix_half()],
+            mixes.at[me, mix_half()],
+            mix_send.at[q],
+            mix_recv.at[q],
+            {"dp": (me + q) % n},
+        )
+
+    def half_copy(q):
+        there = mixes.at[(me + q) % n, mix_half()]
+        return remote(there, there, half_send.at[q], half_recv.at[q], across)
+
+    def half_turn(q):
+        mix_copy(n - q).wait_recv()
+        half_copy(q).start()
 
     def lanes(peer):
         return pl.ds(pl.multiple_of(peer * tokens, 128), tokens)
@@ -486,7 +503,11 @@
         def _():
             hist_copy(q + 1).start()
 
-        mix_copy(n - q).wait_recv()
+        @pl.when(q < n - 1)
+        def _():
+            half_turn(q + 1)
+
+        half_copy(q).wait_recv()
         mix_streams(q)
         cot_copy(q).wait()
         stream_copy(q).start()
@@ -520,6 +541,7 @@
     cot_copy(0).wait()
     own_copy().start()
     across_copy(0, True).start()
+    half_turn(1)
 
     @pl.loop(1, 4)
     def _(q):
@@ -658,6 +680,7 @@
     @pl.loop(1, n)
     def _(q):
         mix_copy(q).wait_send()
+        half_copy(q).wait_send()
         stream_copy(q).wait_send()
 
     @pl.loop(0, n)
@@ -744,7 +767,7 @@
             DMA((ring,)),
             DMA((ring,)),
         ]
-        + [DMA((n,)) for _ in range(6)]
+        + [DMA((n,)) for _ in range(8)]
         + [DMA((2, ring - 1, travel)) for _ in range(2)]
         + [DMA((2, ring, travel)) for _ in range(2)],
         compiler_params=pltpu.CompilerParams(
@@ -1768,7 +1791,7 @@
         n,
         history,
         cot_out,
-        mix_in.T,
+        jnp.pad(mix_in.T, ((0, MIXED - STREAMS * HIST), (0, 0))),
         tables,
         doc_ids,
         group_ids,

time: 812 us -> 805 us (level)
  no operation moved by 1% of the time
where the time goes in v8:
time: 805 us; the launch traced here: 798 us
  Pallas kernels  786 us (98%)
  local copies, waits for them, and re-layouts  11.1 us (1%)
    pallas_call x1, Pallas kernels, backward_exchange(): pl.pallas_call(functools.partial(backward_kernel, n, count), out_shape=[j...  397 us
    pallas_call x1, Pallas kernels, forward_exchange(): pl.pallas_call(functools.partial(forward_kernel, n, count), out_shape=[ja...  375 us

profile of v8, /device:TPU:21, one launch (start us, length us, event | category | flops | bytes accessed | tf_op | source)
XLA Modules:
  0.0 798.3 jit_solution(15485658443711011100)
XLA Ops:
  0.6 0.7 pad_maximum_fusion
  1.4 0.1 copy.40
  1.5 0.6 pad.9.refs_14_
  2.1 1.5 pad.8.refs_2_
  3.6 1.5 copy.42.refs_8_
  5.1 1.5 copy.41.refs_5_.refs_12_
  6.6 375.4 %shard_map.230 = (bf16[5,2048,384]{2,1,0:T(8,128)(2,1)}, f32[16,48,384]{2,1,0:T(8,128)}, bf16[4,2048,384]{2,1,0:T(8,128)(2,1)}, f32[8,384]{1,0:T(8,128)}, bf16[3...) custom-call(bf16[9,128,6144]{2,1,0:T(8,128)(2,1)} %refs_20_.1, ...), custom_call_target="tpu_custom_call" | custom-call | tf_op jit(solution)/shard_map/pallas_call | solution.py:716
  382.0 0.0 copy-start
  382.0 397.1 %shard_map.231 = (bf16[16,4,64,384]{3,2,1,0:T(8,128)(2,1)}, bf16[16,5,128,384]{3,2,1,0:T(8,128)(2,1)}, f32[48,384]{1,0:T(8,128)}, f32[128,128]{1,0:T(8,128)}, f3...) custom-call(bf16[4,2048,384]{2,1,0:T(8,128)(2,1)} %get-tuple-element, ...), custom_call_target="tpu_custom_call" | custom-call | tf_op jit(solution)/shard_map/pallas_call | solution.py:1591
  779.1 1.5 copy.45
  780.7 1.5 slice_bitcast_fusion.1
  782.1 0.0 copy-done
  782.1 0.7 copy.44
  782.8 0.9 slice_bitcast_fusion
  783.8 0.7 copy.46
  784.4 0.0 copy-start.1
  784.4 13.0 %shard_map.232 = (bf16[9,128,6144]{2,1,0:T(8,128)(2,1)}, bf16[128,6144]{1,0:T(8,128)(2,1)}, f32[3,128,1024]{2,1,0:T(8,128)}, f32[128,1024]{1,0:T(8,128)}, f32[128,4096]{1,0:T(8,128)}, /*index=5*/f32[128,4096]{1,0:T(8,128)}) custom-call(bf16[16,5,128,384]{3,2,1,0:T(8,128)(2,1)} %get-tuple-element.62.refs_0_, ...), custom_call_target="tpu_custom_call" | custom-call | tf_op jit(solution)/shard_map/pallas_call | solution.py:1732
  797.5 0.0 copy-done.1
  797.5 0.6 copy.48
Async XLA Ops:
  382.0 400.1 %copy-start = (f32[384,40]{1,0:T(8,128)S(1)}, f32[384,40]{1,0:T(8,128)}, u32[]{:S(2)}) copy-start(f32[384,40]{1,0:T(8,128)} %get-tuple-element.100) | copy-start | bytes 184324
  784.4 13.0 %copy-start.1 = (f32[40,128]{1,0:T(8,128)S(1)}, f32[40,128]{1,0:T(8,128)}, u32[]{:S(2)}) copy-start(f32[40,128]{1,0:T(8,128)} %get-tuple-element.76) | copy-start | bytes 61444
